TPU v7x, 512 devices: a whole 4x8x8 slice. The times are simulated.
512 devices in a mesh: queue: 64 (over z_hi, y, core), seq: 8 (over x, z_lo).
Axes of the slice: x: 4, y: 8, z: 8 (z_hi: 4, z_lo: 2; z = z_hi * 2 + z_lo), core: 2. Of those that a mesh axis runs over, the one named last changes fastest.
Arguments:
- queries: bfloat16 [64, 1024, 3072], P('queue', 'seq'), may hold values from -18 to 18
- key_proj: bfloat16 [64, 1024, 3072], P('queue', 'seq'), may hold values from -18 to 18
- values: bfloat16 [64, 1024, 3072], P('queue', 'seq'), may hold values from -6 to 6
- latents: float32 [64, 1024, 64], P('queue', 'seq'), may hold values from -6 to 6
- head_weight: bfloat16 [3072, 64], replicated, may hold values from -0.109375 to 0.109375
- levels: int32 [64], P('queue'), may hold values from 1 to 256, as said below
- timesteps: int32 [257], replicated, may hold values from 0 to 10240, as said below
- fresh_noise: float32 [1024, 64], P('seq'), may hold values from -6 to 6
Outputs:
- next_queue: float32 [64, 1024, 64], P('queue', 'seq')
- velocity: float32 [64, 1024, 64], P('queue', 'seq')
Inputs may be any that keep to these rules, and one draw needn't show every extreme that they name: `levels`: strictly rising along the queue; position f holds a value from 4 f + 1 to 4 f + 4; the first position holds 1 and the last 256. `timesteps`: strictly rising, starting at 0, with steps of 16 to 64; the steps into levels 2 k + 1 and 2 k + 2 sum to 80.
All inputs are finite; a program needn't handle non-finite values.
Results may differ from a plain program's by a relative error of at most 0.0033.
Values may be sent and summed in bfloat16 or wider, within the bound.
No kernel may reach another device: no remote copies, remote signals or barrier semaphores. Data moves between devices by JAX's collectives and lax.ppermute only.
A program may use at most 64 MiB of HBM per device.

v0:
```python
import math

import jax
import jax.numpy as jnp
from jax import lax
from jax.sharding import PartitionSpec as P

HS = 128


def extended(x, sides, width):
    for axis, dim in sides:
        size, length = (lax.axis_size(axis), x.shape[dim])
        up = [(i, (i + 1) % size) for i in range(size - 1)]
        down = [(j, i) for i, j in up]
        last = lax.slice_in_dim(x, length - width, length, axis=dim)
        leading = lax.slice_in_dim(x, 0, width, axis=dim)
        before = lax.ppermute(last, axis, up)
        after = lax.ppermute(leading, axis, down)
        x = jnp.concatenate([before, x, after], axis=dim)
    return x


def passed_along(value, axis, steps):
    count = lax.axis_size(axis)
    leading, last = (max(0, -steps), min(count, count - steps))
    return lax.ppermute(value, axis, [(source, source + steps) for source in range(leading, last)])


def attend_block(query_block, key_rows, value_rows, key_ok, scale):
    scores = (
        lax.dot_general(
            query_block, key_rows, (((1,), (1,)), ((), ())), preferred_element_type=jnp.float32
        )
        * scale
    )
    scores = jnp.where(key_ok[None, :], scores, -jnp.inf)
    row_peak = jnp.max(scores, axis=1, keepdims=True)
    weights = jnp.exp(scores - row_peak)
    totals = jnp.sum(weights, axis=1)
    probs = weights.astype(jnp.bfloat16)
    mixed = jnp.dot(probs, value_rows, preferred_element_type=jnp.float32) / totals[:, None]
    return mixed.astype(jnp.bfloat16)


def attend_frame(query_local, key_frames, value_frames, key_ok):
    tokens = query_local.shape[0]
    heads_here = query_local.shape[1] // HS
    scale = HS ** (-0.5)
    block_rows = math.gcd(tokens, 512)
    block_count = tokens // block_rows
    query_heads = query_local.reshape(block_count, block_rows, heads_here, HS).transpose(2, 0, 1, 3)
    key_heads = key_frames.reshape(-1, heads_here, HS).transpose(1, 0, 2)
    value_heads = value_frames.reshape(-1, heads_here, HS).transpose(1, 0, 2)

    def per_head(operands):
        query_blocks, key_rows, value_rows = operands
        return lax.map(
            lambda block: attend_block(block, key_rows, value_rows, key_ok, scale), query_blocks
        )

    result = lax.map(per_head, (query_heads, key_heads, value_heads))
    return result.transpose(1, 2, 0, 3).reshape(tokens, heads_here * HS)


def on_device(queries, key_proj, values, latents, head_weight, levels, timesteps, fresh_noise):
    position = lax.axis_index("queue")
    length = lax.axis_size("queue")
    query_here, key_here, value_here = (
        lax.all_to_all(queries, "seq", split_axis=2, concat_axis=1, tiled=True),
        lax.all_to_all(key_proj, "seq", split_axis=2, concat_axis=1, tiled=True),
        lax.all_to_all(values, "seq", split_axis=2, concat_axis=1, tiled=True),
    )
    frames_kv = extended(jnp.stack([key_here, value_here]), (("queue", 1),), 1)
    tokens = query_here.shape[1]
    neighbour = position - 1 + jnp.arange(3, dtype=jnp.int32)
    frame_ok = (neighbour >= 0) & (neighbour < length)
    key_ok = jnp.repeat(frame_ok, tokens)
    attended = attend_frame(query_here[0], frames_kv[0], frames_kv[1], key_ok)
    gathered = lax.all_to_all(attended[None], "seq", split_axis=1, concat_axis=2, tiled=True)
    velocity = jnp.dot(gathered[0], head_weight, preferred_element_type=jnp.float32)
    level_grid = jnp.arange(timesteps.shape[0], dtype=jnp.int32)[None, :]
    lower_level = jnp.maximum(levels - 2, 0)
    time_now = jnp.sum(jnp.where(level_grid == levels[:, None], timesteps[None, :], 0), axis=1)
    time_before = jnp.sum(
        jnp.where(level_grid == lower_level[:, None], timesteps[None, :], 0), axis=1
    )
    step_size = (time_before - time_now).astype(jnp.float32) / 64.0
    advanced = latents + step_size[:, None, None] * velocity[None]
    shifted = passed_along(advanced, "queue", -1)
    next_queue = jnp.where(position == length - 1, fresh_noise[None], shifted)
    return (next_queue, velocity[None])


def solution(mesh):
    in_specs = (
        P("queue", "seq", None),
        P("queue", "seq", None),
        P("queue", "seq", None),
        P("queue", "seq", None),
        P(),
        P("queue"),
        P(),
        P("seq", None),
    )
    out_specs = (P("queue", "seq", None), P("queue", "seq", None))
    return jax.shard_map(
        on_device, mesh=mesh, in_specs=in_specs, out_specs=out_specs, check_vma=False
    )
```

profile of v0, /device:TPU:185, one launch (start us, length us, event | category | flops | bytes accessed | tf_op | source)
XLA Modules:
  0.0 231.0 jit_solution(1066384234028468217)
XLA Ops:
  0.6 3.7 %copy.41 = bf16[1,128,3072]{1,0,2:T(2,128)(2,1)S(1)} copy(bf16[1,128,3072]{2,1,0:T(8,128)(2,1)} %param.14) | data formatting | bytes 1572864 | tf_op args[2]
  4.9 16.9 %reduce.5 = bf16[3072,128]{1,0:T(8,128)(2,1)S(1)} reduce(bf16[3072,1,128]{2,1,0:T(2,128)(2,1)S(1)} %bitcast.88, bf16[]{:T(256)} %broadcast.40), dimensions={1}, to_apply=%bitcast.50.reduce_sub_computation | reduce | bytes 1572866
  23.0 5.8 %all-to-all-start.2 = ((bf16[8,2,24576]{2,1,0:T(2,128)(2,1)}), bf16[8,2,24576]{2,1,0:T(2,128)(2,1)S(1)}, u32[]{:S(2)}, u32[]{:S(2)}) async-start(bf16[8,2,24576]{2,1,0:T(2,128)(2,1)} %reshape.37), calls=%async_computation.2 | async-start | bytes 1572864 | tf_op jit(solution)/shard_map/all_to_all | solution.py:72
  28.8 3.7 %copy.39 = bf16[1,128,3072]{1,0,2:T(2,128)(2,1)S(1)} copy(bf16[1,128,3072]{2,1,0:T(8,128)(2,1)} %param.13) | data formatting | bytes 1572864 | tf_op args[1]
  32.5 17.0 %reduce.6 = bf16[3072,128]{1,0:T(8,128)(2,1)S(1)} reduce(bf16[3072,1,128]{2,1,0:T(2,128)(2,1)S(1)} %bitcast.94, bf16[]{:T(256)} %broadcast.40), dimensions={1}, to_apply=%bitcast.52.reduce_sub_computation | reduce | bytes 1572866
  50.5 5.1 %all-to-all-start.1 = ((bf16[8,2,24576]{2,1,0:T(2,128)(2,1)}), bf16[8,2,24576]{2,1,0:T(2,128)(2,1)}, u32[]{:S(2)}, u32[]{:S(2)}) async-start(bf16[8,2,24576]{2,1,0:T(2,128)(2,1)} %reshape.39), calls=%async_computation.1 | async-start | bytes 1572864 | tf_op jit(solution)/shard_map/all_to_all | solution.py:71
  56.9 10.3 %all-to-all-done.1 = bf16[8,2,24576]{2,1,0:T(2,128)(2,1)} async-done(((bf16[8,2,24576]{2,1,0:T(2,128)(2,1)}), bf16[8,2,24576]{2,1,0:T(2,128)(2,1)}, u32[]{:S(2)}, u32[]{:S(2)}) %all-to-all-start.1) | async-done | bytes 786464 | tf_op jit(solution)/shard_map/all_to_all | solution.py:71
  67.2 4.1 %reshape.40 = bf16[3072,1,128]{2,1,0:T(2,128)(2,1)S(1)} reshape(bf16[8,2,24576]{2,1,0:T(2,128)(2,1)} %all-to-all-done.1) | data formatting | bytes 1572864
  71.8 1.3 pad_maximum_fusion.1
  73.1 7.6 %collective-permute-start = (bf16[2,1,1024,384]{3,2,1,0:T(8,128)(2,1)}, bf16[2,1,1024,384]{3,2,1,0:T(8,128)(2,1)}, u32[]{:S(2)}, u32[]{:S(2)}) collective-permute-start(bf16[2,1,1024,384]{3,2,1,0:T(8,128)(2,1)} %pad_maximum_fusion.1), channel_id=1, source_target_pairs={{0,8},{8,16},{16,24},{24,32},{32,40},{40,48},{48,56},{56,64},{64,7... | collective-permute-start | bytes 4718600 | tf_op jit(solution)/shard_map/ppermute | solution.py:18
  80.7 1.9 collective-permute-start.1
  82.7 3.7 %copy.37 = bf16[1,128,3072]{1,0,2:T(2,128)(2,1)S(1)} copy(bf16[1,128,3072]{2,1,0:T(8,128)(2,1)} %param.12) | data formatting | bytes 1572864 | tf_op args[0]
  86.4 17.9 %reduce.4 = bf16[3072,128]{1,0:T(8,128)(2,1)} reduce(bf16[3072,1,128]{2,1,0:T(2,128)(2,1)S(1)} %bitcast.95, bf16[]{:T(256)} %broadcast.40), dimensions={1}, to_apply=%bitcast.48.reduce_sub_computation | reduce | bytes 1572866
  104.3 2.8 %reshape.35 = bf16[8,2,24576]{2,1,0:T(2,128)(2,1)} reshape(bf16[3072,128]{1,0:T(8,128)(2,1)} %reduce.4) | data formatting | bytes 1572864
  107.1 4.4 %all-to-all-start = ((bf16[8,2,24576]{2,1,0:T(2,128)(2,1)}), bf16[8,2,24576]{2,1,0:T(2,128)(2,1)}, u32[]{:S(2)}, u32[]{:S(2)}) async-start(bf16[8,2,24576]{2,1,0:T(2,128)(2,1)} %reshape.35), calls=%async_computation | async-start | bytes 1572864 | tf_op jit(solution)/shard_map/all_to_all | solution.py:70
  111.6 18.7 %all-to-all-done = bf16[8,2,24576]{2,1,0:T(2,128)(2,1)} async-done(((bf16[8,2,24576]{2,1,0:T(2,128)(2,1)}), bf16[8,2,24576]{2,1,0:T(2,128)(2,1)}, u32[]{:S(2)}, u32[]{:S(2)}) %all-to-all-start) | async-done | bytes 786464 | tf_op jit(solution)/shard_map/all_to_all | solution.py:70
  130.3 4.1 %reshape.36 = bf16[3072,1,128]{2,1,0:T(2,128)(2,1)S(1)} reshape(bf16[8,2,24576]{2,1,0:T(2,128)(2,1)} %all-to-all-done) | data formatting | bytes 1572864
  136.2 2.2 pad_maximum_fusion
  138.4 2.6 %fusion.26 = (bf16[1,3,1024,384]{3,2,1,0:T(8,128)(2,1)}, bf16[1,3,1024,384]{3,2,1,0:T(8,128)(2,1)}) fusion(bf16[2,3,1024,384]{3,2,1,0:T(8,128)(2,1)S(1)} %pad_maximum_fusion), kind=kLoop, calls=%fused_computation.31 | loop fusion | bytes 9437184 | tf_op jit(solution)/shard_map/slice | solution.py:79
  141.0 5.9 %reshape_squeeze.10 = bf16[3072,3,128]{2,1,0:T(4,128)(2,1)S(1)} reshape(bf16[1,3,1024,384]{3,2,1,0:T(8,128)(2,1)} %get-tuple-element.138) | data formatting | bytes 4718592 | tf_op jit(solution)/shard_map/reshape;squeeze | solution.py:53
  146.9 1.8 copy.44
  148.6 5.9 %reshape_squeeze.11 = bf16[3072,3,128]{2,1,0:T(4,128)(2,1)S(1)} reshape(bf16[1,3,1024,384]{3,2,1,0:T(8,128)(2,1)} %get-tuple-element.137) | data formatting | bytes 4718592 | tf_op jit(solution)/shard_map/reshape;squeeze | solution.py:54
  154.5 1.7 copy.45
  156.3 36.6 %while.24 = (s32[]{:T(128)}, bf16[3,2,512,128]{3,2,1,0:T(8,128)(2,1)}, bf16[3,2,512,128]{2,1,3,0:T(2,128)(2,1)}, bf16[3,3072,128]{2,1,0:T(8,128)(2,1)}, bf16[3,3...) while((s32[]{:T(128)}, ...), condition=%wide.region_7.8_spmd.clone, body=%wide.region_2.7_spmd.clone.sunk | while | flops 822737920 | bytes 25469736 | solution.py:62
  156.3 1.5 dynamic-slice_bitcast_fusion.3
  159.8 7.9 %while.25 = (s32[]{:T(128)}, bf16[2,512,128]{2,1,0:T(8,128)(2,1)S(1)}, pred[3,1024]{1,0:T(4,128)(4,1)}, bf16[2,512,128]{2,1,0:T(8,128)(2,1)S(1)}, bf16[3072,128]...) while((s32[]{:T(128)}, ...), condition=%wide.wide.region_6.6_spmd, body=%wide.wide.region_3.5_spmd.sunk | while | flops 822737920 | bytes 20728924 | solution.py:58
  160.9 1.4 fusion.47
  162.3 1.4 fusion.48
  164.9 1.4 fusion.47
  166.3 1.4 fusion.48
  168.5 1.5 dynamic-slice_bitcast_fusion.3
  172.0 7.9 %while.25 = (s32[]{:T(128)}, bf16[2,512,128]{2,1,0:T(8,128)(2,1)S(1)}, pred[3,1024]{1,0:T(4,128)(4,1)}, bf16[2,512,128]{2,1,0:T(8,128)(2,1)S(1)}, bf16[3072,128]...) while((s32[]{:T(128)}, ...), condition=%wide.wide.region_6.6_spmd, body=%wide.wide.region_3.5_spmd.sunk | while | flops 822737920 | bytes 20728924 | solution.py:58
  173.1 1.4 fusion.47
  174.5 1.4 fusion.48
  177.1 1.4 fusion.47
  178.5 1.4 fusion.48
  180.6 1.5 dynamic-slice_bitcast_fusion.3
  184.2 7.9 %while.25 = (s32[]{:T(128)}, bf16[2,512,128]{2,1,0:T(8,128)(2,1)S(1)}, pred[3,1024]{1,0:T(4,128)(4,1)}, bf16[2,512,128]{2,1,0:T(8,128)(2,1)S(1)}, bf16[3072,128]...) while((s32[]{:T(128)}, ...), condition=%wide.wide.region_6.6_spmd, body=%wide.wide.region_3.5_spmd.sunk | while | flops 822737920 | bytes 20728924 | solution.py:58
  185.3 1.4 fusion.47
  186.7 1.4 fusion.48
  189.3 1.4 fusion.47
  190.7 1.4 fusion.48
  192.8 1.8 copy.49
  195.8 5.4 %reduce.7 = bf16[1024,384]{1,0:T(8,128)(2,1)S(1)} reduce(bf16[1024,1,384]{2,1,0:T(2,128)(2,1)S(1)} %bitcast.89, bf16[]{:T(256)} %broadcast.40), dimensions={1}, to_apply=%bitcast.54.reduce_sub_computation | reduce | bytes 1572866
  202.3 3.7 %all-to-all-start.3 = ((bf16[8,2,24576]{2,1,0:T(2,128)(2,1)}), bf16[8,2,24576]{2,1,0:T(2,128)(2,1)S(1)}, u32[]{:S(2)}, u32[]{:S(2)}) async-start(bf16[8,2,24576]{2,1,0:T(2,128)(2,1)} %reshape.41), calls=%async_computation.3 | async-start | bytes 1572864 | tf_op jit(solution)/shard_map/all_to_all | solution.py:80
  208.5 10.1 %all-to-all-done.3 = bf16[8,2,24576]{2,1,0:T(2,128)(2,1)S(1)} async-done(((bf16[8,2,24576]{2,1,0:T(2,128)(2,1)}), bf16[8,2,24576]{2,1,0:T(2,128)(2,1)S(1)}, u32[]{:S(2)}, u32[]{:S(2)}) %all-to-all-start.3) | async-done | bytes 786464 | tf_op jit(solution)/shard_map/all_to_all | solution.py:80
  220.8 3.1 %collective-permute-start.2 = (f32[1,128,64]{1,2,0:T(8,128)S(1)}, f32[1,128,64]{1,2,0:T(8,128)S(1)}, u32[]{:S(2)}, u32[]{:S(2)}) collective-permute-start(f32[1,128,64]{1,2,0:T(8,128)S(1)} %get-tuple-element.139), channel_id=1, source_target_pairs={{8,0},{16,8},{24,16},{32,24},{40,32},{48,40},{56,48},{64,56},{72,6... | collective-permute-start | bytes 98312 | tf_op jit(solution)/shard_map/ppermute | solution.py:27
  223.9 6.4 %collective-permute-done.2 = f32[1,128,64]{1,2,0:T(8,128)S(1)} collective-permute-done((f32[1,128,64]{1,2,0:T(8,128)S(1)}, f32[1,128,64]{1,2,0:T(8,128)S(1)}, u32[]{:S(2)}, u32[]{:S(2)}) %collective-permute-start.2) | collective-permute-done | bytes 32800 | tf_op jit(solution)/shard_map/ppermute | solution.py:27
  (62 shorter events, 27.0 us)
Async XLA Ops:
  0.6 219.3 %copy-start = (bf16[3072,64]{0,1:T(8,128)(2,1)S(1)}, bf16[3072,64]{0,1:T(8,128)(2,1)}, u32[]{:S(2)}) copy-start(bf16[3072,64]{0,1:T(8,128)(2,1)} %param.16) | copy-start | bytes 1179652
  23.0 27.5 %all-to-all-start.2 = ((bf16[8,2,24576]{2,1,0:T(2,128)(2,1)}), bf16[8,2,24576]{2,1,0:T(2,128)(2,1)S(1)}, u32[]{:S(2)}, u32[]{:S(2)}) async-start(bf16[8,2,24576]{2,1,0:T(2,128)(2,1)} %reshape.37), calls=%async_computation.2 | async-start | bytes 1572864 | tf_op jit(solution)/shard_map/all_to_all | solution.py:72
  50.5 16.7 %all-to-all-start.1 = ((bf16[8,2,24576]{2,1,0:T(2,128)(2,1)}), bf16[8,2,24576]{2,1,0:T(2,128)(2,1)}, u32[]{:S(2)}, u32[]{:S(2)}) async-start(bf16[8,2,24576]{2,1,0:T(2,128)(2,1)} %reshape.39), calls=%async_computation.1 | async-start | bytes 1572864 | tf_op jit(solution)/shard_map/all_to_all | solution.py:71
  73.1 63.1 %collective-permute-start = (bf16[2,1,1024,384]{3,2,1,0:T(8,128)(2,1)}, bf16[2,1,1024,384]{3,2,1,0:T(8,128)(2,1)}, u32[]{:S(2)}, u32[]{:S(2)}) collective-permute-start(bf16[2,1,1024,384]{3,2,1,0:T(8,128)(2,1)} %pad_maximum_fusion.1), channel_id=1, source_target_pairs={{0,8},{8,16},{16,24},{24,32},{32,40},{40,48},{48,56},{56,64},{64,7... | collective-permute-start | bytes 4718600 | tf_op jit(solution)/shard_map/ppermute | solution.py:18
  80.7 55.4 %collective-permute-start.1 = (bf16[2,1,1024,384]{3,2,1,0:T(8,128)(2,1)}, bf16[2,1,1024,384]{3,2,1,0:T(8,128)(2,1)}, u32[]{:S(2)}, u32[]{:S(2)}) collective-permute-start(bf16[2,1,1024,384]{3,2,1,0:T(8,128)(2,1)} %pad_maximum_fusion.1), channel_id=1, source_target_pairs={{8,0},{16,8},{24,16},{32,24},{40,32},{48,40},{56,48},{64,56},{72,6... | collective-permute-start | bytes 4718600 | tf_op jit(solution)/shard_map/ppermute | solution.py:19
  107.1 23.2 %all-to-all-start = ((bf16[8,2,24576]{2,1,0:T(2,128)(2,1)}), bf16[8,2,24576]{2,1,0:T(2,128)(2,1)}, u32[]{:S(2)}, u32[]{:S(2)}) async-start(bf16[8,2,24576]{2,1,0:T(2,128)(2,1)} %reshape.35), calls=%async_computation | async-start | bytes 1572864 | tf_op jit(solution)/shard_map/all_to_all | solution.py:70
  159.2 0.6 copy-start.1
  171.4 0.6 copy-start.1
  183.6 0.6 copy-start.1
  192.8 13.8 %copy-start.4 = (s32[257]{0:T(512)S(1)}, s32[257]{0:T(512)}, u32[]{:S(2)}) copy-start(s32[257]{0:T(512)} %param.18) | copy-start | bytes 3088
  201.2 18.7 %copy-start.2 = (f32[1,128,64]{1,2,0:T(8,128)S(1)}, f32[1,128,64]{1,2,0:T(8,128)}, u32[]{:S(2)}) copy-start(f32[1,128,64]{1,2,0:T(8,128)} %param.15) | copy-start | bytes 98308
  202.3 28.1 %copy-start.3 = (f32[128,64]{0,1:T(8,128)S(1)}, f32[128,64]{0,1:T(8,128)}, u32[]{:S(2)}) copy-start(f32[128,64]{0,1:T(8,128)} %param.19) | copy-start | bytes 98308
  202.3 16.3 %all-to-all-start.3 = ((bf16[8,2,24576]{2,1,0:T(2,128)(2,1)}), bf16[8,2,24576]{2,1,0:T(2,128)(2,1)S(1)}, u32[]{:S(2)}, u32[]{:S(2)}) async-start(bf16[8,2,24576]{2,1,0:T(2,128)(2,1)} %reshape.41), calls=%async_computation.3 | async-start | bytes 1572864 | tf_op jit(solution)/shard_map/all_to_all | solution.py:80
  220.8 9.5 %collective-permute-start.2 = (f32[1,128,64]{1,2,0:T(8,128)S(1)}, f32[1,128,64]{1,2,0:T(8,128)S(1)}, u32[]{:S(2)}, u32[]{:S(2)}) collective-permute-start(f32[1,128,64]{1,2,0:T(8,128)S(1)} %get-tuple-element.139), channel_id=1, source_target_pairs={{8,0},{16,8},{24,16},{32,24},{40,32},{48,40},{56,48},{64,56},{72,6... | collective-permute-start | bytes 98312 | tf_op jit(solution)/shard_map/ppermute | solution.py:27
where the time goes:
time: 232 us; the launch traced here: 231 us
  other arithmetic  70.5 us (30%)
  local copies, waits for them, and re-layouts  64.2 us (28%)
  waiting for transfers between devices  45.4 us (20%)
  starting transfers between devices  31.8 us (14%)
  matrix products  16.1 us (7%)
  between operations  2.74 us (1%)
    unnamed x4, other arithmetic  57.2 us
    unnamed x26, local copies, waits for them, and re-layouts  31.4 us
    all_to_all x1, waiting for transfers between devices, on_device(): lax.all_to_all(queries, 'seq', split_axis=2, concat_axis=1, tiled=True)  18.7 us
    all_to_all x1, waiting for transfers between devices, on_device(): lax.all_to_all(key_proj, 'seq', split_axis=2, concat_axis=1, tiled=True)  10.3 us
    all_to_all x1, waiting for transfers between devices, on_device(): lax.all_to_all(attended[None], 'seq', split_axis=1, concat_axis=2, tiled=...  10.1 us
    reduce_sum x6, other arithmetic, attend_block(): totals = jnp.sum(weights, axis=1)  8.47 us
    dot_general x6, matrix products, attend_block(): jnp.dot(probs, value_rows, preferred_element_type=jnp.float32)  8.44 us
    ppermute x1, starting transfers between devices, extended(): before = lax.ppermute(last, axis, up)  7.64 us
  transfers between devices with their start and end apart: 7, of which 4 were waited for; matrix products, arithmetic and copies ran while one was open for 23% of the time, Pallas kernels for 0%

commit v1 on v0

v1 whole, which is shorter than its diff:
```python
import math

import jax
import jax.numpy as jnp
from jax import lax
from jax.experimental import pallas as pl
from jax.experimental.pallas import tpu as pltpu
from jax.sharding import PartitionSpec as P

HS = 128
HALF = 64
MIB = 1 << 20
NT = (((1,), (1,)), ((), ()))
VMEM = pl.BlockSpec(memory_space=pltpu.VMEM)
SMEM = pl.BlockSpec(memory_space=pltpu.SMEM)


def pack_kv_kernel(key_ref, value_ref, weight_ref, out_ref):
    tokens = key_ref.shape[0]
    for h in range(3):
        out_ref[0, h * tokens : (h + 1) * tokens, :] = key_ref[:, h * HS : (h + 1) * HS]
    weight = [weight_ref[:, h * HS : (h + 1) * HS] for h in range(3)]
    zero = jnp.zeros_like(weight[0])

    def diagonal(a, b):
        return jnp.concatenate(
            [jnp.concatenate([a, zero], axis=1), jnp.concatenate([zero, b], axis=1)], axis=0
        )

    half = tokens // 2
    first = lax.dot_general(
        value_ref[:, : 2 * HS], diagonal(weight[0], weight[1]), NT, preferred_element_type=jnp.float32
    )
    third = jnp.concatenate([value_ref[:half, 2 * HS :], value_ref[half:, 2 * HS :]], axis=1)
    third = lax.dot_general(
        third, diagonal(weight[2], weight[2]), NT, preferred_element_type=jnp.float32
    )
    out_ref[0, 3 * tokens : 4 * tokens, :] = first.astype(jnp.bfloat16)
    out_ref[0, 4 * tokens :, :] = third.astype(jnp.bfloat16)


def pack_kv(keys, values, weight_t, groups):
    tokens, width = keys.shape
    part = width // groups
    rows = tokens * 3 + tokens + tokens // 2
    return pl.pallas_call(
        pack_kv_kernel,
        grid=(groups,),
        in_specs=[
            pl.BlockSpec((tokens, part), lambda s: (0, s)),
            pl.BlockSpec((tokens, part), lambda s: (0, s)),
            pl.BlockSpec((HALF, part), lambda s: (0, s)),
        ],
        out_specs=pl.BlockSpec((1, rows, HS), lambda s: (s, 0, 0)),
        out_shape=jax.ShapeDtypeStruct((groups, rows, HS), jnp.bfloat16),
        name="pack_kv",
    )(keys, values, weight_t)


def pack_q_kernel(query_ref, out_ref):
    tokens = query_ref.shape[0]
    for h in range(3):
        out_ref[0, h * tokens : (h + 1) * tokens, :] = query_ref[:, h * HS : (h + 1) * HS]


def pack_q(queries, groups):
    tokens, width = queries.shape
    part = width // groups
    return pl.pallas_call(
        pack_q_kernel,
        grid=(groups,),
        in_specs=[pl.BlockSpec((tokens, part), lambda s: (0, s))],
        out_specs=pl.BlockSpec((1, 3 * tokens, HS), lambda s: (s, 0, 0)),
        out_shape=jax.ShapeDtypeStruct((groups, 3 * tokens, HS), jnp.bfloat16),
        name="pack_q",
    )(queries)


def scaled_queries(query_ref, split_ref):
    groups, rows, _ = query_ref.shape
    tokens = rows // 3
    scale = HS ** (-0.5) * math.log2(math.e)
    for h in range(3):
        q = query_ref[:, h * tokens : (h + 1) * tokens, :].reshape(groups * tokens, HS)
        q = q.astype(jnp.float32) * scale
        high = q.astype(jnp.bfloat16)
        low = (q - high.astype(jnp.float32)).astype(jnp.bfloat16)
        split_ref[h, :, :HS] = high
        split_ref[h, :, HS:] = low


def attend(split_ref, kv_ref, block_rows, emit):
    groups, rows, _ = kv_ref.shape
    tokens = rows * 2 // 9
    count = groups * tokens
    pair = kv_ref[:, 3 * tokens : 4 * tokens, :].reshape(count, HS)
    last = kv_ref[:, 4 * tokens :, :]
    swapped = jnp.concatenate([last[:, :, HALF:], last[:, :, :HALF]], axis=2)
    last = jnp.concatenate([last, swapped], axis=1).reshape(count, HS)
    ones = jnp.ones((count, HS), jnp.bfloat16)
    for h in range(3):
        k = kv_ref[:, h * tokens : (h + 1) * tokens, :].reshape(count, HS)
        keys = jnp.concatenate([k, k], axis=1)
        mix = jnp.concatenate([last if h == 2 else pair, ones], axis=1)
        for b in range(count // block_rows):
            span = slice(b * block_rows, (b + 1) * block_rows)
            scores = lax.dot_general(split_ref[h, span, :], keys, NT, preferred_element_type=jnp.float32)
            peak = jnp.ceil(jnp.max(scores, axis=1, keepdims=True))
            probs = jnp.exp2(scores - peak).astype(jnp.bfloat16)
            emit(h, span, peak, jnp.dot(probs, mix, preferred_element_type=jnp.float32))


def lanes(h, rows):
    lane = lax.broadcasted_iota(jnp.int32, (rows, HS), 1)
    if h == 1:
        lane = HS - 1 - lane
    return lane


def packed(h, peak, mixed):
    lane = lanes(h, mixed.shape[0])
    return jnp.where(lane < HALF, mixed[:, :HS], jnp.where(lane < HALF + 32, mixed[:, HS:], peak))


def unpacked(h, state):
    total, peak = (HALF, HALF + 32) if h != 1 else (HALF - 1, 0)
    return state[:, total : total + 1], state[:, peak : peak + 1]


def own_kernel(query_ref, kv_ref, state_ref, split_ref):
    scaled_queries(query_ref, split_ref)

    def emit(h, span, peak, mixed):
        state_ref[h, span, :] = packed(h, peak, mixed)

    attend(split_ref, kv_ref, 256, emit)


def halo_kernel(ok_ref, query_ref, before_ref, after_ref, own_ref, out_ref, split_ref, state_ref):
    scaled_queries(query_ref, split_ref)
    state_ref[...] = own_ref[...]

    def emit(h, span, peak, mixed):
        state = state_ref[h, span, :]
        _, old_peak = unpacked(h, state)
        new_peak = jnp.maximum(old_peak, peak)
        new = packed(h, new_peak, mixed)
        kept, added = jnp.exp2(old_peak - new_peak), jnp.exp2(peak - new_peak)
        lane = lanes(h, state.shape[0])
        state_ref[h, span, :] = jnp.where(lane < HALF + 32, state * kept + new * added, new)

    for i, ref in enumerate((before_ref, after_ref)):
        @pl.when(ok_ref[i] > 0)
        def _():
            attend(split_ref, ref, 256, emit)

    groups, _, tokens = out_ref.shape
    for s in range(groups):
        span = slice(s * tokens, (s + 1) * tokens)
        parts = []
        for h in range(3):
            state = state_ref[h, span, :]
            total, _ = unpacked(h, state)
            parts.append(state / total)
        lane = lanes(0, tokens)
        both = jnp.where(lane < HALF, parts[0] + parts[2], parts[1])
        turned = both.T
        out_ref[s] = turned[:HALF] + turned[HALF:]


def params(mib):
    return pltpu.CompilerParams(vmem_limit_bytes=mib * MIB)


def attend_own(q, kv):
    count = q.shape[0] * q.shape[1] // 3
    return pl.pallas_call(
        own_kernel,
        in_specs=[VMEM] * 2,
        out_specs=VMEM,
        out_shape=jax.ShapeDtypeStruct((3, count, HS), jnp.float32),
        scratch_shapes=[pltpu.VMEM((3, count, 2 * HS), jnp.bfloat16)],
        compiler_params=params(24),
        cost_estimate=pl.CostEstimate(
            flops=12 * count * count * 256, bytes_accessed=8 * MIB, transcendentals=3 * count * count
        ),
        name="attend_own",
    )(q, kv)


def attend_halo(ok, q, before, after, own):
    groups, rows, _ = q.shape
    tokens = rows // 3
    count = groups * tokens
    return pl.pallas_call(
        halo_kernel,
        in_specs=[SMEM] + [VMEM] * 4,
        out_specs=VMEM,
        out_shape=jax.ShapeDtypeStruct((groups, HALF, tokens), jnp.float32),
        scratch_shapes=[
            pltpu.VMEM((3, count, 2 * HS), jnp.bfloat16),
            pltpu.VMEM((3, count, HS), jnp.float32),
        ],
        compiler_params=params(24),
        cost_estimate=pl.CostEstimate(
            flops=24 * count * count * 256, bytes_accessed=8 * MIB, transcendentals=6 * count * count
        ),
        name="attend_halo",
    )(ok, q, before, after, own)


def finish_kernel(position_ref, levels_ref, timesteps_ref, parts_ref, latent_ref, fresh_ref, velocity_ref, sent_ref):
    velocity = parts_ref[0]
    for s in range(1, parts_ref.shape[0]):
        velocity = velocity + parts_ref[s]
    level = levels_ref[0]
    step = timesteps_ref[jnp.maximum(level - 2, 0)] - timesteps_ref[level]
    velocity_ref[...] = velocity
    advanced = latent_ref[...] + (step.astype(jnp.float32) / 64.0) * velocity
    sent_ref[...] = jnp.where(position_ref[0] == 0, fresh_ref[...], advanced)


def finish(position, levels, timesteps, parts, latent_t, fresh_t):
    shape = jax.ShapeDtypeStruct(latent_t.shape, jnp.float32)
    return pl.pallas_call(
        finish_kernel,
        in_specs=[SMEM] * 3 + [VMEM] * 3,
        out_specs=[VMEM] * 2,
        out_shape=[shape, shape],
        name="finish",
    )(position, levels, timesteps, parts, latent_t, fresh_t)


def on_device(queries, key_proj, values, latents, head_weight, levels, timesteps, fresh_noise):
    position = lax.axis_index("queue")
    length = lax.axis_size("queue")
    groups = lax.axis_size("seq")
    kv = pack_kv(key_proj[0], values[0], head_weight.T, groups)
    kv = lax.all_to_all(kv, "seq", split_axis=0, concat_axis=0, tiled=True)
    q = pack_q(queries[0], groups)
    q = lax.all_to_all(q, "seq", split_axis=0, concat_axis=0, tiled=True)
    up = [(i, i + 1) for i in range(length - 1)]
    before = lax.ppermute(kv, "queue", up)
    after = lax.ppermute(kv, "queue", [(j, i) for i, j in up])
    own = attend_own(q, kv)
    ok = jnp.stack([position > 0, position < length - 1]).astype(jnp.int32)
    parts = attend_halo(ok, q, before, after, own)
    parts = lax.all_to_all(parts, "seq", split_axis=0, concat_axis=0, tiled=True)
    velocity, sent = finish(
        position[None].astype(jnp.int32), levels, timesteps, parts, latents[0].T, fresh_noise.T
    )
    shifted = lax.ppermute(sent, "queue", [(i, (i - 1) % length) for i in range(length)])
    return (shifted.T[None], velocity.T[None])


def solution(mesh):
    in_specs = (
        P("queue", "seq", None),
        P("queue", "seq", None),
        P("queue", "seq", None),
        P("queue", "seq", None),
        P(),
        P("queue"),
        P(),
        P("seq", None),
    )
    out_specs = (P("queue", "seq", None), P("queue", "seq", None))
    return jax.shard_map(
        on_device, mesh=mesh, in_specs=in_specs, out_specs=out_specs, check_vma=False
    )
```

time: 232 us -> 109 us (0.47)
  other arithmetic: 70.5 us -> 0.08 us
  local copies, waits for them, and re-layouts: 64.2 us -> 1.33 us
  Pallas kernels: 0 us -> 29.4 us
  matrix products: 16.1 us -> 0 us
  starting transfers between devices: 31.8 us -> 28.3 us
    unnamed x4 -> x0, other arithmetic: 57.2 us -> none
    unnamed x26 -> x3, local copies, waits for them, and re-layouts: 31.4 us -> 1.33 us
    pallas_call x0 -> x5, Pallas kernels: none -> 29.4 us  [the longest x1 12.6 us: attend_halo(): pl.pallas_call(halo_kernel, in_specs=[SMEM] + [VMEM] * 4, out_specs=VMEM,...]
    dot_general x13 -> x0, matrix products: 16.1 us -> none  [the longest x6 8.44 us: attend_block(): jnp.dot(probs, value_rows, preferred_element_type=jnp.float32)]
    another operation x5 -> x0, local copies, waits for them, and re-layouts: 15.9 us -> none  [the longest x1 5.89 us: attend_frame(): key_heads = key_frames.reshape(-1, heads_here, HS).transpose(1, 0, 2)]
    reduce_sum x7 -> x0, other arithmetic: 9.17 us -> none  [the longest x6 8.47 us: attend_block(): totals = jnp.sum(weights, axis=1)]
    all_to_all x4 -> x3, starting transfers between devices: 19.1 us -> 13 us  [the longest x1 5.83 us: on_device(): kv = lax.all_to_all(kv, 'seq', split_axis=0, concat_axis=0, tiled=True)]
    squeeze x3 -> x0, local copies, waits for them, and re-layouts: 4.42 us -> none  [attend_frame(): result = lax.map(per_head, (query_heads, key_heads, value_heads))]
  transfers between devices with their start and end apart: 7 -> 6, of which waited for: 4 -> 4; matrix products, arithmetic and copies ran while one was open for 23% -> 0% of each run, Pallas kernels for 0% -> 8%
where the time goes in v1:
time: 109 us; the launch traced here: 108 us
  waiting for transfers between devices  47.6 us (44%)
  Pallas kernels  29.4 us (27%)
  starting transfers between devices  28.3 us (26%)
  between operations  1.35 us (1%)
  local copies, waits for them, and re-layouts  1.33 us (1%)
    all_to_all x1, waiting for transfers between devices, on_device(): q = lax.all_to_all(q, 'seq', split_axis=0, concat_axis=0, tiled=True)  26.8 us
    pallas_call x1, Pallas kernels, attend_halo(): pl.pallas_call(halo_kernel, in_specs=[SMEM] + [VMEM] * 4, out_specs=VMEM,...  12.6 us
    all_to_all x1, waiting for transfers between devices, on_device(): kv = lax.all_to_all(kv, 'seq', split_axis=0, concat_axis=0, tiled=True)  11.1 us
    ppermute x1, starting transfers between devices, on_device(): before = lax.ppermute(kv, 'queue', up)  6.23 us
    pallas_call x1, Pallas kernels, pack_kv(): pl.pallas_call(pack_kv_kernel, grid=(groups,), in_specs=[pl.BlockSpec((to...  6.08 us
    all_to_all x1, starting transfers between devices, on_device(): kv = lax.all_to_all(kv, 'seq', split_axis=0, concat_axis=0, tiled=True)  5.83 us
    ppermute x1, starting transfers between devices, on_device(): lax.ppermute(sent, 'queue', [(i, (i - 1) % length) for i in range(length)])  5.54 us
    all_to_all x1, waiting for transfers between devices, on_device(): lax.all_to_all(parts, 'seq', split_axis=0, concat_axis=0, tiled=True)  5.42 us
  transfers between devices with their start and end apart: 6, of which 4 were waited for; matrix products, arithmetic and copies ran while one was open for 0% of the time, Pallas kernels for 8%

profile of v1, /device:TPU:185, one launch (start us, length us, event | category | flops | bytes accessed | tf_op | source)
XLA Modules:
  0.0 108.0 jit_solution(10281844386463458869)
XLA Ops:
  0.6 6.1 %pack_kv.1 = bf16[8,576,128]{2,1,0:T(8,128)(2,1)} custom-call(bf16[128,3072]{1,0:T(8,128)(2,1)} %bitcast.18, bf16[128,3072]{1,0:T(8,128)(2,1)} %bitcast.19, bf16[64,3072]{1,0:T(8,128)(2,1)} %bitcast.20), custom_call_target="tpu_custom_call" | custom-call | tf_op jit(solution)/shard_map/pack_kv/pallas_call | solution.py:46
  6.7 5.8 %all-to-all-start.1 = ((bf16[8,576,128]{2,1,0:T(8,128)(2,1)}), bf16[8,576,128]{2,1,0:T(8,128)(2,1)S(1)}, u32[]{:S(2)}, u32[]{:S(2)}) async-start(bf16[8,576,128]{2,1,0:T(8,128)(2,1)} %pack_kv.1), calls=%async_computation.1 | async-start | bytes 2359296 | tf_op jit(solution)/shard_map/all_to_all | solution.py:239
  12.5 5.1 %pack_q.1 = bf16[8,384,128]{2,1,0:T(8,128)(2,1)} custom-call(bf16[128,3072]{1,0:T(8,128)(2,1)} %bitcast.17), custom_call_target="tpu_custom_call" | custom-call | tf_op jit(solution)/shard_map/pack_q/pallas_call | solution.py:69
  17.6 11.1 %all-to-all-done.1.kv_ref = bf16[8,576,128]{2,1,0:T(8,128)(2,1)S(1)} async-done(((bf16[8,576,128]{2,1,0:T(8,128)(2,1)}), bf16[8,576,128]{2,1,0:T(8,128)(2,1)S(1)}, u32[]{:S(2)}, u32[]{:S(2)}) %all-to-all-start.1) | async-done | bytes 1179680 | tf_op jit(solution)/shard_map/all_to_all | solution.py:239
  28.8 3.8 %all-to-all-start = ((bf16[8,384,128]{2,1,0:T(8,128)(2,1)}), bf16[8,384,128]{2,1,0:T(8,128)(2,1)S(1)}, u32[]{:S(2)}, u32[]{:S(2)}) async-start(bf16[8,384,128]{2,1,0:T(8,128)(2,1)} %pack_q.1), calls=%async_computation | async-start | bytes 1572864 | tf_op jit(solution)/shard_map/all_to_all | solution.py:241
  32.6 3.5 %collective-permute-start.1 = (bf16[8,576,128]{2,1,0:T(8,128)(2,1)S(1)}, bf16[8,576,128]{2,1,0:T(8,128)(2,1)S(1)}, u32[]{:S(2)}, u32[]{:S(2)}) collective-permute-start(bf16[8,576,128]{2,1,0:T(8,128)(2,1)S(1)} %all-to-all-done.1.kv_ref), channel_id=1, source_target_pairs={{8,0},{16,8},{24,16},{32,24},{40,32},{48,40},{56,48},{64,56},{72,6... | collective-permute-start | bytes 3538952 | tf_op jit(solution)/shard_map/ppermute | solution.py:244
  36.1 6.2 %collective-permute-start = (bf16[8,576,128]{2,1,0:T(8,128)(2,1)S(1)}, bf16[8,576,128]{2,1,0:T(8,128)(2,1)}, u32[]{:S(2)}, u32[]{:S(2)}) collective-permute-start(bf16[8,576,128]{2,1,0:T(8,128)(2,1)S(1)} %all-to-all-done.1.kv_ref), channel_id=1, source_target_pairs={{0,8},{8,16},{16,24},{24,32},{32,40},{40,48},{48,56},{56,64},{64,7... | collective-permute-start | bytes 3538952 | tf_op jit(solution)/shard_map/ppermute | solution.py:243
  42.4 0.1 add_convert_fusion.ok_ref
  42.4 26.8 %all-to-all-done.query_ref = bf16[8,384,128]{2,1,0:T(8,128)(2,1)S(1)} async-done(((bf16[8,384,128]{2,1,0:T(8,128)(2,1)}), bf16[8,384,128]{2,1,0:T(8,128)(2,1)S(1)}, u32[]{:S(2)}, u32[]{:S(2)}) %all-to-all-start) | async-done | bytes 786464 | tf_op jit(solution)/shard_map/all_to_all | solution.py:241
  69.3 4.0 %attend_own.1.own_ref = f32[3,1024,128]{2,1,0:T(8,128)S(1)} custom-call(bf16[8,384,128]{2,1,0:T(8,128)(2,1)S(1)} %all-to-all-done.query_ref, bf16[8,576,128]{2,1,0:T(8,128)(2,1)S(1)} %all-to-all-done.1.kv_ref), custom_call_target="tpu_custom_call" | custom-call | flops 3221225472 | bytes 8388608 | tf_op jit(solution)/shard_map/attend_own/pallas_call | solution.py:177
  73.3 0.0 collective-permute-done.1.after_ref
  73.3 0.0 collective-permute-done.before_ref
  73.3 12.6 %attend_halo.1 = f32[8,64,128]{2,1,0:T(8,128)} custom-call(s32[2]{0:T(128)S(1)} %add_convert_fusion.ok_ref, bf16[8,384,128]{2,1,0:T(8,128)(2,1)S(1)} %all-to-all-done.query_ref, bf16[8,576,128]{2,1,0:T(8,128)(2,1)} %collective-permute-done.before_ref, bf16[8,576,128]{2,1,0:T(8,128)(2,1)S(1)} %collective-permute-done.1.after_ref, ...), custom_call_target="tpu_custom_call" | custom-call | flops 6442450944 | bytes 8388608 | tf_op jit(solution)/shard_map/attend_halo/pallas_call | solution.py:195
  85.9 3.4 %all-to-all-start.2 = ((f32[8,64,128]{2,1,0:T(8,128)}), f32[8,64,128]{2,1,0:T(8,128)S(1)}, u32[]{:S(2)}, u32[]{:S(2)}) async-start(f32[8,64,128]{2,1,0:T(8,128)} %attend_halo.1), calls=%async_computation.2 | async-start | bytes 524288 | tf_op jit(solution)/shard_map/all_to_all | solution.py:248
  89.9 5.4 %all-to-all-done.2.parts_ref = f32[8,64,128]{2,1,0:T(8,128)S(1)} async-done(((f32[8,64,128]{2,1,0:T(8,128)}), f32[8,64,128]{2,1,0:T(8,128)S(1)}, u32[]{:S(2)}, u32[]{:S(2)}) %all-to-all-start.2) | async-done | bytes 262176 | tf_op jit(solution)/shard_map/all_to_all | solution.py:248
  95.4 0.0 copy-start
  95.4 0.7 copy-done
  96.1 1.6 %finish.1 = (f32[64,128]{1,0:T(8,128)}, f32[64,128]{1,0:T(8,128)}) custom-call(s32[1]{0:T(128)} %bitcast.position_ref, s32[1]{0:T(128)S(6)} %copy.11.levels_ref, s32[257]{0:T(512)} %timesteps_ref.1, f32[8,64,128]{2,1,0:T(8,128)} %copy-done, f32[64,128]{1,0:T(8,128)} %bitcast.21, f32[64,128]{1,0:T(8,128)} %bitcast.22), custom_call_target="tpu_custom_call" | custom-call | tf_op jit(solution)/shard_map/finish/pallas_call | solution.py:225
  97.7 5.5 %collective-permute-start.2 = (f32[64,128]{1,0:T(8,128)}, f32[64,128]{1,0:T(8,128)S(1)}, u32[]{:S(2)}, u32[]{:S(2)}) collective-permute-start(f32[64,128]{1,0:T(8,128)} %get-tuple-element.4), channel_id=1, source_target_pairs={{0,504},{8,0},{16,8},{24,16},{32,24},{40,32},{48,40},{56,48},{64,5... | collective-permute-start | bytes 98312 | tf_op jit(solution)/shard_map/ppermute | solution.py:252
  103.2 4.2 %collective-permute-done.2 = f32[64,128]{1,0:T(8,128)S(1)} collective-permute-done((f32[64,128]{1,0:T(8,128)}, f32[64,128]{1,0:T(8,128)S(1)}, u32[]{:S(2)}, u32[]{:S(2)}) %collective-permute-start.2) | collective-permute-done | bytes 32800 | tf_op jit(solution)/shard_map/ppermute | solution.py:252
  107.4 0.6 copy.12
Async XLA Ops:
  6.7 22.1 %all-to-all-start.1 = ((bf16[8,576,128]{2,1,0:T(8,128)(2,1)}), bf16[8,576,128]{2,1,0:T(8,128)(2,1)S(1)}, u32[]{:S(2)}, u32[]{:S(2)}) async-start(bf16[8,576,128]{2,1,0:T(8,128)(2,1)} %pack_kv.1), calls=%async_computation.1 | async-start | bytes 2359296 | tf_op jit(solution)/shard_map/all_to_all | solution.py:239
  28.8 40.5 %all-to-all-start = ((bf16[8,384,128]{2,1,0:T(8,128)(2,1)}), bf16[8,384,128]{2,1,0:T(8,128)(2,1)S(1)}, u32[]{:S(2)}, u32[]{:S(2)}) async-start(bf16[8,384,128]{2,1,0:T(8,128)(2,1)} %pack_q.1), calls=%async_computation | async-start | bytes 1572864 | tf_op jit(solution)/shard_map/all_to_all | solution.py:241
  32.6 40.7 %collective-permute-start.1 = (bf16[8,576,128]{2,1,0:T(8,128)(2,1)S(1)}, bf16[8,576,128]{2,1,0:T(8,128)(2,1)S(1)}, u32[]{:S(2)}, u32[]{:S(2)}) collective-permute-start(bf16[8,576,128]{2,1,0:T(8,128)(2,1)S(1)} %all-to-all-done.1.kv_ref), channel_id=1, source_target_pairs={{8,0},{16,8},{24,16},{32,24},{40,32},{48,40},{56,48},{64,56},{72,6... | collective-permute-start | bytes 3538952 | tf_op jit(solution)/shard_map/ppermute | solution.py:244
  36.1 37.2 %collective-permute-start = (bf16[8,576,128]{2,1,0:T(8,128)(2,1)S(1)}, bf16[8,576,128]{2,1,0:T(8,128)(2,1)}, u32[]{:S(2)}, u32[]{:S(2)}) collective-permute-start(bf16[8,576,128]{2,1,0:T(8,128)(2,1)S(1)} %all-to-all-done.1.kv_ref), channel_id=1, source_target_pairs={{0,8},{8,16},{16,24},{24,32},{32,40},{40,48},{48,56},{56,64},{64,7... | collective-permute-start | bytes 3538952 | tf_op jit(solution)/shard_map/ppermute | solution.py:243
  85.9 9.5 %all-to-all-start.2 = ((f32[8,64,128]{2,1,0:T(8,128)}), f32[8,64,128]{2,1,0:T(8,128)S(1)}, u32[]{:S(2)}, u32[]{:S(2)}) async-start(f32[8,64,128]{2,1,0:T(8,128)} %attend_halo.1), calls=%async_computation.2 | async-start | bytes 524288 | tf_op jit(solution)/shard_map/all_to_all | solution.py:248
  95.4 0.7 copy-start
  97.7 9.7 %collective-permute-start.2 = (f32[64,128]{1,0:T(8,128)}, f32[64,128]{1,0:T(8,128)S(1)}, u32[]{:S(2)}, u32[]{:S(2)}) collective-permute-start(f32[64,128]{1,0:T(8,128)} %get-tuple-element.4), channel_id=1, source_target_pairs={{0,504},{8,0},{16,8},{24,16},{32,24},{40,32},{48,40},{56,48},{64,5... | collective-permute-start | bytes 98312 | tf_op jit(solution)/shard_map/ppermute | solution.py:252

commit v2 on v1

v2 whole, which is shorter than its diff:
```python
import math

import jax
import jax.numpy as jnp
from jax import lax
from jax.experimental import pallas as pl
from jax.experimental.pallas import tpu as pltpu
from jax.sharding import PartitionSpec as P

HS = 128
HALF = 64
MIB = 1 << 20
ROWS = 256
NT = (((1,), (1,)), ((), ()))
VMEM = pl.BlockSpec(memory_space=pltpu.VMEM)
HBM = pl.BlockSpec(memory_space=pltpu.HBM)
SMEM = pl.BlockSpec(memory_space=pltpu.SMEM)


def pack_kv_kernel(key_ref, value_ref, weight_ref, out_ref, value_buf, weight_buf, key_sem, value_sem, weight_sem):
    groups, rows, part = out_ref.shape
    tokens = rows * 2 // 3
    half = tokens // 2
    keys, values, weights = [], [], []
    for s in range(groups):
        span = pl.ds(s * part, part)
        values.append(pltpu.make_async_copy(value_ref.at[:, span], value_buf.at[s], value_sem.at[s]))
        weights.append(pltpu.make_async_copy(weight_ref.at[:, span], weight_buf.at[s], weight_sem.at[s]))
        keys.append(pltpu.make_async_copy(key_ref.at[:, span], out_ref.at[s, pl.ds(0, tokens)], key_sem.at[s]))
        values[s].start()
        weights[s].start()
    for s in range(groups):
        keys[s].start()
    zero = jnp.zeros((HALF, HS), jnp.bfloat16)

    def diagonal(x, y):
        return jnp.concatenate(
            [jnp.concatenate([x, zero], axis=1), jnp.concatenate([zero, y], axis=1)], axis=0
        )

    for s in range(groups):
        values[s].wait()
        weights[s].wait()
        weight = [weight_buf[s, :, h * HS : (h + 1) * HS] for h in range(3)]
        pair = lax.dot_general(
            value_buf[s, :, : 2 * HS],
            diagonal(weight[0], weight[1]),
            NT,
            preferred_element_type=jnp.float32,
        ).astype(jnp.bfloat16)
        last = jnp.concatenate([value_buf[s, :half, 2 * HS :], value_buf[s, half:, 2 * HS :]], axis=1)
        last = lax.dot_general(
            last, diagonal(weight[2], weight[2]), NT, preferred_element_type=jnp.float32
        ).astype(jnp.bfloat16)
        out_ref[s, tokens:, :HS] = pair[:half]
        out_ref[s, tokens:, HS : 2 * HS] = pair[half:]
        out_ref[s, tokens:, 2 * HS :] = last
    for s in range(groups):
        keys[s].wait()


def params(mib):
    return pltpu.CompilerParams(vmem_limit_bytes=mib * MIB)


def pack_kv(keys, values, weight_t, groups):
    tokens, width = keys.shape
    part = width // groups
    return pl.pallas_call(
        pack_kv_kernel,
        in_specs=[HBM] * 3,
        out_specs=VMEM,
        out_shape=jax.ShapeDtypeStruct((groups, tokens * 3 // 2, part), jnp.bfloat16),
        scratch_shapes=[
            pltpu.VMEM((groups, tokens, part), jnp.bfloat16),
            pltpu.VMEM((groups, HALF, part), jnp.bfloat16),
            pltpu.SemaphoreType.DMA((groups,)),
            pltpu.SemaphoreType.DMA((groups,)),
            pltpu.SemaphoreType.DMA((groups,)),
        ],
        compiler_params=params(8),
        name="pack_kv",
    )(keys, values, weight_t)


def pack_q_kernel(query_ref, out_ref, sem):
    groups, _, part = out_ref.shape
    copies = [
        pltpu.make_async_copy(query_ref.at[:, pl.ds(s * part, part)], out_ref.at[s], sem.at[s])
        for s in range(groups)
    ]
    for copy in copies:
        copy.start()
    for copy in copies:
        copy.wait()


def pack_q(queries, groups):
    tokens, width = queries.shape
    part = width // groups
    return pl.pallas_call(
        pack_q_kernel,
        in_specs=[HBM],
        out_specs=VMEM,
        out_shape=jax.ShapeDtypeStruct((groups, tokens, part), jnp.bfloat16),
        scratch_shapes=[pltpu.SemaphoreType.DMA((groups,))],
        compiler_params=params(4),
        name="pack_q",
    )(queries)


def scaled_queries(query_ref, split_ref):
    groups, tokens, _ = query_ref.shape
    scale = HS ** (-0.5) * math.log2(math.e)
    for h in range(3):
        q = query_ref[:, :, h * HS : (h + 1) * HS].reshape(groups * tokens, HS)
        q = q.astype(jnp.float32) * scale
        high = q.astype(jnp.bfloat16)
        low = (q - high.astype(jnp.float32)).astype(jnp.bfloat16)
        split_ref[h, :, :HS] = high
        split_ref[h, :, HS:] = low


def attend(split_ref, kv_ref, emit):
    groups, rows, _ = kv_ref.shape
    tokens = rows * 2 // 3
    count = groups * tokens
    pair = [kv_ref[:, tokens:, :HS], kv_ref[:, tokens:, HS : 2 * HS]]
    pair = jnp.concatenate(pair, axis=1).reshape(count, HS)
    last = kv_ref[:, tokens:, 2 * HS :]
    swapped = jnp.concatenate([last[:, :, HALF:], last[:, :, :HALF]], axis=2)
    last = jnp.concatenate([last, swapped], axis=1).reshape(count, HS)
    ones = jnp.ones((count, HS), jnp.bfloat16)
    for h in range(3):
        k = kv_ref[:, :tokens, h * HS : (h + 1) * HS].reshape(count, HS)
        keys = jnp.concatenate([k, k], axis=1)
        mix = jnp.concatenate([last if h == 2 else pair, ones], axis=1)
        for b in range(split_ref.shape[1] // ROWS):
            span = slice(b * ROWS, (b + 1) * ROWS)
            scores = lax.dot_general(split_ref[h, span, :], keys, NT, preferred_element_type=jnp.float32)
            peak = jnp.ceil(jnp.max(scores, axis=1, keepdims=True))
            probs = jnp.exp2(scores - peak).astype(jnp.bfloat16)
            emit(h, span, peak, jnp.dot(probs, mix, preferred_element_type=jnp.float32))


def lanes(h, rows):
    lane = lax.broadcasted_iota(jnp.int32, (rows, HS), 1)
    if h == 1:
        lane = HS - 1 - lane
    return lane


def packed(h, peak, mixed):
    lane = lanes(h, mixed.shape[0])
    return jnp.where(lane < HALF, mixed[:, :HS], jnp.where(lane < HALF + 32, mixed[:, HS:], peak))


def unpacked(h, state):
    total, peak = (HALF, HALF + 32) if h != 1 else (HALF - 1, 0)
    return state[:, total : total + 1], state[:, peak : peak + 1]


def merge_into(state_ref):
    def emit(h, span, peak, mixed):
        state = state_ref[h, span, :]
        _, old_peak = unpacked(h, state)
        new_peak = jnp.maximum(old_peak, peak)
        new = packed(h, new_peak, mixed)
        kept, added = jnp.exp2(old_peak - new_peak), jnp.exp2(peak - new_peak)
        lane = lanes(h, state.shape[0])
        state_ref[h, span, :] = jnp.where(lane < HALF + 32, state * kept + new * added, new)

    return emit


def own_kernel(query_ref, kv_ref, state_ref, split_ref):
    scaled_queries(query_ref, split_ref)

    def emit(h, span, peak, mixed):
        state_ref[h, span, :] = packed(h, peak, mixed)

    attend(split_ref, kv_ref, emit)


def near_kernel(ok_ref, split_ref, before_ref, after_ref, own_ref, state_ref):
    state_ref[...] = own_ref[...]
    for i, ref in enumerate((before_ref, after_ref)):
        @pl.when(ok_ref[i] > 0)
        def _():
            attend(split_ref, ref, merge_into(state_ref))


def far_kernel(ok_ref, split_ref, direct_ref, turned_ref, near_ref, out_ref, state_ref, kv_ref):
    state_ref[...] = near_ref[...]

    @pl.when(ok_ref[2] > 0)
    def _():
        cut = direct_ref.shape[0]
        kv_ref[:cut] = direct_ref[...]
        kv_ref[cut:] = turned_ref[...]
        attend(split_ref, kv_ref, merge_into(state_ref))

    groups, _, tokens = out_ref.shape
    for s in range(groups):
        span = slice(s * tokens, (s + 1) * tokens)
        parts = []
        for h in range(3):
            state = state_ref[h, span, :]
            total, _ = unpacked(h, state)
            parts.append(state / total)
        lane = lanes(0, tokens)
        both = jnp.where(lane < HALF, parts[0] + parts[2], parts[1])
        turned = both.T
        out_ref[s] = turned[:HALF] + turned[HALF:]


def cost(frames, count):
    return pl.CostEstimate(
        flops=frames * 12 * count * count * 256,
        bytes_accessed=4 * MIB,
        transcendentals=frames * 3 * count * count,
    )


def attend_own(q, kv):
    count = q.shape[0] * q.shape[1]
    return pl.pallas_call(
        own_kernel,
        in_specs=[VMEM] * 2,
        out_specs=[VMEM] * 2,
        out_shape=[
            jax.ShapeDtypeStruct((3, count, HS), jnp.float32),
            jax.ShapeDtypeStruct((3, count, 2 * HS), jnp.bfloat16),
        ],
        compiler_params=params(16),
        cost_estimate=cost(1, count),
        name="attend_own",
    )(q, kv)


def attend_near(ok, split, before, after, state):
    return pl.pallas_call(
        near_kernel,
        in_specs=[SMEM] + [VMEM] * 4,
        out_specs=VMEM,
        out_shape=jax.ShapeDtypeStruct(state.shape, jnp.float32),
        compiler_params=params(16),
        cost_estimate=cost(2, state.shape[1]),
        name="attend_near",
    )(ok, split, before, after, state)


def attend_far(ok, split, direct, turned, state, groups):
    count = state.shape[1]
    whole = (direct.shape[0] + turned.shape[0],) + direct.shape[1:]
    return pl.pallas_call(
        far_kernel,
        in_specs=[SMEM] + [VMEM] * 4,
        out_specs=VMEM,
        out_shape=jax.ShapeDtypeStruct((groups, HALF, count // groups), jnp.float32),
        scratch_shapes=[pltpu.VMEM(state.shape, jnp.float32), pltpu.VMEM(whole, jnp.bfloat16)],
        compiler_params=params(16),
        cost_estimate=cost(1, count),
        name="attend_far",
    )(ok, split, direct, turned, state)


def finish_kernel(position_ref, levels_ref, timesteps_ref, parts_ref, latent_ref, fresh_ref, velocity_ref, sent_ref):
    velocity = parts_ref[0]
    for s in range(1, parts_ref.shape[0]):
        velocity = velocity + parts_ref[s]
    level = levels_ref[0]
    step = timesteps_ref[jnp.maximum(level - 2, 0)] - timesteps_ref[level]
    velocity_ref[...] = velocity
    advanced = latent_ref[...] + (step.astype(jnp.float32) / 64.0) * velocity
    sent_ref[...] = jnp.where(position_ref[0] == 0, fresh_ref[...], advanced)


def finish(position, levels, timesteps, parts, latent_t, fresh_t):
    shape = jax.ShapeDtypeStruct(latent_t.shape, jnp.float32)
    return pl.pallas_call(
        finish_kernel,
        in_specs=[SMEM] * 3 + [VMEM] * 3,
        out_specs=[VMEM] * 2,
        out_shape=[shape, shape],
        compiler_params=params(2),
        name="finish",
    )(position, levels, timesteps, parts, latent_t, fresh_t)


def turned(pairs):
    return [(j, i) for i, j in pairs]


def on_device(queries, key_proj, values, latents, head_weight, levels, timesteps, fresh_noise):
    position = lax.axis_index("queue")
    length = lax.axis_size("queue")
    groups = lax.axis_size("seq")
    kv = pack_kv(key_proj[0], values[0], head_weight.T, groups)
    kv = lax.all_to_all(kv, "seq", split_axis=0, concat_axis=0, tiled=True)
    q = pack_q(queries[0], groups)
    q = lax.all_to_all(q, "seq", split_axis=0, concat_axis=0, tiled=True)
    column = length // 4
    up = [(i, i + 1) for i in range(length - 1) if (i + 1) % column]
    before = lax.ppermute(kv, "queue", up)
    after = lax.ppermute(kv, "queue", turned(up))
    cross = [(i, i + 1) for i in range(column - 1, length - 1, column)]
    along_z = [(i, i + column) for i, _ in cross] + [(j, j - column) for _, j in cross]
    along_y = [(i + column, j) for i, j in cross] + [(j - column, i) for i, j in cross]
    cut = groups * 5 // 8
    direct = lax.ppermute(kv[:cut], "queue", cross + turned(cross))
    carried = lax.ppermute(kv[cut:], "queue", along_z)
    carried = lax.ppermute(carried, "queue", along_y)
    place = position % column
    has_before, has_after = place > 0, place < column - 1
    has_far = ((place == 0) & (position > 0)) | ((place == column - 1) & (position < length - 1))
    ok = jnp.stack([has_before, has_after, has_far]).astype(jnp.int32)
    state, split = attend_own(q, kv)
    state = attend_near(ok, split, before, after, state)
    parts = attend_far(ok, split, direct, carried, state, groups)
    parts = lax.all_to_all(parts, "seq", split_axis=0, concat_axis=0, tiled=True)
    velocity, sent = finish(
        position[None].astype(jnp.int32), levels, timesteps, parts, latents[0].T, fresh_noise.T
    )
    shifted = lax.ppermute(sent, "queue", [(i, (i - 1) % length) for i in range(length)])
    return (shifted.T[None], velocity.T[None])


def solution(mesh):
    in_specs = (
        P("queue", "seq", None),
        P("queue", "seq", None),
        P("queue", "seq", None),
        P("queue", "seq", None),
        P(),
        P("queue"),
        P(),
        P("seq", None),
    )
    out_specs = (P("queue", "seq", None), P("queue", "seq", None))
    return jax.shard_map(
        on_device, mesh=mesh, in_specs=in_specs, out_specs=out_specs, check_vma=False
    )
```

time: 109 us -> 103 us (0.945)
  waiting for transfers between devices: 47.6 us -> 36.5 us
  starting transfers between devices: 28.3 us -> 35.1 us
  Pallas kernels: 29.4 us -> 23.9 us
  local copies, waits for them, and re-layouts: 1.33 us -> 5.65 us
    all_to_all x1, waiting for transfers between devices: 26.8 us -> 0.01 us  [on_device(): q = lax.all_to_all(q, 'seq', split_axis=0, concat_axis=0, tiled=True)]
    ppermute x1 -> x4, starting transfers between devices: 3.54 us -> 15.2 us  [the longest x1 6.11 us: on_device(): carried = lax.ppermute(kv[cut:], 'queue', along_z)]
    ppermute x1 -> x4, waiting for transfers between devices: 0.01 us -> 8.31 us  [the longest x1 5.25 us: on_device(): direct = lax.ppermute(kv[:cut], 'queue', cross + turned(cross))]
    pallas_call x4 -> x5, Pallas kernels: 27.8 us -> 22.7 us  [the longest x1 7.55 us: attend_far(): pl.pallas_call(far_kernel, in_specs=[SMEM] + [VMEM] * 4, out_specs=VMEM,...]
    ppermute x1, starting transfers between devices: 6.23 us -> 1.28 us  [on_device(): before = lax.ppermute(kv, 'queue', up)]
    all_to_all x1, waiting for transfers between devices: 11.1 us -> 15.1 us  [on_device(): kv = lax.all_to_all(kv, 'seq', split_axis=0, concat_axis=0, tiled=True)]
    ppermute x1, starting transfers between devices: 5.54 us -> 1.91 us  [on_device(): lax.ppermute(sent, 'queue', [(i, (i - 1) % length) for i in range(length)])]
    all_to_all x1, starting transfers between devices: 3.41 us -> 7.01 us  [on_device(): lax.all_to_all(parts, 'seq', split_axis=0, concat_axis=0, tiled=True)]
  transfers between devices with their start and end apart: 6 -> 9, of which waited for: 4 -> 5; matrix products, arithmetic and copies ran while one was open for 0% -> 2% of each run, Pallas kernels for 8% -> 12%
where the time goes in v2:
time: 103 us
  waiting for transfers between devices  36.5 us (35%)
  starting transfers between devices  35.1 us (34%)
  Pallas kernels  23.9 us (23%)
  local copies, waits for them, and re-layouts  5.65 us (5%)
  between operations  1.46 us (1%)
    all_to_all x1, waiting for transfers between devices, on_device(): kv = lax.all_to_all(kv, 'seq', split_axis=0, concat_axis=0, tiled=True)  15.1 us
    ppermute x1, waiting for transfers between devices, on_device(): lax.ppermute(sent, 'queue', [(i, (i - 1) % length) for i in range(length)])  7.58 us
    pallas_call x1, Pallas kernels, attend_far(): pl.pallas_call(far_kernel, in_specs=[SMEM] + [VMEM] * 4, out_specs=VMEM,...  7.55 us
    all_to_all x1, starting transfers between devices, on_device(): lax.all_to_all(parts, 'seq', split_axis=0, concat_axis=0, tiled=True)  7.01 us
    pallas_call x1, Pallas kernels, attend_near(): pl.pallas_call(near_kernel, in_specs=[SMEM] + [VMEM] * 4, out_specs=VMEM,...  6.75 us
    ppermute x1, starting transfers between devices, on_device(): carried = lax.ppermute(kv[cut:], 'queue', along_z)  6.11 us
    all_to_all x1, starting transfers between devices, on_device(): kv = lax.all_to_all(kv, 'seq', split_axis=0, concat_axis=0, tiled=True)  5.97 us
    all_to_all x1, waiting for transfers between devices, on_device(): lax.all_to_all(parts, 'seq', split_axis=0, concat_axis=0, tiled=True)  5.48 us
  transfers between devices with their start and end apart: 9, of which 5 were waited for; matrix products, arithmetic and copies ran while one was open for 2% of the time, Pallas kernels for 12%

profile of v2, /device:TPU:185, one launch (start us, length us, event | category | flops | bytes accessed | tf_op | source)
XLA Modules:
  0.0 102.7 jit_solution(15535389125574185110)
XLA Ops:
  0.6 0.0 copy-start.1
  0.6 1.1 %copy-done.1 = bf16[1,128,3072]{2,1,0:T(8,128)(2,1)S(1)} copy-done((bf16[1,128,3072]{2,1,0:T(8,128)(2,1)S(1)}, bf16[1,128,3072]{2,1,0:T(8,128)(2,1)}, u32[]{:S(2)}) %copy-start.1) | copy-done | bytes 786456
  1.8 0.0 copy-start.2
  1.8 1.1 %copy-done.2 = bf16[1,128,3072]{2,1,0:T(8,128)(2,1)S(1)} copy-done((bf16[1,128,3072]{2,1,0:T(8,128)(2,1)S(1)}, bf16[1,128,3072]{2,1,0:T(8,128)(2,1)}, u32[]{:S(2)}) %copy-start.2) | copy-done | bytes 786456
  2.9 0.0 copy-start.3
  2.9 1.0 copy-done.3
  3.9 3.1 %pack_kv.1 = bf16[8,192,384]{2,1,0:T(8,128)(2,1)} custom-call(bf16[128,3072]{1,0:T(8,128)(2,1)S(1)} %bitcast.19, bf16[128,3072]{1,0:T(8,128)(2,1)S(1)} %bitcast.20, bf16[64,3072]{1,0:T(8,128)(2,1)S(1)} %bitcast.21), custom_call_target="tpu_custom_call" | custom-call | tf_op jit(solution)/shard_map/pack_kv/pallas_call | solution.py:69
  7.0 0.0 copy-start
  7.0 6.0 %all-to-all-start.1 = ((bf16[8,192,384]{2,1,0:T(8,128)(2,1)}), bf16[8,192,384]{2,1,0:T(8,128)(2,1)S(1)}, u32[]{:S(2)}, u32[]{:S(2)}) async-start(bf16[8,192,384]{2,1,0:T(8,128)(2,1)} %pack_kv.1), calls=%async_computation.1 | async-start | bytes 2359296 | tf_op jit(solution)/shard_map/all_to_all | solution.py:300
  13.0 0.0 copy-done
  13.0 1.1 %pack_q.1 = bf16[8,128,384]{2,1,0:T(8,128)(2,1)} custom-call(bf16[128,3072]{1,0:T(8,128)(2,1)S(1)} %bitcast.18), custom_call_target="tpu_custom_call" | custom-call | tf_op jit(solution)/shard_map/pack_q/pallas_call | solution.py:101
  14.1 15.1 %all-to-all-done.1.kv_ref = bf16[8,192,384]{2,1,0:T(8,128)(2,1)S(1)} async-done(((bf16[8,192,384]{2,1,0:T(8,128)(2,1)}), bf16[8,192,384]{2,1,0:T(8,128)(2,1)S(1)}, u32[]{:S(2)}, u32[]{:S(2)}) %all-to-all-start.1) | async-done | bytes 1179680 | tf_op jit(solution)/shard_map/all_to_all | solution.py:300
  29.2 3.8 %all-to-all-start = ((bf16[8,128,384]{2,1,0:T(8,128)(2,1)}), bf16[8,128,384]{2,1,0:T(8,128)(2,1)S(1)}, u32[]{:S(2)}, u32[]{:S(2)}) async-start(bf16[8,128,384]{2,1,0:T(8,128)(2,1)} %pack_q.1), calls=%async_computation | async-start | bytes 1572864 | tf_op jit(solution)/shard_map/all_to_all | solution.py:302
  33.0 1.3 %collective-permute-start.3 = (bf16[8,192,384]{2,1,0:T(8,128)(2,1)S(1)}, bf16[8,192,384]{2,1,0:T(8,128)(2,1)S(1)}, u32[]{:S(2)}, u32[]{:S(2)}) collective-permute-start(bf16[8,192,384]{2,1,0:T(8,128)(2,1)S(1)} %all-to-all-done.1.kv_ref), channel_id=1, source_target_pairs={{0,8},{8,16},{16,24},{24,32},{32,40},{40,48},{48,56},{56,64},{64,7... | collective-permute-start | bytes 3538952 | tf_op jit(solution)/shard_map/ppermute | solution.py:305
  34.3 5.2 %collective-permute-start.4 = (bf16[8,192,384]{2,1,0:T(8,128)(2,1)S(1)}, bf16[8,192,384]{2,1,0:T(8,128)(2,1)}, u32[]{:S(2)}, u32[]{:S(2)}) collective-permute-start(bf16[8,192,384]{2,1,0:T(8,128)(2,1)S(1)} %all-to-all-done.1.kv_ref), channel_id=1, source_target_pairs={{8,0},{16,8},{24,16},{32,24},{40,32},{48,40},{56,48},{64,56},{72,6... | collective-permute-start | bytes 3538952 | tf_op jit(solution)/shard_map/ppermute | solution.py:306
  39.5 0.8 slice.9
  40.3 6.1 %collective-permute-start.1 = (bf16[3,192,384]{2,1,0:T(8,128)(2,1)}, bf16[3,192,384]{2,1,0:T(8,128)(2,1)}, u32[]{:S(2)}, u32[]{:S(2)}) collective-permute-start(bf16[3,192,384]{2,1,0:T(8,128)(2,1)} %slice.9), channel_id=1, source_target_pairs={{120,248},{248,376},{376,504},{128,0},{256,128},{384,256},{121,249... | collective-permute-start | bytes 1327112 | tf_op jit(solution)/shard_map/ppermute | solution.py:312
  46.5 0.1 add_convert_fusion.ok_ref
  46.6 1.0 slice.8
  47.5 1.9 %collective-permute-start = (bf16[5,192,384]{2,1,0:T(8,128)(2,1)}, bf16[5,192,384]{2,1,0:T(8,128)(2,1)}, u32[]{:S(2)}, u32[]{:S(2)}) collective-permute-start(bf16[5,192,384]{2,1,0:T(8,128)(2,1)} %slice.8), channel_id=1, source_target_pairs={{120,128},{248,256},{376,384},{128,120},{256,248},{384,376},{121,1... | collective-permute-start | bytes 2211848 | tf_op jit(solution)/shard_map/ppermute | solution.py:311
  49.4 0.0 all-to-all-done.query_ref
  49.4 4.2 %attend_own.1 = (f32[3,1024,128]{2,1,0:T(8,128)S(1)}, bf16[3,1024,256]{2,1,0:T(8,128)(2,1)S(1)}) custom-call(bf16[8,128,384]{2,1,0:T(8,128)(2,1)S(1)} %all-to-all-done.query_ref, bf16[8,192,384]{2,1,0:T(8,128)(2,1)S(1)} %all-to-all-done.1.kv_ref), custom_call_target="tpu_custom_call" | custom-call | flops 3221225472 | bytes 4194304 | tf_op jit(solution)/shard_map/attend_own/pallas_call | solution.py:227
  53.7 3.1 %collective-permute-done.1 = bf16[3,192,384]{2,1,0:T(8,128)(2,1)} collective-permute-done((bf16[3,192,384]{2,1,0:T(8,128)(2,1)}, bf16[3,192,384]{2,1,0:T(8,128)(2,1)}, u32[]{:S(2)}, u32[]{:S(2)}) %collective-permute-start.1) | collective-permute-done | bytes 442400 | tf_op jit(solution)/shard_map/ppermute | solution.py:312
  56.7 1.9 %collective-permute-start.2 = (bf16[3,192,384]{2,1,0:T(8,128)(2,1)}, bf16[3,192,384]{2,1,0:T(8,128)(2,1)S(1)}, u32[]{:S(2)}, u32[]{:S(2)}) collective-permute-start(bf16[3,192,384]{2,1,0:T(8,128)(2,1)} %collective-permute-done.1), channel_id=1, source_target_pairs={{248,128},{376,256},{504,384},{0,120},{128,248},{256,376},{249,129... | collective-permute-start | bytes 1327112 | tf_op jit(solution)/shard_map/ppermute | solution.py:313
  58.6 0.0 collective-permute-done.3.before_ref
  58.7 0.0 collective-permute-done.4.after_ref
  58.7 6.7 %attend_near.1.near_ref = f32[3,1024,128]{2,1,0:T(8,128)S(1)} custom-call(s32[3]{0:T(128)S(1)} %add_convert_fusion.ok_ref, bf16[3,1024,256]{2,1,0:T(8,128)(2,1)S(1)} %get-tuple-element.6.split_ref, bf16[8,192,384]{2,1,0:T(8,128)(2,1)S(1)} %collective-permute-done.3.before_ref, bf16[8,192,384]{2,1,0:T(8,128)(2,1)} %collective-permute-done.4.after_ref, ...), custom_call_target="tpu_custom_call" | custom-call | flops 6442450944 | bytes 4194304 | tf_op jit(solution)/shard_map/attend_near/pallas_call | solution.py:242
  65.4 0.0 copy-start.4
  65.4 0.0 copy-start.5
  65.4 0.0 copy-start.6
  65.5 5.2 %collective-permute-done.direct_ref = bf16[5,192,384]{2,1,0:T(8,128)(2,1)} collective-permute-done((bf16[5,192,384]{2,1,0:T(8,128)(2,1)}, bf16[5,192,384]{2,1,0:T(8,128)(2,1)}, u32[]{:S(2)}, u32[]{:S(2)}) %collective-permute-start) | collective-permute-done | bytes 737312 | tf_op jit(solution)/shard_map/ppermute | solution.py:311
  70.7 0.0 collective-permute-done.2.turned_ref
  70.7 7.5 %attend_far.1 = f32[8,64,128]{2,1,0:T(8,128)} custom-call(s32[3]{0:T(128)S(1)} %add_convert_fusion.ok_ref, bf16[3,1024,256]{2,1,0:T(8,128)(2,1)S(1)} %get-tuple-element.6.split_ref, bf16[5,192,384]{2,1,0:T(8,128)(2,1)} %collective-permute-done.direct_ref, bf16[3,192,384]{2,1,0:T(8,128)(2,1)S(1)} %collective-permute-done.2.turned_ref, ...), custom_call_target="tpu_custom_call" | custom-call | flops 3221225472 | bytes 4194304 | tf_op jit(solution)/shard_map/attend_far/pallas_call | solution.py:256
  78.3 7.0 %all-to-all-start.2 = ((f32[8,64,128]{2,1,0:T(8,128)}), f32[8,64,128]{2,1,0:T(8,128)S(1)}, u32[]{:S(2)}, u32[]{:S(2)}) async-start(f32[8,64,128]{2,1,0:T(8,128)} %attend_far.1), calls=%async_computation.2 | async-start | bytes 524288 | tf_op jit(solution)/shard_map/all_to_all | solution.py:321
  85.9 5.5 %all-to-all-done.2.parts_ref = f32[8,64,128]{2,1,0:T(8,128)S(1)} async-done(((f32[8,64,128]{2,1,0:T(8,128)}), f32[8,64,128]{2,1,0:T(8,128)S(1)}, u32[]{:S(2)}, u32[]{:S(2)}) %all-to-all-start.2) | async-done | bytes 262176 | tf_op jit(solution)/shard_map/all_to_all | solution.py:321
  91.4 0.0 copy-done.4
  91.4 0.0 copy-done.5
  91.4 0.0 copy-done.6
  91.4 1.2 %finish.1 = (f32[64,128]{1,0:T(8,128)}, f32[64,128]{1,0:T(8,128)S(1)}) custom-call(s32[1]{0:T(128)} %bitcast.position_ref, s32[1]{0:T(128)S(6)} %copy.11.levels_ref, s32[257]{0:T(512)S(1)} %copy-done.6, f32[8,64,128]{2,1,0:T(8,128)S(1)} %all-to-all-done.2.parts_ref, f32[64,128]{1,0:T(8,128)S(1)} %bitcast.22, f32[64,128]{1,0:T(8,128)S(1)} %bitcast.23), custom_call_target="tpu_custom_call" | custom-call | tf_op jit(solution)/shard_map/finish/pallas_call | solution.py:281
  92.6 1.9 %collective-permute-start.5 = (f32[64,128]{1,0:T(8,128)S(1)}, f32[64,128]{1,0:T(8,128)S(1)}, u32[]{:S(2)}, u32[]{:S(2)}) collective-permute-start(f32[64,128]{1,0:T(8,128)S(1)} %get-tuple-element.8), channel_id=1, source_target_pairs={{0,504},{8,0},{16,8},{24,16},{32,24},{40,32},{48,40},{56,48},{64,5... | collective-permute-start | bytes 98312 | tf_op jit(solution)/shard_map/ppermute | solution.py:325
  94.5 7.6 %collective-permute-done.5 = f32[64,128]{1,0:T(8,128)S(1)} collective-permute-done((f32[64,128]{1,0:T(8,128)S(1)}, f32[64,128]{1,0:T(8,128)S(1)}, u32[]{:S(2)}, u32[]{:S(2)}) %collective-permute-start.5) | collective-permute-done | bytes 32800 | tf_op jit(solution)/shard_map/ppermute | solution.py:325
  102.1 0.6 copy.12
Async XLA Ops:
  0.6 1.1 %copy-start.1 = (bf16[1,128,3072]{2,1,0:T(8,128)(2,1)S(1)}, bf16[1,128,3072]{2,1,0:T(8,128)(2,1)}, u32[]{:S(2)}) copy-start(bf16[1,128,3072]{2,1,0:T(8,128)(2,1)} %param.9) | copy-start | bytes 2359300
  1.8 1.1 %copy-start.2 = (bf16[1,128,3072]{2,1,0:T(8,128)(2,1)S(1)}, bf16[1,128,3072]{2,1,0:T(8,128)(2,1)}, u32[]{:S(2)}) copy-start(bf16[1,128,3072]{2,1,0:T(8,128)(2,1)} %param.10) | copy-start | bytes 2359300
  2.9 1.0 copy-start.3
  7.0 6.0 %copy-start = (bf16[1,128,3072]{2,1,0:T(8,128)(2,1)S(1)}, bf16[1,128,3072]{2,1,0:T(8,128)(2,1)}, u32[]{:S(2)}) copy-start(bf16[1,128,3072]{2,1,0:T(8,128)(2,1)} %param.8) | copy-start | bytes 2359300
  7.0 22.2 %all-to-all-start.1 = ((bf16[8,192,384]{2,1,0:T(8,128)(2,1)}), bf16[8,192,384]{2,1,0:T(8,128)(2,1)S(1)}, u32[]{:S(2)}, u32[]{:S(2)}) async-start(bf16[8,192,384]{2,1,0:T(8,128)(2,1)} %pack_kv.1), calls=%async_computation.1 | async-start | bytes 2359296 | tf_op jit(solution)/shard_map/all_to_all | solution.py:300
  29.2 20.2 %all-to-all-start = ((bf16[8,128,384]{2,1,0:T(8,128)(2,1)}), bf16[8,128,384]{2,1,0:T(8,128)(2,1)S(1)}, u32[]{:S(2)}, u32[]{:S(2)}) async-start(bf16[8,128,384]{2,1,0:T(8,128)(2,1)} %pack_q.1), calls=%async_computation | async-start | bytes 1572864 | tf_op jit(solution)/shard_map/all_to_all | solution.py:302
  33.0 25.6 %collective-permute-start.3 = (bf16[8,192,384]{2,1,0:T(8,128)(2,1)S(1)}, bf16[8,192,384]{2,1,0:T(8,128)(2,1)S(1)}, u32[]{:S(2)}, u32[]{:S(2)}) collective-permute-start(bf16[8,192,384]{2,1,0:T(8,128)(2,1)S(1)} %all-to-all-done.1.kv_ref), channel_id=1, source_target_pairs={{0,8},{8,16},{16,24},{24,32},{32,40},{40,48},{48,56},{56,64},{64,7... | collective-permute-start | bytes 3538952 | tf_op jit(solution)/shard_map/ppermute | solution.py:305
  34.3 24.4 %collective-permute-start.4 = (bf16[8,192,384]{2,1,0:T(8,128)(2,1)S(1)}, bf16[8,192,384]{2,1,0:T(8,128)(2,1)}, u32[]{:S(2)}, u32[]{:S(2)}) collective-permute-start(bf16[8,192,384]{2,1,0:T(8,128)(2,1)S(1)} %all-to-all-done.1.kv_ref), channel_id=1, source_target_pairs={{8,0},{16,8},{24,16},{32,24},{40,32},{48,40},{56,48},{64,56},{72,6... | collective-permute-start | bytes 3538952 | tf_op jit(solution)/shard_map/ppermute | solution.py:306
  40.3 16.4 %collective-permute-start.1 = (bf16[3,192,384]{2,1,0:T(8,128)(2,1)}, bf16[3,192,384]{2,1,0:T(8,128)(2,1)}, u32[]{:S(2)}, u32[]{:S(2)}) collective-permute-start(bf16[3,192,384]{2,1,0:T(8,128)(2,1)} %slice.9), channel_id=1, source_target_pairs={{120,248},{248,376},{376,504},{128,0},{256,128},{384,256},{121,249... | collective-permute-start | bytes 1327112 | tf_op jit(solution)/shard_map/ppermute | solution.py:312
  47.5 23.2 %collective-permute-start = (bf16[5,192,384]{2,1,0:T(8,128)(2,1)}, bf16[5,192,384]{2,1,0:T(8,128)(2,1)}, u32[]{:S(2)}, u32[]{:S(2)}) collective-permute-start(bf16[5,192,384]{2,1,0:T(8,128)(2,1)} %slice.8), channel_id=1, source_target_pairs={{120,128},{248,256},{376,384},{128,120},{256,248},{384,376},{121,1... | collective-permute-start | bytes 2211848 | tf_op jit(solution)/shard_map/ppermute | solution.py:311
  56.7 14.0 %collective-permute-start.2 = (bf16[3,192,384]{2,1,0:T(8,128)(2,1)}, bf16[3,192,384]{2,1,0:T(8,128)(2,1)S(1)}, u32[]{:S(2)}, u32[]{:S(2)}) collective-permute-start(bf16[3,192,384]{2,1,0:T(8,128)(2,1)} %collective-permute-done.1), channel_id=1, source_target_pairs={{248,128},{376,256},{504,384},{0,120},{128,248},{256,376},{249,129... | collective-permute-start | bytes 1327112 | tf_op jit(solution)/shard_map/ppermute | solution.py:313
  65.4 26.0 %copy-start.4 = (f32[1,128,64]{1,2,0:T(8,128)S(1)}, f32[1,128,64]{1,2,0:T(8,128)}, u32[]{:S(2)}) copy-start(f32[1,128,64]{1,2,0:T(8,128)} %param.11) | copy-start | bytes 98308
  65.4 26.0 %copy-start.5 = (f32[128,64]{0,1:T(8,128)S(1)}, f32[128,64]{0,1:T(8,128)}, u32[]{:S(2)}) copy-start(f32[128,64]{0,1:T(8,128)} %param.15) | copy-start | bytes 98308
  65.4 26.0 %copy-start.6 = (s32[257]{0:T(512)S(1)}, s32[257]{0:T(512)}, u32[]{:S(2)}) copy-start(s32[257]{0:T(512)} %timesteps_ref.1) | copy-start | bytes 3088
  78.3 13.1 %all-to-all-start.2 = ((f32[8,64,128]{2,1,0:T(8,128)}), f32[8,64,128]{2,1,0:T(8,128)S(1)}, u32[]{:S(2)}, u32[]{:S(2)}) async-start(f32[8,64,128]{2,1,0:T(8,128)} %attend_far.1), calls=%async_computation.2 | async-start | bytes 524288 | tf_op jit(solution)/shard_map/all_to_all | solution.py:321
  92.6 9.5 %collective-permute-start.5 = (f32[64,128]{1,0:T(8,128)S(1)}, f32[64,128]{1,0:T(8,128)S(1)}, u32[]{:S(2)}, u32[]{:S(2)}) collective-permute-start(f32[64,128]{1,0:T(8,128)S(1)} %get-tuple-element.8), channel_id=1, source_target_pairs={{0,504},{8,0},{16,8},{24,16},{32,24},{40,32},{48,40},{56,48},{64,5... | collective-permute-start | bytes 98312 | tf_op jit(solution)/shard_map/ppermute | solution.py:325

commit v3 on v2

v3 whole, which is shorter than its diff:
```python
import math

import jax
import jax.numpy as jnp
from jax import lax
from jax.experimental import pallas as pl
from jax.experimental.pallas import tpu as pltpu
from jax.sharding import PartitionSpec as P

HS = 128
HALF = 64
MIB = 1 << 20
ROWS = 256
PACK_MIB = 56
CUT = 5
NT = (((1,), (1,)), ((), ()))
VMEM = pl.BlockSpec(memory_space=pltpu.VMEM)
HBM = pl.BlockSpec(memory_space=pltpu.HBM)
SMEM = pl.BlockSpec(memory_space=pltpu.SMEM)


def pack_kernel(query_ref, key_ref, value_ref, weight_ref, out_ref, value_buf, weight_buf, query_sem, key_sem, value_sem, weight_sem):
    groups, rows, part = out_ref.shape
    tokens = rows * 2 // 5
    half = tokens // 2
    queries, keys, values, weights = [], [], [], []
    for s in range(groups):
        span = pl.ds(s * part, part)
        values.append(pltpu.make_async_copy(value_ref.at[:, span], value_buf.at[s], value_sem.at[s]))
        weights.append(pltpu.make_async_copy(weight_ref.at[:, span], weight_buf.at[s], weight_sem.at[s]))
        keys.append(pltpu.make_async_copy(key_ref.at[:, span], out_ref.at[s, pl.ds(tokens, tokens)], key_sem.at[s]))
        queries.append(pltpu.make_async_copy(query_ref.at[:, span], out_ref.at[s, pl.ds(0, tokens)], query_sem.at[s]))
        values[s].start()
        weights[s].start()
    for s in range(groups):
        queries[s].start()
        keys[s].start()
    zero = jnp.zeros((HALF, HS), jnp.bfloat16)

    def diagonal(x, y):
        return jnp.concatenate(
            [jnp.concatenate([x, zero], axis=1), jnp.concatenate([zero, y], axis=1)], axis=0
        )

    for s in range(groups):
        values[s].wait()
        weights[s].wait()
        weight = [weight_buf[s, :, h * HS : (h + 1) * HS] for h in range(3)]
        pair = lax.dot_general(
            value_buf[s, :, : 2 * HS],
            diagonal(weight[0], weight[1]),
            NT,
            preferred_element_type=jnp.float32,
        ).astype(jnp.bfloat16)
        last = jnp.concatenate([value_buf[s, :half, 2 * HS :], value_buf[s, half:, 2 * HS :]], axis=1)
        last = lax.dot_general(
            last, diagonal(weight[2], weight[2]), NT, preferred_element_type=jnp.float32
        ).astype(jnp.bfloat16)
        out_ref[s, 2 * tokens :, :HS] = pair[:half]
        out_ref[s, 2 * tokens :, HS : 2 * HS] = pair[half:]
        out_ref[s, 2 * tokens :, 2 * HS :] = last
    for s in range(groups):
        queries[s].wait()
        keys[s].wait()


def params(mib):
    return pltpu.CompilerParams(vmem_limit_bytes=mib * MIB)


def pack(queries, keys, values, weight_t, groups):
    tokens, width = keys.shape
    part = width // groups
    return pl.pallas_call(
        pack_kernel,
        in_specs=[HBM] * 4,
        out_specs=VMEM,
        out_shape=jax.ShapeDtypeStruct((groups, tokens * 5 // 2, part), jnp.bfloat16),
        scratch_shapes=[
            pltpu.VMEM((groups, tokens, part), jnp.bfloat16),
            pltpu.VMEM((groups, HALF, part), jnp.bfloat16),
        ]
        + [pltpu.SemaphoreType.DMA((groups,))] * 4,
        compiler_params=params(PACK_MIB),
        name="pack",
    )(queries, keys, values, weight_t)


def scaled_queries(query_ref, split_ref):
    groups, rows, _ = query_ref.shape
    tokens = rows * 2 // 5
    scale = HS ** (-0.5) * math.log2(math.e)
    for h in range(3):
        q = query_ref[:, :tokens, h * HS : (h + 1) * HS].reshape(groups * tokens, HS)
        q = q.astype(jnp.float32) * scale
        high = q.astype(jnp.bfloat16)
        low = (q - high.astype(jnp.float32)).astype(jnp.bfloat16)
        split_ref[h, :, :HS] = high
        split_ref[h, :, HS:] = low


def keys_and_values(ref, tokens, start, h):
    groups = ref.shape[0]
    count = groups * tokens
    k = ref[:, start : start + tokens, h * HS : (h + 1) * HS].reshape(count, HS)
    start += tokens
    if h == 2:
        first = ref[:, start : start + tokens // 2, 2 * HS :]
        second = jnp.concatenate([first[:, :, HALF:], first[:, :, :HALF]], axis=2)
    else:
        first = ref[:, start : start + tokens // 2, :HS]
        second = ref[:, start : start + tokens // 2, HS : 2 * HS]
    mix = jnp.concatenate([first, second], axis=1).reshape(count, HS)
    return k, mix


def attend(split_ref, sources, emit):
    for h in range(3):
        parts = [keys_and_values(ref, tokens, start, h) for ref, tokens, start in sources]
        k = jnp.concatenate([part[0] for part in parts], axis=0)
        mix = jnp.concatenate([part[1] for part in parts], axis=0)
        k = jnp.concatenate([k, k], axis=1)
        mix = jnp.concatenate([mix, jnp.ones_like(mix)], axis=1)
        for b in range(split_ref.shape[1] // ROWS):
            span = slice(b * ROWS, (b + 1) * ROWS)
            scores = lax.dot_general(split_ref[h, span, :], k, NT, preferred_element_type=jnp.float32)
            peak = jnp.ceil(jnp.max(scores, axis=1, keepdims=True))
            probs = jnp.exp2(scores - peak).astype(jnp.bfloat16)
            emit(h, span, peak, jnp.dot(probs, mix, preferred_element_type=jnp.float32))


def near_kernel(own_ref, mate_ref, sums_ref, totals_ref, peaks_ref, split_ref):
    scaled_queries(own_ref, split_ref)
    tokens = own_ref.shape[1] * 2 // 5

    def emit(h, span, peak, mixed):
        sums_ref[h, span, :] = mixed[:, :HS]
        totals_ref[h, span, :] = mixed[:, HS:]
        peaks_ref[h, span, :] = jnp.broadcast_to(peak, (ROWS, HS))

    attend(split_ref, [(own_ref, tokens, tokens), (mate_ref, tokens, tokens)], emit)


def far_kernel(flag_ref, split_ref, direct_ref, plain_ref, carried_ref, sums_ref, totals_ref, peaks_ref, out_ref, both_ref, rest_ref):
    tokens = direct_ref.shape[1] * 2 // 3
    chunk = out_ref.shape[2]

    def finish_head(h, span, sums, total):
        share = sums / total
        if h == 0:
            both_ref[span, :] = share
            return
        lane = lax.broadcasted_iota(jnp.int32, share.shape, 1)
        if h == 1:
            both_ref[span, :] = jnp.where(lane < HALF, both_ref[span, :], share)
            return
        whole = both_ref[span, :] + jnp.where(lane < HALF, share, 0.0)
        whole = whole.T
        whole = whole[:HALF] + whole[HALF:]
        for i in range(ROWS // chunk):
            out_ref[span.start // chunk + i] = whole[:, i * chunk : (i + 1) * chunk]

    @pl.when(flag_ref[1] > 0)
    def _():
        rest_ref[...] = carried_ref[...]

    @pl.when(flag_ref[1] == 0)
    def _():
        rest_ref[...] = plain_ref[...]

    def emit(h, span, peak, mixed):
        old_peak = peaks_ref[h, span, :]
        new_peak = jnp.maximum(old_peak, peak)
        kept, added = jnp.exp2(old_peak - new_peak), jnp.exp2(peak - new_peak)
        sums = sums_ref[h, span, :] * kept + mixed[:, :HS] * added
        total = totals_ref[h, span, :] * kept + mixed[:, HS:] * added
        finish_head(h, span, sums, total)

    @pl.when(flag_ref[0] > 0)
    def _():
        attend(split_ref, [(direct_ref, tokens, 0), (rest_ref, tokens, 0)], emit)

    @pl.when(flag_ref[0] == 0)
    def _():
        for h in range(3):
            for b in range(split_ref.shape[1] // ROWS):
                span = slice(b * ROWS, (b + 1) * ROWS)
                finish_head(h, span, sums_ref[h, span, :], totals_ref[h, span, :])


def cost(frames, count):
    return pl.CostEstimate(
        flops=frames * 12 * count * count * 256,
        bytes_accessed=4 * MIB,
        transcendentals=frames * 3 * count * count,
    )


def attend_near(own, mate):
    count = own.shape[0] * own.shape[1] * 2 // 5
    return pl.pallas_call(
        near_kernel,
        in_specs=[VMEM] * 2,
        out_specs=[VMEM] * 4,
        out_shape=[jax.ShapeDtypeStruct((3, count, HS), jnp.float32)] * 3
        + [jax.ShapeDtypeStruct((3, count, 2 * HS), jnp.bfloat16)],
        compiler_params=params(20),
        cost_estimate=cost(2, count),
        name="attend_near",
    )(own, mate)


def attend_far(flags, split, direct, plain, carried, state, groups):
    count = split.shape[1]
    return pl.pallas_call(
        far_kernel,
        in_specs=[SMEM] + [VMEM] * 7,
        out_specs=VMEM,
        out_shape=jax.ShapeDtypeStruct((groups, HALF, count // groups), jnp.float32),
        scratch_shapes=[pltpu.VMEM((count, HS), jnp.float32), pltpu.VMEM(plain.shape, jnp.bfloat16)],
        compiler_params=params(16),
        cost_estimate=cost(1, count),
        name="attend_far",
    )(flags, split, direct, plain, carried, *state)


def finish_kernel(position_ref, levels_ref, timesteps_ref, parts_ref, latent_ref, fresh_ref, velocity_ref, sent_ref):
    velocity = parts_ref[0]
    for s in range(1, parts_ref.shape[0]):
        velocity = velocity + parts_ref[s]
    level = levels_ref[0]
    step = timesteps_ref[jnp.maximum(level - 2, 0)] - timesteps_ref[level]
    velocity_ref[...] = velocity
    advanced = latent_ref[...] + (step.astype(jnp.float32) / 64.0) * velocity
    sent_ref[...] = jnp.where(position_ref[0] == 0, fresh_ref[...], advanced)


def finish(position, levels, timesteps, parts, latent_t, fresh_t):
    shape = jax.ShapeDtypeStruct(latent_t.shape, jnp.float32)
    return pl.pallas_call(
        finish_kernel,
        in_specs=[SMEM] * 3 + [VMEM] * 3,
        out_specs=[VMEM] * 2,
        out_shape=[shape, shape],
        compiler_params=params(2),
        name="finish",
    )(position, levels, timesteps, parts, latent_t, fresh_t)


def turned(pairs):
    return [(j, i) for i, j in pairs]


def on_device(queries, key_proj, values, latents, head_weight, levels, timesteps, fresh_noise):
    position = lax.axis_index("queue")
    length = lax.axis_size("queue")
    groups = lax.axis_size("seq")
    sent = pack(queries[0], key_proj[0], values[0], head_weight.T, groups)
    own = lax.all_to_all(sent, "seq", split_axis=0, concat_axis=0, tiled=True)
    kv = own[:, queries.shape[1] :]
    cut = groups * CUT // 8
    column = length // 4
    inner = [(i, i + 1) for i in range(1, length - 1, 2) if (i + 1) % column]
    cross = [(i, i + 1) for i in range(column - 1, length - 1, column)]
    along_z = [(i, i + column) for i, _ in cross] + [(j, j - column) for _, j in cross]
    along_y = [(i + column, j) for i, j in cross] + [(j - column, i) for i, j in cross]
    pairs = inner + cross
    direct = lax.ppermute(kv[:cut], "queue", pairs + turned(pairs))
    plain = lax.ppermute(kv[cut:], "queue", inner + turned(inner) + along_z)
    mates = [(i, i + 1) for i in range(0, length, 2)]
    mate = lax.ppermute(own, "queue", mates + turned(mates))
    carried = lax.ppermute(plain, "queue", along_y)
    place = position % column
    has_far = (position > 0) & (position < length - 1)
    at_cross = (place == 0) | (place == column - 1)
    flags = jnp.stack([has_far, at_cross]).astype(jnp.int32)
    *state, split = attend_near(own, mate)
    parts = attend_far(flags, split, direct, plain, carried, state, groups)
    parts = lax.all_to_all(parts, "seq", split_axis=0, concat_axis=0, tiled=True)
    velocity, sent = finish(
        position[None].astype(jnp.int32), levels, timesteps, parts, latents[0].T, fresh_noise.T
    )
    shifted = lax.ppermute(sent, "queue", [(i, (i - 1) % length) for i in range(length)])
    return (shifted.T[None], velocity.T[None])


def solution(mesh):
    in_specs = (
        P("queue", "seq", None),
        P("queue", "seq", None),
        P("queue", "seq", None),
        P("queue", "seq", None),
        P(),
        P("queue"),
        P(),
        P("seq", None),
    )
    out_specs = (P("queue", "seq", None), P("queue", "seq", None))
    return jax.shard_map(
        on_device, mesh=mesh, in_specs=in_specs, out_specs=out_specs, check_vma=False
    )
```

time: 103 us -> 99.2 us (0.963)
  blocking collectives: 0 us -> 30.7 us
  starting transfers between devices: 35.1 us -> 20.4 us
  waiting for transfers between devices: 36.5 us -> 22.3 us
  local copies, waits for them, and re-layouts: 5.65 us -> 2.42 us
  Pallas kernels: 23.9 us -> 21.5 us
    all_to_all x0 -> x1, blocking collectives: none -> 30.7 us  [on_device(): own = lax.all_to_all(sent, 'seq', split_axis=0, concat_axis=0, tiled=True)]
    all_to_all x2 -> x0, waiting for transfers between devices: 15.1 us -> none  [the longest x1 15.1 us: on_device(): kv = lax.all_to_all(kv, 'seq', split_axis=0, concat_axis=0, tiled=True)]
    all_to_all x2 -> x0, starting transfers between devices: 9.75 us -> none  [the longest x1 5.97 us: on_device(): kv = lax.all_to_all(kv, 'seq', split_axis=0, concat_axis=0, tiled=True)]
    all_to_all x1, starting transfers between devices: 7.01 us -> 3.41 us  [on_device(): lax.all_to_all(parts, 'seq', split_axis=0, concat_axis=0, tiled=True)]
    unnamed x15 -> x7, local copies, waits for them, and re-layouts: 3.89 us -> 0.63 us
    pallas_call x5 -> x3, Pallas kernels: 22.7 us -> 20.3 us  [the longest x1 9.89 us: attend_near(): pl.pallas_call(near_kernel, in_specs=[VMEM] * 2, out_specs=[VMEM] * 4, ou...]
    ppermute x5 -> x4, starting transfers between devices: 16.4 us -> 15.1 us  [the longest x1 6.11 us: on_device(): plain = lax.ppermute(kv[cut:], 'queue', inner + turned(inner) + along_z)]
    ppermute x5 -> x4, waiting for transfers between devices: 8.32 us -> 9.29 us  [the longest x1 6.5 us: on_device(): plain = lax.ppermute(kv[cut:], 'queue', inner + turned(inner) + along_z)]
  transfers between devices with their start and end apart: 9 -> 6, of which waited for: 5 -> 4; matrix products, arithmetic and copies ran while one was open for 2% -> 2% of each run, Pallas kernels for 12% -> 10%
where the time goes in v3:
time: 99.2 us; the launch traced here: 98.8 us
  blocking collectives  30.7 us (31%)
  waiting for transfers between devices  22.3 us (22%)
  Pallas kernels  21.5 us (22%)
  starting transfers between devices  20.4 us (21%)
  local copies, waits for them, and re-layouts  2.42 us (2%)
  between operations  1.39 us (1%)
    all_to_all x1, blocking collectives, on_device(): own = lax.all_to_all(sent, 'seq', split_axis=0, concat_axis=0, tiled=True)  30.7 us
    pallas_call x1, Pallas kernels, attend_near(): pl.pallas_call(near_kernel, in_specs=[VMEM] * 2, out_specs=[VMEM] * 4, ou...  9.89 us
    ppermute x1, waiting for transfers between devices, on_device(): lax.ppermute(sent, 'queue', [(i, (i - 1) % length) for i in range(length)])  7.59 us
    ppermute x1, waiting for transfers between devices, on_device(): plain = lax.ppermute(kv[cut:], 'queue', inner + turned(inner) + along_z)  6.5 us
    ppermute x1, starting transfers between devices, on_device(): plain = lax.ppermute(kv[cut:], 'queue', inner + turned(inner) + along_z)  6.11 us
    pallas_call x1, Pallas kernels, attend_far(): pl.pallas_call(far_kernel, in_specs=[SMEM] + [VMEM] * 7, out_specs=VMEM,...  6.03 us
    all_to_all x1, waiting for transfers between devices, on_device(): lax.all_to_all(parts, 'seq', split_axis=0, concat_axis=0, tiled=True)  5.42 us
    pallas_call x1, Pallas kernels, pack(): pl.pallas_call(pack_kernel, in_specs=[HBM] * 4, out_specs=VMEM, out_shape...  4.38 us
  transfers between devices with their start and end apart: 6, of which 4 were waited for; matrix products, arithmetic and copies ran while one was open for 2% of the time, Pallas kernels for 10%

profile of v3, /device:TPU:185, one launch (start us, length us, event | category | flops | bytes accessed | tf_op | source)
XLA Modules:
  0.0 98.8 jit_solution(3644094776494798026)
XLA Ops:
  0.6 4.4 %pack.1 = bf16[8,320,384]{2,1,0:T(8,128)(2,1)} custom-call(bf16[128,3072]{1,0:T(8,128)(2,1)} %bitcast.19, bf16[128,3072]{1,0:T(8,128)(2,1)} %bitcast.20, bf16[128,3072]{1,0:T(8,128)(2,1)} %bitcast.21, bf16[64,3072]{1,0:T(8,128)(2,1)} %bitcast.22), custom_call_target="tpu_custom_call" | custom-call | tf_op jit(solution)/shard_map/pack/pallas_call | solution.py:74
  5.0 30.7 %all_to_all.10.own_ref = bf16[8,320,384]{2,1,0:T(8,128)(2,1)S(1)} all-to-all(bf16[8,320,384]{2,1,0:T(8,128)(2,1)} %pack.1), channel_id=1, replica_groups=mesh['queue'=64,'seq'=8] {'seq'}, dimensions={0} | all-to-all | bytes 3932160 | tf_op jit(solution)/shard_map/all_to_all | solution.py:259
  35.7 3.8 %collective-permute-start = (bf16[8,320,384]{2,1,0:T(8,128)(2,1)S(1)}, bf16[8,320,384]{2,1,0:T(8,128)(2,1)}, u32[]{:S(2)}, u32[]{:S(2)}) collective-permute-start(bf16[8,320,384]{2,1,0:T(8,128)(2,1)S(1)} %all_to_all.10.own_ref), channel_id=1, source_target_pairs={{0,8},{16,24},{32,40},{48,56},{64,72},{80,88},{96,104},{112,120},{... | collective-permute-start | bytes 5898248 | tf_op jit(solution)/shard_map/ppermute | solution.py:271
  39.5 0.8 slice.12
  40.3 6.1 %collective-permute-start.2 = (bf16[3,192,384]{2,1,0:T(8,128)(2,1)}, bf16[3,192,384]{2,1,0:T(8,128)(2,1)S(1)}, u32[]{:S(2)}, u32[]{:S(2)}) collective-permute-start(bf16[3,192,384]{2,1,0:T(8,128)(2,1)} %slice.12), channel_id=1, source_target_pairs={{8,16},{24,32},{40,48},{56,64},{72,80},{88,96},{104,112},{136,144}... | collective-permute-start | bytes 1327112 | tf_op jit(solution)/shard_map/ppermute | solution.py:269
  46.4 1.0 slice.11
  47.4 1.9 %collective-permute-start.1 = (bf16[5,192,384]{2,1,0:T(8,128)(2,1)}, bf16[5,192,384]{2,1,0:T(8,128)(2,1)S(1)}, u32[]{:S(2)}, u32[]{:S(2)}) collective-permute-start(bf16[5,192,384]{2,1,0:T(8,128)(2,1)} %slice.11), channel_id=1, source_target_pairs={{8,16},{24,32},{40,48},{56,64},{72,80},{88,96},{104,112},{136,144}... | collective-permute-start | bytes 2211848 | tf_op jit(solution)/shard_map/ppermute | solution.py:268
  49.4 0.1 add_convert_fusion.flag_ref
  49.4 6.5 %collective-permute-done.2.plain_ref = bf16[3,192,384]{2,1,0:T(8,128)(2,1)S(1)} collective-permute-done((bf16[3,192,384]{2,1,0:T(8,128)(2,1)}, bf16[3,192,384]{2,1,0:T(8,128)(2,1)S(1)}, u32[]{:S(2)}, u32[]{:S(2)}) %collective-permute-start.2) | collective-permute-done | bytes 442400 | tf_op jit(solution)/shard_map/ppermute | solution.py:269
  55.9 3.3 %collective-permute-start.3 = (bf16[3,192,384]{2,1,0:T(8,128)(2,1)S(1)}, bf16[3,192,384]{2,1,0:T(8,128)(2,1)S(1)}, u32[]{:S(2)}, u32[]{:S(2)}) collective-permute-start(bf16[3,192,384]{2,1,0:T(8,128)(2,1)S(1)} %collective-permute-done.2.plain_ref), channel_id=1, source_target_pairs={{248,128},{376,256},{504,384},{0,120},{128,248},{256,376},{249,129... | collective-permute-start | bytes 1327112 | tf_op jit(solution)/shard_map/ppermute | solution.py:272
  59.2 0.0 collective-permute-done.mate_ref
  59.2 9.9 %attend_near.1 = (f32[3,1024,128]{2,1,0:T(8,128)S(1)}, f32[3,1024,128]{2,1,0:T(8,128)S(1)}, f32[3,1024,128]{2,1,0:T(8,128)S(1)}, bf16[3,1024,256]{2,1,0:T(8,128)(2,1)S(1)}) custom-call(bf16[8,320,384]{2,1,0:T(8,128)(2,1)S(1)} %all_to_all.10.own_ref, bf16[8,320,384]{2,1,0:T(8,128)(2,1)} %collective-permute-done.mate_ref), custom_call_target="tpu_custom_call" | custom-call | flops 6442450944 | bytes 4194304 | tf_op jit(solution)/shard_map/attend_near/pallas_call | solution.py:201
  69.1 2.8 %collective-permute-done.1.direct_ref = bf16[5,192,384]{2,1,0:T(8,128)(2,1)S(1)} collective-permute-done((bf16[5,192,384]{2,1,0:T(8,128)(2,1)}, bf16[5,192,384]{2,1,0:T(8,128)(2,1)S(1)}, u32[]{:S(2)}, u32[]{:S(2)}) %collective-permute-start.1) | collective-permute-done | bytes 737312 | tf_op jit(solution)/shard_map/ppermute | solution.py:268
  71.9 0.0 collective-permute-done.3.carried_ref
  71.9 0.0 copy-start
  71.9 0.0 copy-start.1
  71.9 0.0 copy-start.2
  71.9 6.0 %attend_far.1 = f32[8,64,128]{2,1,0:T(8,128)} custom-call(s32[2]{0:T(128)S(1)} %add_convert_fusion.flag_ref, bf16[3,1024,256]{2,1,0:T(8,128)(2,1)S(1)} %get-tuple-element.8.split_ref, bf16[5,192,384]{2,1,0:T(8,128)(2,1)S(1)} %collective-permute-done.1.direct_ref, bf16[3,192,384]{2,1,0:T(8,128)(2,1)S(1)} %collective-permute-done.2.plain_ref, ...), custom_call_target="tpu_custom_call" | custom-call | flops 3221225472 | bytes 4194304 | tf_op jit(solution)/shard_map/attend_far/pallas_call | solution.py:215
  78.0 3.4 %all-to-all-start.1 = ((f32[8,64,128]{2,1,0:T(8,128)}), f32[8,64,128]{2,1,0:T(8,128)S(1)}, u32[]{:S(2)}, u32[]{:S(2)}) async-start(f32[8,64,128]{2,1,0:T(8,128)} %attend_far.1), calls=%async_computation.1 | async-start | bytes 524288 | tf_op jit(solution)/shard_map/all_to_all | solution.py:279
  82.0 5.4 %all-to-all-done.1.parts_ref = f32[8,64,128]{2,1,0:T(8,128)S(1)} async-done(((f32[8,64,128]{2,1,0:T(8,128)}), f32[8,64,128]{2,1,0:T(8,128)S(1)}, u32[]{:S(2)}, u32[]{:S(2)}) %all-to-all-start.1) | async-done | bytes 262176 | tf_op jit(solution)/shard_map/all_to_all | solution.py:279
  87.5 0.0 copy-done
  87.5 0.0 copy-done.1
  87.5 0.0 copy-done.2
  87.5 1.2 %finish.1 = (f32[64,128]{1,0:T(8,128)}, f32[64,128]{1,0:T(8,128)S(1)}) custom-call(s32[1]{0:T(128)} %bitcast.position_ref, s32[1]{0:T(128)S(6)} %copy.11.levels_ref, s32[257]{0:T(512)S(1)} %copy-done.2, f32[8,64,128]{2,1,0:T(8,128)S(1)} %all-to-all-done.1.parts_ref, f32[64,128]{1,0:T(8,128)S(1)} %bitcast.17, f32[64,128]{1,0:T(8,128)S(1)} %bitcast.18), custom_call_target="tpu_custom_call" | custom-call | tf_op jit(solution)/shard_map/finish/pallas_call | solution.py:240
  88.7 1.9 %collective-permute-start.4 = (f32[64,128]{1,0:T(8,128)S(1)}, f32[64,128]{1,0:T(8,128)S(1)}, u32[]{:S(2)}, u32[]{:S(2)}) collective-permute-start(f32[64,128]{1,0:T(8,128)S(1)} %get-tuple-element.12), channel_id=1, source_target_pairs={{0,504},{8,0},{16,8},{24,16},{32,24},{40,32},{48,40},{56,48},{64,5... | collective-permute-start | bytes 98312 | tf_op jit(solution)/shard_map/ppermute | solution.py:283
  90.6 7.6 %collective-permute-done.4 = f32[64,128]{1,0:T(8,128)S(1)} collective-permute-done((f32[64,128]{1,0:T(8,128)S(1)}, f32[64,128]{1,0:T(8,128)S(1)}, u32[]{:S(2)}, u32[]{:S(2)}) %collective-permute-start.4) | collective-permute-done | bytes 32800 | tf_op jit(solution)/shard_map/ppermute | solution.py:283
  98.2 0.6 copy.12
Async XLA Ops:
  35.7 23.5 %collective-permute-start = (bf16[8,320,384]{2,1,0:T(8,128)(2,1)S(1)}, bf16[8,320,384]{2,1,0:T(8,128)(2,1)}, u32[]{:S(2)}, u32[]{:S(2)}) collective-permute-start(bf16[8,320,384]{2,1,0:T(8,128)(2,1)S(1)} %all_to_all.10.own_ref), channel_id=1, source_target_pairs={{0,8},{16,24},{32,40},{48,56},{64,72},{80,88},{96,104},{112,120},{... | collective-permute-start | bytes 5898248 | tf_op jit(solution)/shard_map/ppermute | solution.py:271
  40.3 15.6 %collective-permute-start.2 = (bf16[3,192,384]{2,1,0:T(8,128)(2,1)}, bf16[3,192,384]{2,1,0:T(8,128)(2,1)S(1)}, u32[]{:S(2)}, u32[]{:S(2)}) collective-permute-start(bf16[3,192,384]{2,1,0:T(8,128)(2,1)} %slice.12), channel_id=1, source_target_pairs={{8,16},{24,32},{40,48},{56,64},{72,80},{88,96},{104,112},{136,144}... | collective-permute-start | bytes 1327112 | tf_op jit(solution)/shard_map/ppermute | solution.py:269
  47.4 24.5 %collective-permute-start.1 = (bf16[5,192,384]{2,1,0:T(8,128)(2,1)}, bf16[5,192,384]{2,1,0:T(8,128)(2,1)S(1)}, u32[]{:S(2)}, u32[]{:S(2)}) collective-permute-start(bf16[5,192,384]{2,1,0:T(8,128)(2,1)} %slice.11), channel_id=1, source_target_pairs={{8,16},{24,32},{40,48},{56,64},{72,80},{88,96},{104,112},{136,144}... | collective-permute-start | bytes 2211848 | tf_op jit(solution)/shard_map/ppermute | solution.py:268
  55.9 16.0 %collective-permute-start.3 = (bf16[3,192,384]{2,1,0:T(8,128)(2,1)S(1)}, bf16[3,192,384]{2,1,0:T(8,128)(2,1)S(1)}, u32[]{:S(2)}, u32[]{:S(2)}) collective-permute-start(bf16[3,192,384]{2,1,0:T(8,128)(2,1)S(1)} %collective-permute-done.2.plain_ref), channel_id=1, source_target_pairs={{248,128},{376,256},{504,384},{0,120},{128,248},{256,376},{249,129... | collective-permute-start | bytes 1327112 | tf_op jit(solution)/shard_map/ppermute | solution.py:272
  71.9 15.5 %copy-start = (f32[1,128,64]{1,2,0:T(8,128)S(1)}, f32[1,128,64]{1,2,0:T(8,128)}, u32[]{:S(2)}) copy-start(f32[1,128,64]{1,2,0:T(8,128)} %param.11) | copy-start | bytes 98308
  71.9 15.5 %copy-start.1 = (f32[128,64]{0,1:T(8,128)S(1)}, f32[128,64]{0,1:T(8,128)}, u32[]{:S(2)}) copy-start(f32[128,64]{0,1:T(8,128)} %param.15) | copy-start | bytes 98308
  71.9 15.5 %copy-start.2 = (s32[257]{0:T(512)S(1)}, s32[257]{0:T(512)}, u32[]{:S(2)}) copy-start(s32[257]{0:T(512)} %timesteps_ref.1) | copy-start | bytes 3088
  78.0 9.5 %all-to-all-start.1 = ((f32[8,64,128]{2,1,0:T(8,128)}), f32[8,64,128]{2,1,0:T(8,128)S(1)}, u32[]{:S(2)}, u32[]{:S(2)}) async-start(f32[8,64,128]{2,1,0:T(8,128)} %attend_far.1), calls=%async_computation.1 | async-start | bytes 524288 | tf_op jit(solution)/shard_map/all_to_all | solution.py:279
  88.7 9.5 %collective-permute-start.4 = (f32[64,128]{1,0:T(8,128)S(1)}, f32[64,128]{1,0:T(8,128)S(1)}, u32[]{:S(2)}, u32[]{:S(2)}) collective-permute-start(f32[64,128]{1,0:T(8,128)S(1)} %get-tuple-element.12), channel_id=1, source_target_pairs={{0,504},{8,0},{16,8},{24,16},{32,24},{40,32},{48,40},{56,48},{64,5... | collective-permute-start | bytes 98312 | tf_op jit(solution)/shard_map/ppermute | solution.py:283

commit v4 on v3

--- a/solution.py
+++ b/solution.py
@@ -1,3 +1,4 @@
+import functools
 import math
 
 import jax
@@ -12,15 +13,16 @@
 MIB = 1 << 20
 ROWS = 256
 PACK_MIB = 56
-CUT = 5
+CUT = 6
 NT = (((1,), (1,)), ((), ()))
 VMEM = pl.BlockSpec(memory_space=pltpu.VMEM)
+ANY = pl.BlockSpec(memory_space=pl.ANY)
 HBM = pl.BlockSpec(memory_space=pltpu.HBM)
 SMEM = pl.BlockSpec(memory_space=pltpu.SMEM)
 
 
-def pack_kernel(query_ref, key_ref, value_ref, weight_ref, out_ref, value_buf, weight_buf, query_sem, key_sem, value_sem, weight_sem):
-    groups, rows, part = out_ref.shape
+def pack_kernel(position_ref, query_ref, key_ref, value_ref, weight_ref, out_ref, stage, value_buf, weight_buf, query_sem, key_sem, value_sem, weight_sem, out_sem):
+    groups, rows, part = stage.shape
     tokens = rows * 2 // 5
     half = tokens // 2
     queries, keys, values, weights = [], [], [], []
@@ -28,13 +30,12 @@
         span = pl.ds(s * part, part)
         values.append(pltpu.make_async_copy(value_ref.at[:, span], value_buf.at[s], value_sem.at[s]))
         weights.append(pltpu.make_async_copy(weight_ref.at[:, span], weight_buf.at[s], weight_sem.at[s]))
-        keys.append(pltpu.make_async_copy(key_ref.at[:, span], out_ref.at[s, pl.ds(tokens, tokens)], key_sem.at[s]))
-        queries.append(pltpu.make_async_copy(query_ref.at[:, span], out_ref.at[s, pl.ds(0, tokens)], query_sem.at[s]))
+        keys.append(pltpu.make_async_copy(key_ref.at[:, span], stage.at[s, pl.ds(tokens, tokens)], key_sem.at[s]))
+        queries.append(pltpu.make_async_copy(query_ref.at[:, span], stage.at[s, pl.ds(0, tokens)], query_sem.at[s]))
         values[s].start()
         weights[s].start()
-    for s in range(groups):
+        keys[s].start()
         queries[s].start()
-        keys[s].start()
     zero = jnp.zeros((HALF, HS), jnp.bfloat16)
 
     def diagonal(x, y):
@@ -42,6 +43,7 @@
             [jnp.concatenate([x, zero], axis=1), jnp.concatenate([zero, y], axis=1)], axis=0
         )
 
+    outs = []
     for s in range(groups):
         values[s].wait()
         weights[s].wait()
@@ -56,34 +58,38 @@
         last = lax.dot_general(
             last, diagonal(weight[2], weight[2]), NT, preferred_element_type=jnp.float32
         ).astype(jnp.bfloat16)
-        out_ref[s, 2 * tokens :, :HS] = pair[:half]
-        out_ref[s, 2 * tokens :, HS : 2 * HS] = pair[half:]
-        out_ref[s, 2 * tokens :, 2 * HS :] = last
-    for s in range(groups):
+        stage[s, 2 * tokens :, :HS] = pair[:half]
+        stage[s, 2 * tokens :, HS : 2 * HS] = pair[half:]
+        stage[s, 2 * tokens :, 2 * HS :] = last
+        keys[s].wait()
         queries[s].wait()
-        keys[s].wait()
+        outs.append(pltpu.make_async_copy(stage.at[s], out_ref.at[s], out_sem.at[s]))
+        outs[s].start()
+    for out in outs:
+        out.wait()
 
 
 def params(mib):
     return pltpu.CompilerParams(vmem_limit_bytes=mib * MIB)
 
 
-def pack(queries, keys, values, weight_t, groups):
+def pack(position, queries, keys, values, weight_t, groups):
     tokens, width = keys.shape
     part = width // groups
     return pl.pallas_call(
         pack_kernel,
-        in_specs=[HBM] * 4,
-        out_specs=VMEM,
+        in_specs=[SMEM] + [HBM] * 4,
+        out_specs=HBM,
         out_shape=jax.ShapeDtypeStruct((groups, tokens * 5 // 2, part), jnp.bfloat16),
         scratch_shapes=[
+            pltpu.VMEM((groups, tokens * 5 // 2, part), jnp.bfloat16),
             pltpu.VMEM((groups, tokens, part), jnp.bfloat16),
             pltpu.VMEM((groups, HALF, part), jnp.bfloat16),
         ]
-        + [pltpu.SemaphoreType.DMA((groups,))] * 4,
+        + [pltpu.SemaphoreType.DMA((groups,))] * 5,
         compiler_params=params(PACK_MIB),
         name="pack",
-    )(queries, keys, values, weight_t)
+    )(position, queries, keys, values, weight_t)
 
 
 def scaled_queries(query_ref, split_ref):
@@ -129,7 +135,13 @@
             emit(h, span, peak, jnp.dot(probs, mix, preferred_element_type=jnp.float32))
 
 
-def near_kernel(own_ref, mate_ref, sums_ref, totals_ref, peaks_ref, split_ref):
+def cut_kernel(own_ref, direct_ref, rest_ref):
+    cut, rows, _ = direct_ref.shape
+    direct_ref[...] = own_ref[:cut, -rows:, :]
+    rest_ref[...] = own_ref[cut:, -rows:, :]
+
+
+def near_kernel(own_ref, mate_ref, split_ref, sums_ref, totals_ref, peaks_ref):
     scaled_queries(own_ref, split_ref)
     tokens = own_ref.shape[1] * 2 // 5
 
@@ -141,7 +153,15 @@
     attend(split_ref, [(own_ref, tokens, tokens), (mate_ref, tokens, tokens)], emit)
 
 
-def far_kernel(flag_ref, split_ref, direct_ref, plain_ref, carried_ref, sums_ref, totals_ref, peaks_ref, out_ref, both_ref, rest_ref):
+def pass_kernel(rest_ref, after_ref, out_ref):
+    pass
+
+
+def far_kernel(column, length, position_ref, split_ref, direct_ref, plain_ref, carried_ref, sums_ref, totals_ref, peaks_ref, out_ref, both_ref, rest_ref):
+    position = position_ref[0]
+    place = lax.rem(position, column)
+    has_far = jnp.logical_and(position > 0, position < length - 1)
+    at_cross = jnp.logical_or(place == 0, place == column - 1)
     tokens = direct_ref.shape[1] * 2 // 3
     chunk = out_ref.shape[2]
 
@@ -160,15 +180,16 @@
         for i in range(ROWS // chunk):
             out_ref[span.start // chunk + i] = whole[:, i * chunk : (i + 1) * chunk]
 
-    @pl.when(flag_ref[1] > 0)
+    @pl.when(at_cross)
     def _():
         rest_ref[...] = carried_ref[...]
 
-    @pl.when(flag_ref[1] == 0)
+    @pl.when(jnp.logical_not(at_cross))
     def _():
         rest_ref[...] = plain_ref[...]
 
     def emit(h, span, peak, mixed):
+        peak = jnp.where(has_far, peak, -1e30)
         old_peak = peaks_ref[h, span, :]
         new_peak = jnp.maximum(old_peak, peak)
         kept, added = jnp.exp2(old_peak - new_peak), jnp.exp2(peak - new_peak)
@@ -176,16 +197,7 @@
         total = totals_ref[h, span, :] * kept + mixed[:, HS:] * added
         finish_head(h, span, sums, total)
 
-    @pl.when(flag_ref[0] > 0)
-    def _():
-        attend(split_ref, [(direct_ref, tokens, 0), (rest_ref, tokens, 0)], emit)
-
-    @pl.when(flag_ref[0] == 0)
-    def _():
-        for h in range(3):
-            for b in range(split_ref.shape[1] // ROWS):
-                span = slice(b * ROWS, (b + 1) * ROWS)
-                finish_head(h, span, sums_ref[h, span, :], totals_ref[h, span, :])
+    attend(split_ref, [(direct_ref, tokens, 0), (rest_ref, tokens, 0)], emit)
 
 
 def cost(frames, count):
@@ -196,24 +208,49 @@
     )
 
 
+def cut_rows(own, cut):
+    groups, rows, part = own.shape
+    rows = rows * 3 // 5
+    return pl.pallas_call(
+        cut_kernel,
+        in_specs=[VMEM],
+        out_specs=[VMEM] * 2,
+        out_shape=[jax.ShapeDtypeStruct((count, rows, part), own.dtype) for count in (cut, groups - cut)],
+        compiler_params=params(2),
+        name="cut_rows",
+    )(own)
+
+
+def passed_after(rest, after):
+    return pl.pallas_call(
+        pass_kernel,
+        in_specs=[ANY] * 2,
+        out_specs=ANY,
+        out_shape=jax.ShapeDtypeStruct(rest.shape, rest.dtype),
+        input_output_aliases={0: 0},
+        compiler_params=params(2),
+        name="passed_after",
+    )(rest, after)
+
+
 def attend_near(own, mate):
     count = own.shape[0] * own.shape[1] * 2 // 5
     return pl.pallas_call(
         near_kernel,
         in_specs=[VMEM] * 2,
         out_specs=[VMEM] * 4,
-        out_shape=[jax.ShapeDtypeStruct((3, count, HS), jnp.float32)] * 3
-        + [jax.ShapeDtypeStruct((3, count, 2 * HS), jnp.bfloat16)],
-        compiler_params=params(20),
+        out_shape=[jax.ShapeDtypeStruct((3, count, 2 * HS), jnp.bfloat16)]
+        + [jax.ShapeDtypeStruct((3, count, HS), jnp.float32)] * 3,
+        compiler_params=params(16),
         cost_estimate=cost(2, count),
         name="attend_near",
     )(own, mate)
 
 
-def attend_far(flags, split, direct, plain, carried, state, groups):
+def attend_far(position, split, direct, plain, carried, state, groups, column, length):
     count = split.shape[1]
     return pl.pallas_call(
-        far_kernel,
+        functools.partial(far_kernel, column, length),
         in_specs=[SMEM] + [VMEM] * 7,
         out_specs=VMEM,
         out_shape=jax.ShapeDtypeStruct((groups, HALF, count // groups), jnp.float32),
@@ -221,7 +258,7 @@
         compiler_params=params(16),
         cost_estimate=cost(1, count),
         name="attend_far",
-    )(flags, split, direct, plain, carried, *state)
+    )(position, split, direct, plain, carried, *state)
 
 
 def finish_kernel(position_ref, levels_ref, timesteps_ref, parts_ref, latent_ref, fresh_ref, velocity_ref, sent_ref):
@@ -252,33 +289,29 @@
 
 
 def on_device(queries, key_proj, values, latents, head_weight, levels, timesteps, fresh_noise):
-    position = lax.axis_index("queue")
+    position = lax.axis_index("queue")[None].astype(jnp.int32)
     length = lax.axis_size("queue")
     groups = lax.axis_size("seq")
-    sent = pack(queries[0], key_proj[0], values[0], head_weight.T, groups)
+    sent = pack(position, queries[0], key_proj[0], values[0], head_weight.T, groups)
     own = lax.all_to_all(sent, "seq", split_axis=0, concat_axis=0, tiled=True)
-    kv = own[:, queries.shape[1] :]
-    cut = groups * CUT // 8
+    direct, rest = cut_rows(own, groups * CUT // 8)
     column = length // 4
     inner = [(i, i + 1) for i in range(1, length - 1, 2) if (i + 1) % column]
     cross = [(i, i + 1) for i in range(column - 1, length - 1, column)]
     along_z = [(i, i + column) for i, _ in cross] + [(j, j - column) for _, j in cross]
     along_y = [(i + column, j) for i, j in cross] + [(j - column, i) for i, j in cross]
     pairs = inner + cross
-    direct = lax.ppermute(kv[:cut], "queue", pairs + turned(pairs))
-    plain = lax.ppermute(kv[cut:], "queue", inner + turned(inner) + along_z)
+    direct = lax.ppermute(direct, "queue", pairs + turned(pairs))
+    plain = lax.ppermute(rest, "queue", inner + turned(inner) + along_z)
     mates = [(i, i + 1) for i in range(0, length, 2)]
     mate = lax.ppermute(own, "queue", mates + turned(mates))
+    split, *state = attend_near(own, mate)
+    plain = passed_after(plain, split)
     carried = lax.ppermute(plain, "queue", along_y)
-    place = position % column
-    has_far = (position > 0) & (position < length - 1)
-    at_cross = (place == 0) | (place == column - 1)
-    flags = jnp.stack([has_far, at_cross]).astype(jnp.int32)
-    *state, split = attend_near(own, mate)
-    parts = attend_far(flags, split, direct, plain, carried, state, groups)
+    parts = attend_far(position, split, direct, plain, carried, state, groups, column, length)
     parts = lax.all_to_all(parts, "seq", split_axis=0, concat_axis=0, tiled=True)
     velocity, sent = finish(
-        position[None].astype(jnp.int32), levels, timesteps, parts, latents[0].T, fresh_noise.T
+        position, levels, timesteps, parts, latents[0].T, fresh_noise.T
     )
     shifted = lax.ppermute(sent, "queue", [(i, (i - 1) % length) for i in range(length)])
     return (shifted.T[None], velocity.T[None])

time: 99.2 us -> 99.2 us (level)
  waiting for transfers between devices: 22.3 us -> 28 us
  Pallas kernels: 21.5 us -> 18.1 us
  local copies, waits for them, and re-layouts: 2.42 us -> 0.63 us
    ppermute x2, waiting for transfers between devices: 9.29 us -> 15 us  [the longest x1 15 us: on_device(): direct = lax.ppermute(direct, 'queue', pairs + turned(pairs))]
    pallas_call x1, Pallas kernels: 9.89 us -> 7.72 us  [attend_near(): pl.pallas_call(near_kernel, in_specs=[VMEM] * 2, out_specs=[VMEM] * 4, ou...]
    slice x2 -> x0, local copies, waits for them, and re-layouts: 1.79 us -> none  [the longest x1 0.97 us: on_device(): direct = lax.ppermute(kv[:cut], 'queue', pairs + turned(pairs))]
    pallas_call x2 -> x4, Pallas kernels: 10.4 us -> 9.19 us  [the longest x1 5.25 us: attend_far(): pl.pallas_call(functools.partial(far_kernel, column, length), in_specs=[S...]
  transfers between devices with their start and end apart: 6 -> 6, of which waited for: 4 -> 3; matrix products, arithmetic and copies ran while one was open for 2% -> 0% of each run, Pallas kernels for 10% -> 8%
where the time goes in v4:
time: 99.2 us; the launch traced here: 98.7 us
  blocking collectives  30.7 us (31%)
  waiting for transfers between devices  28 us (28%)
  starting transfers between devices  19.9 us (20%)
  Pallas kernels  18.1 us (18%)
  between operations  1.39 us (1%)
    all_to_all x1, blocking collectives, on_device(): own = lax.all_to_all(sent, 'seq', split_axis=0, concat_axis=0, tiled=True)  30.7 us
    ppermute x1, waiting for transfers between devices, on_device(): direct = lax.ppermute(direct, 'queue', pairs + turned(pairs))  15 us
    pallas_call x1, Pallas kernels, attend_near(): pl.pallas_call(near_kernel, in_specs=[VMEM] * 2, out_specs=[VMEM] * 4, ou...  7.72 us
    ppermute x1, waiting for transfers between devices, on_device(): lax.ppermute(sent, 'queue', [(i, (i - 1) % length) for i in range(length)])  7.59 us
    ppermute x1, starting transfers between devices, on_device(): plain = lax.ppermute(rest, 'queue', inner + turned(inner) + along_z)  6.12 us
    all_to_all x1, waiting for transfers between devices, on_device(): lax.all_to_all(parts, 'seq', split_axis=0, concat_axis=0, tiled=True)  5.42 us
    pallas_call x1, Pallas kernels, attend_far(): pl.pallas_call(functools.partial(far_kernel, column, length), in_specs=[S...  5.25 us
    pallas_call x1, Pallas kernels, pack(): pl.pallas_call(pack_kernel, in_specs=[SMEM] + [HBM] * 4, out_specs=HBM, o...  3.84 us
  transfers between devices with their start and end apart: 6, of which 3 were waited for; matrix products, arithmetic and copies ran while one was open for 0% of the time, Pallas kernels for 8%

profile of v4, /device:TPU:185, one launch (start us, length us, event | category | flops | bytes accessed | tf_op | source)
XLA Modules:
  0.0 98.7 jit_solution(10708308586485206143)
XLA Ops:
  0.6 3.8 %pack.1 = bf16[8,320,384]{2,1,0:T(8,128)(2,1)} custom-call(s32[1]{0:T(128)} %bitcast.position_ref, bf16[128,3072]{1,0:T(8,128)(2,1)} %bitcast.17, bf16[128,3072]{1,0:T(8,128)(2,1)} %bitcast.18, bf16[128,3072]{1,0:T(8,128)(2,1)} %bitcast.19, bf16[64,3072]{1,0:T(8,128)(2,1)} %bitcast.20), custom_call_target="tpu_custom_call" | custom-call | tf_op jit(solution)/shard_map/pack/pallas_call | solution.py:79
  4.5 30.7 %all_to_all.10.own_ref = bf16[8,320,384]{2,1,0:T(8,128)(2,1)S(1)} all-to-all(bf16[8,320,384]{2,1,0:T(8,128)(2,1)} %pack.1), channel_id=1, replica_groups=mesh['queue'=64,'seq'=8] {'seq'}, dimensions={0} | all-to-all | bytes 3932160 | tf_op jit(solution)/shard_map/all_to_all | solution.py:296
  35.2 3.8 %collective-permute-start = (bf16[8,320,384]{2,1,0:T(8,128)(2,1)S(1)}, bf16[8,320,384]{2,1,0:T(8,128)(2,1)S(1)}, u32[]{:S(2)}, u32[]{:S(2)}) collective-permute-start(bf16[8,320,384]{2,1,0:T(8,128)(2,1)S(1)} %all_to_all.10.own_ref), channel_id=1, source_target_pairs={{0,8},{16,24},{32,40},{48,56},{64,72},{80,88},{96,104},{112,120},{... | collective-permute-start | bytes 5898248 | tf_op jit(solution)/shard_map/ppermute | solution.py:307
  39.0 0.1 cut_rows.1
  39.1 6.1 %collective-permute-start.2 = (bf16[2,192,384]{2,1,0:T(8,128)(2,1)S(1)}, bf16[2,192,384]{2,1,0:T(8,128)(2,1)S(1)}, u32[]{:S(2)}, u32[]{:S(2)}) collective-permute-start(bf16[2,192,384]{2,1,0:T(8,128)(2,1)S(1)} %get-tuple-element.12), channel_id=1, source_target_pairs={{8,16},{24,32},{40,48},{56,64},{72,80},{88,96},{104,112},{136,144}... | collective-permute-start | bytes 884744 | tf_op jit(solution)/shard_map/ppermute | solution.py:305
  45.2 1.9 %collective-permute-start.1 = (bf16[6,192,384]{2,1,0:T(8,128)(2,1)S(1)}, bf16[6,192,384]{2,1,0:T(8,128)(2,1)S(1)}, u32[]{:S(2)}, u32[]{:S(2)}) collective-permute-start(bf16[6,192,384]{2,1,0:T(8,128)(2,1)S(1)} %get-tuple-element.11), channel_id=1, source_target_pairs={{8,16},{24,32},{40,48},{56,64},{72,80},{88,96},{104,112},{136,144}... | collective-permute-start | bytes 2654216 | tf_op jit(solution)/shard_map/ppermute | solution.py:304
  47.2 0.0 collective-permute-done.mate_ref
  47.2 7.7 %attend_near.1 = (bf16[3,1024,256]{2,1,0:T(8,128)(2,1)S(1)}, f32[3,1024,128]{2,1,0:T(8,128)S(1)}, f32[3,1024,128]{2,1,0:T(8,128)S(1)}, f32[3,1024,128]{2,1,0:T(8,128)S(1)}) custom-call(bf16[8,320,384]{2,1,0:T(8,128)(2,1)S(1)} %all_to_all.10.own_ref, bf16[8,320,384]{2,1,0:T(8,128)(2,1)S(1)} %collective-permute-done.mate_ref), custom_call_target="tpu_custom_call" | custom-call | flops 6442450944 | bytes 4194304 | tf_op jit(solution)/shard_map/attend_near/pallas_call | solution.py:238
  54.9 0.0 collective-permute-done.2.rest_ref
  54.9 2.7 %collective-permute-start.3 = (bf16[2,192,384]{2,1,0:T(8,128)(2,1)S(1)}, bf16[2,192,384]{2,1,0:T(8,128)(2,1)S(1)}, u32[]{:S(2)}, u32[]{:S(2)}) collective-permute-start(bf16[2,192,384]{2,1,0:T(8,128)(2,1)S(1)} %passed_after.1.plain_ref), channel_id=1, source_target_pairs={{248,128},{376,256},{504,384},{0,120},{128,248},{256,376},{249,129... | collective-permute-start | bytes 884744 | tf_op jit(solution)/shard_map/ppermute | solution.py:310
  57.7 15.0 %collective-permute-done.1.direct_ref = bf16[6,192,384]{2,1,0:T(8,128)(2,1)S(1)} collective-permute-done((bf16[6,192,384]{2,1,0:T(8,128)(2,1)S(1)}, bf16[6,192,384]{2,1,0:T(8,128)(2,1)S(1)}, u32[]{:S(2)}, u32[]{:S(2)}) %collective-permute-start.1) | collective-permute-done | bytes 884768 | tf_op jit(solution)/shard_map/ppermute | solution.py:304
  72.6 0.0 collective-permute-done.3.carried_ref
  72.7 0.0 copy-start
  72.7 0.0 copy-start.1
  72.7 0.0 copy-start.2
  72.7 5.2 %attend_far.1 = f32[8,64,128]{2,1,0:T(8,128)} custom-call(s32[1]{0:T(128)} %bitcast.position_ref, bf16[3,1024,256]{2,1,0:T(8,128)(2,1)S(1)} %get-tuple-element.10.after_ref.split_ref, bf16[6,192,384]{2,1,0:T(8,128)(2,1)S(1)} %collective-permute-done.1.direct_ref, bf16[2,192,384]{2,1,0:T(8,128)(2,1)S(1)} %passed_after.1.plain_ref, ...), custom_call_target="tpu_custom_call" | custom-call | flops 3221225472 | bytes 4194304 | tf_op jit(solution)/shard_map/attend_far/pallas_call | solution.py:252
  77.9 3.4 %all-to-all-start.1 = ((f32[8,64,128]{2,1,0:T(8,128)}), f32[8,64,128]{2,1,0:T(8,128)S(1)}, u32[]{:S(2)}, u32[]{:S(2)}) async-start(f32[8,64,128]{2,1,0:T(8,128)} %attend_far.1), calls=%async_computation.1 | async-start | bytes 524288 | tf_op jit(solution)/shard_map/all_to_all | solution.py:312
  82.0 5.4 %all-to-all-done.1.parts_ref = f32[8,64,128]{2,1,0:T(8,128)S(1)} async-done(((f32[8,64,128]{2,1,0:T(8,128)}), f32[8,64,128]{2,1,0:T(8,128)S(1)}, u32[]{:S(2)}, u32[]{:S(2)}) %all-to-all-start.1) | async-done | bytes 262176 | tf_op jit(solution)/shard_map/all_to_all | solution.py:312
  87.4 0.0 copy-done
  87.4 0.0 copy-done.1
  87.4 0.0 copy-done.2
  87.4 1.2 %finish.1 = (f32[64,128]{1,0:T(8,128)}, f32[64,128]{1,0:T(8,128)S(1)}) custom-call(s32[1]{0:T(128)} %bitcast.position_ref, s32[1]{0:T(128)S(6)} %copy.13.levels_ref, s32[257]{0:T(512)S(1)} %copy-done.2, f32[8,64,128]{2,1,0:T(8,128)S(1)} %all-to-all-done.1.parts_ref, f32[64,128]{1,0:T(8,128)S(1)} %bitcast.15, f32[64,128]{1,0:T(8,128)S(1)} %bitcast.16), custom_call_target="tpu_custom_call" | custom-call | tf_op jit(solution)/shard_map/finish/pallas_call | solution.py:277
  88.6 1.9 %collective-permute-start.4 = (f32[64,128]{1,0:T(8,128)S(1)}, f32[64,128]{1,0:T(8,128)S(1)}, u32[]{:S(2)}, u32[]{:S(2)}) collective-permute-start(f32[64,128]{1,0:T(8,128)S(1)} %get-tuple-element.16), channel_id=1, source_target_pairs={{0,504},{8,0},{16,8},{24,16},{32,24},{40,32},{48,40},{56,48},{64,5... | collective-permute-start | bytes 98312 | tf_op jit(solution)/shard_map/ppermute | solution.py:316
  90.5 7.6 %collective-permute-done.4 = f32[64,128]{1,0:T(8,128)S(1)} collective-permute-done((f32[64,128]{1,0:T(8,128)S(1)}, f32[64,128]{1,0:T(8,128)S(1)}, u32[]{:S(2)}, u32[]{:S(2)}) %collective-permute-start.4) | collective-permute-done | bytes 32800 | tf_op jit(solution)/shard_map/ppermute | solution.py:316
  98.1 0.6 copy.14
  (1 shorter events, 0.0 us)
Async XLA Ops:
  35.2 11.9 %collective-permute-start = (bf16[8,320,384]{2,1,0:T(8,128)(2,1)S(1)}, bf16[8,320,384]{2,1,0:T(8,128)(2,1)S(1)}, u32[]{:S(2)}, u32[]{:S(2)}) collective-permute-start(bf16[8,320,384]{2,1,0:T(8,128)(2,1)S(1)} %all_to_all.10.own_ref), channel_id=1, source_target_pairs={{0,8},{16,24},{32,40},{48,56},{64,72},{80,88},{96,104},{112,120},{... | collective-permute-start | bytes 5898248 | tf_op jit(solution)/shard_map/ppermute | solution.py:307
  39.1 15.8 %collective-permute-start.2 = (bf16[2,192,384]{2,1,0:T(8,128)(2,1)S(1)}, bf16[2,192,384]{2,1,0:T(8,128)(2,1)S(1)}, u32[]{:S(2)}, u32[]{:S(2)}) collective-permute-start(bf16[2,192,384]{2,1,0:T(8,128)(2,1)S(1)} %get-tuple-element.12), channel_id=1, source_target_pairs={{8,16},{24,32},{40,48},{56,64},{72,80},{88,96},{104,112},{136,144}... | collective-permute-start | bytes 884744 | tf_op jit(solution)/shard_map/ppermute | solution.py:305
  45.2 27.4 %collective-permute-start.1 = (bf16[6,192,384]{2,1,0:T(8,128)(2,1)S(1)}, bf16[6,192,384]{2,1,0:T(8,128)(2,1)S(1)}, u32[]{:S(2)}, u32[]{:S(2)}) collective-permute-start(bf16[6,192,384]{2,1,0:T(8,128)(2,1)S(1)} %get-tuple-element.11), channel_id=1, source_target_pairs={{8,16},{24,32},{40,48},{56,64},{72,80},{88,96},{104,112},{136,144}... | collective-permute-start | bytes 2654216 | tf_op jit(solution)/shard_map/ppermute | solution.py:304
  54.9 17.7 %collective-permute-start.3 = (bf16[2,192,384]{2,1,0:T(8,128)(2,1)S(1)}, bf16[2,192,384]{2,1,0:T(8,128)(2,1)S(1)}, u32[]{:S(2)}, u32[]{:S(2)}) collective-permute-start(bf16[2,192,384]{2,1,0:T(8,128)(2,1)S(1)} %passed_after.1.plain_ref), channel_id=1, source_target_pairs={{248,128},{376,256},{504,384},{0,120},{128,248},{256,376},{249,129... | collective-permute-start | bytes 884744 | tf_op jit(solution)/shard_map/ppermute | solution.py:310
  72.7 14.7 %copy-start = (f32[1,128,64]{1,2,0:T(8,128)S(1)}, f32[1,128,64]{1,2,0:T(8,128)}, u32[]{:S(2)}) copy-start(f32[1,128,64]{1,2,0:T(8,128)} %param.11) | copy-start | bytes 98308
  72.7 14.7 %copy-start.1 = (f32[128,64]{0,1:T(8,128)S(1)}, f32[128,64]{0,1:T(8,128)}, u32[]{:S(2)}) copy-start(f32[128,64]{0,1:T(8,128)} %param.15) | copy-start | bytes 98308
  72.7 14.7 %copy-start.2 = (s32[257]{0:T(512)S(1)}, s32[257]{0:T(512)}, u32[]{:S(2)}) copy-start(s32[257]{0:T(512)} %timesteps_ref.1) | copy-start | bytes 3088
  77.9 9.5 %all-to-all-start.1 = ((f32[8,64,128]{2,1,0:T(8,128)}), f32[8,64,128]{2,1,0:T(8,128)S(1)}, u32[]{:S(2)}, u32[]{:S(2)}) async-start(f32[8,64,128]{2,1,0:T(8,128)} %attend_far.1), calls=%async_computation.1 | async-start | bytes 524288 | tf_op jit(solution)/shard_map/all_to_all | solution.py:312
  88.6 9.5 %collective-permute-start.4 = (f32[64,128]{1,0:T(8,128)S(1)}, f32[64,128]{1,0:T(8,128)S(1)}, u32[]{:S(2)}, u32[]{:S(2)}) collective-permute-start(f32[64,128]{1,0:T(8,128)S(1)} %get-tuple-element.16), channel_id=1, source_target_pairs={{0,504},{8,0},{16,8},{24,16},{32,24},{40,32},{48,40},{56,48},{64,5... | collective-permute-start | bytes 98312 | tf_op jit(solution)/shard_map/ppermute | solution.py:316

commit v5 on v4

--- a/solution.py
+++ b/solution.py
@@ -13,7 +13,7 @@
 MIB = 1 << 20
 ROWS = 256
 PACK_MIB = 56
-CUT = 6
+CUT = 5
 NT = (((1,), (1,)), ((), ()))
 VMEM = pl.BlockSpec(memory_space=pltpu.VMEM)
 ANY = pl.BlockSpec(memory_space=pl.ANY)
@@ -21,21 +21,19 @@
 SMEM = pl.BlockSpec(memory_space=pltpu.SMEM)
 
 
-def pack_kernel(position_ref, query_ref, key_ref, value_ref, weight_ref, out_ref, stage, value_buf, weight_buf, query_sem, key_sem, value_sem, weight_sem, out_sem):
+def pack_kv_kernel(position_ref, key_ref, value_ref, weight_ref, out_ref, stage, value_buf, weight_buf, key_sem, value_sem, weight_sem, out_sem):
     groups, rows, part = stage.shape
-    tokens = rows * 2 // 5
+    tokens = rows * 2 // 3
     half = tokens // 2
-    queries, keys, values, weights = [], [], [], []
+    keys, values, weights = [], [], []
     for s in range(groups):
         span = pl.ds(s * part, part)
         values.append(pltpu.make_async_copy(value_ref.at[:, span], value_buf.at[s], value_sem.at[s]))
         weights.append(pltpu.make_async_copy(weight_ref.at[:, span], weight_buf.at[s], weight_sem.at[s]))
-        keys.append(pltpu.make_async_copy(key_ref.at[:, span], stage.at[s, pl.ds(tokens, tokens)], key_sem.at[s]))
-        queries.append(pltpu.make_async_copy(query_ref.at[:, span], stage.at[s, pl.ds(0, tokens)], query_sem.at[s]))
+        keys.append(pltpu.make_async_copy(key_ref.at[:, span], stage.at[s, pl.ds(0, tokens)], key_sem.at[s]))
         values[s].start()
         weights[s].start()
         keys[s].start()
-        queries[s].start()
     zero = jnp.zeros((HALF, HS), jnp.bfloat16)
 
     def diagonal(x, y):
@@ -58,11 +56,10 @@
         last = lax.dot_general(
             last, diagonal(weight[2], weight[2]), NT, preferred_element_type=jnp.float32
         ).astype(jnp.bfloat16)
-        stage[s, 2 * tokens :, :HS] = pair[:half]
-        stage[s, 2 * tokens :, HS : 2 * HS] = pair[half:]
-        stage[s, 2 * tokens :, 2 * HS :] = last
+        stage[s, tokens:, :HS] = pair[:half]
+        stage[s, tokens:, HS : 2 * HS] = pair[half:]
+        stage[s, tokens:, 2 * HS :] = last
         keys[s].wait()
-        queries[s].wait()
         outs.append(pltpu.make_async_copy(stage.at[s], out_ref.at[s], out_sem.at[s]))
         outs[s].start()
     for out in outs:
@@ -73,31 +70,57 @@
     return pltpu.CompilerParams(vmem_limit_bytes=mib * MIB)
 
 
-def pack(position, queries, keys, values, weight_t, groups):
+def pack_kv(position, keys, values, weight_t, groups):
     tokens, width = keys.shape
     part = width // groups
-    return pl.pallas_call(
-        pack_kernel,
-        in_specs=[SMEM] + [HBM] * 4,
+    out = jax.ShapeDtypeStruct((groups, tokens * 3 // 2, part), jnp.bfloat16)
+    return pl.pallas_call(
+        pack_kv_kernel,
+        in_specs=[SMEM] + [HBM] * 3,
         out_specs=HBM,
-        out_shape=jax.ShapeDtypeStruct((groups, tokens * 5 // 2, part), jnp.bfloat16),
+        out_shape=out,
         scratch_shapes=[
-            pltpu.VMEM((groups, tokens * 5 // 2, part), jnp.bfloat16),
+            pltpu.VMEM(out.shape, jnp.bfloat16),
             pltpu.VMEM((groups, tokens, part), jnp.bfloat16),
             pltpu.VMEM((groups, HALF, part), jnp.bfloat16),
         ]
-        + [pltpu.SemaphoreType.DMA((groups,))] * 5,
+        + [pltpu.SemaphoreType.DMA((groups,))] * 4,
         compiler_params=params(PACK_MIB),
-        name="pack",
-    )(position, queries, keys, values, weight_t)
+        name="pack_kv",
+    )(position, keys, values, weight_t)
+
+
+def pack_q_kernel(query_ref, out_ref, sem):
+    groups, _, part = out_ref.shape
+    copies = [
+        pltpu.make_async_copy(query_ref.at[:, pl.ds(s * part, part)], out_ref.at[s], sem.at[s])
+        for s in range(groups)
+    ]
+    for copy in copies:
+        copy.start()
+    for copy in copies:
+        copy.wait()
+
+
+def pack_q(queries, groups):
+    tokens, width = queries.shape
+    part = width // groups
+    return pl.pallas_call(
+        pack_q_kernel,
+        in_specs=[HBM],
+        out_specs=VMEM,
+        out_shape=jax.ShapeDtypeStruct((groups, tokens, part), jnp.bfloat16),
+        scratch_shapes=[pltpu.SemaphoreType.DMA((groups,))],
+        compiler_params=params(PACK_MIB),
+        name="pack_q",
+    )(queries)
 
 
 def scaled_queries(query_ref, split_ref):
-    groups, rows, _ = query_ref.shape
-    tokens = rows * 2 // 5
+    groups, tokens, _ = query_ref.shape
     scale = HS ** (-0.5) * math.log2(math.e)
     for h in range(3):
-        q = query_ref[:, :tokens, h * HS : (h + 1) * HS].reshape(groups * tokens, HS)
+        q = query_ref[:, :, h * HS : (h + 1) * HS].reshape(groups * tokens, HS)
         q = q.astype(jnp.float32) * scale
         high = q.astype(jnp.bfloat16)
         low = (q - high.astype(jnp.float32)).astype(jnp.bfloat16)
@@ -136,21 +159,21 @@
 
 
 def cut_kernel(own_ref, direct_ref, rest_ref):
-    cut, rows, _ = direct_ref.shape
-    direct_ref[...] = own_ref[:cut, -rows:, :]
-    rest_ref[...] = own_ref[cut:, -rows:, :]
-
-
-def near_kernel(own_ref, mate_ref, split_ref, sums_ref, totals_ref, peaks_ref):
-    scaled_queries(own_ref, split_ref)
-    tokens = own_ref.shape[1] * 2 // 5
+    cut = direct_ref.shape[0]
+    direct_ref[...] = own_ref[:cut]
+    rest_ref[...] = own_ref[cut:]
+
+
+def near_kernel(query_ref, own_ref, mate_ref, split_ref, sums_ref, totals_ref, peaks_ref):
+    scaled_queries(query_ref, split_ref)
+    tokens = query_ref.shape[1]
 
     def emit(h, span, peak, mixed):
         sums_ref[h, span, :] = mixed[:, :HS]
         totals_ref[h, span, :] = mixed[:, HS:]
         peaks_ref[h, span, :] = jnp.broadcast_to(peak, (ROWS, HS))
 
-    attend(split_ref, [(own_ref, tokens, tokens), (mate_ref, tokens, tokens)], emit)
+    attend(split_ref, [(own_ref, tokens, 0), (mate_ref, tokens, 0)], emit)
 
 
 def pass_kernel(rest_ref, after_ref, out_ref):
@@ -210,7 +233,6 @@
 
 def cut_rows(own, cut):
     groups, rows, part = own.shape
-    rows = rows * 3 // 5
     return pl.pallas_call(
         cut_kernel,
         in_specs=[VMEM],
@@ -233,18 +255,18 @@
     )(rest, after)
 
 
-def attend_near(own, mate):
-    count = own.shape[0] * own.shape[1] * 2 // 5
+def attend_near(q, own, mate):
+    count = q.shape[0] * q.shape[1]
     return pl.pallas_call(
         near_kernel,
-        in_specs=[VMEM] * 2,
+        in_specs=[VMEM] * 3,
         out_specs=[VMEM] * 4,
         out_shape=[jax.ShapeDtypeStruct((3, count, 2 * HS), jnp.bfloat16)]
         + [jax.ShapeDtypeStruct((3, count, HS), jnp.float32)] * 3,
         compiler_params=params(16),
         cost_estimate=cost(2, count),
         name="attend_near",
-    )(own, mate)
+    )(q, own, mate)
 
 
 def attend_far(position, split, direct, plain, carried, state, groups, column, length):
@@ -292,20 +314,22 @@
     position = lax.axis_index("queue")[None].astype(jnp.int32)
     length = lax.axis_size("queue")
     groups = lax.axis_size("seq")
-    sent = pack(position, queries[0], key_proj[0], values[0], head_weight.T, groups)
-    own = lax.all_to_all(sent, "seq", split_axis=0, concat_axis=0, tiled=True)
-    direct, rest = cut_rows(own, groups * CUT // 8)
+    own = pack_kv(position, key_proj[0], values[0], head_weight.T, groups)
+    own = lax.all_to_all(own, "seq", split_axis=0, concat_axis=0, tiled=True)
+    first, rest = cut_rows(own, groups * CUT // 8)
     column = length // 4
     inner = [(i, i + 1) for i in range(1, length - 1, 2) if (i + 1) % column]
     cross = [(i, i + 1) for i in range(column - 1, length - 1, column)]
     along_z = [(i, i + column) for i, _ in cross] + [(j, j - column) for _, j in cross]
     along_y = [(i + column, j) for i, j in cross] + [(j - column, i) for i, j in cross]
     pairs = inner + cross
-    direct = lax.ppermute(direct, "queue", pairs + turned(pairs))
+    direct = lax.ppermute(first, "queue", pairs + turned(pairs))
     plain = lax.ppermute(rest, "queue", inner + turned(inner) + along_z)
     mates = [(i, i + 1) for i in range(0, length, 2)]
     mate = lax.ppermute(own, "queue", mates + turned(mates))
-    split, *state = attend_near(own, mate)
+    q = passed_after(pack_q(queries[0], groups), first)
+    q = lax.all_to_all(q, "seq", split_axis=0, concat_axis=0, tiled=True)
+    split, *state = attend_near(q, own, mate)
     plain = passed_after(plain, split)
     carried = lax.ppermute(plain, "queue", along_y)
     parts = attend_far(position, split, direct, plain, carried, state, groups, column, length)

time: 99.2 us -> 95.3 us (0.961)
  the two profiles are of different devices: /device:TPU:185 before, /device:TPU:57 now
where the time goes in v5:
time: 95.3 us; the launch traced here: 94.7 us
  waiting for transfers between devices  35.4 us (37%)
  starting transfers between devices  33.2 us (35%)
  Pallas kernels  20.9 us (22%)
  local copies, waits for them, and re-layouts  3.7 us (4%)
  between operations  1.41 us (1%)
    all_to_all x1, waiting for transfers between devices, on_device(): own = lax.all_to_all(own, 'seq', split_axis=0, concat_axis=0, tiled=True)  14.1 us
    ppermute x1, waiting for transfers between devices, on_device(): carried = lax.ppermute(plain, 'queue', along_y)  9.52 us
    pallas_call x1, Pallas kernels, attend_near(): pl.pallas_call(near_kernel, in_specs=[VMEM] * 3, out_specs=[VMEM] * 4, ou...  7.72 us
    ppermute x1, waiting for transfers between devices, on_device(): lax.ppermute(sent, 'queue', [(i, (i - 1) % length) for i in range(length)])  6.37 us
    pallas_call x1, Pallas kernels, attend_far(): pl.pallas_call(functools.partial(far_kernel, column, length), in_specs=[S...  6.34 us
    ppermute x1, starting transfers between devices, on_device(): plain = lax.ppermute(rest, 'queue', inner + turned(inner) + along_z)  6.14 us
    all_to_all x1, starting transfers between devices, on_device(): own = lax.all_to_all(own, 'seq', split_axis=0, concat_axis=0, tiled=True)  5.84 us
    all_to_all x1, starting transfers between devices, on_device(): lax.all_to_all(parts, 'seq', split_axis=0, concat_axis=0, tiled=True)  5.78 us
  transfers between devices with their start and end apart: 8, of which 4 were waited for; matrix products, arithmetic and copies ran while one was open for 0% of the time, Pallas kernels for 10%

profile of v5, /device:TPU:57, one launch (start us, length us, event | category | flops | bytes accessed | tf_op | source)
XLA Modules:
  0.0 94.7 jit_solution(3457770824005488264)
XLA Ops:
  0.6 3.4 %pack_kv.1 = bf16[8,192,384]{2,1,0:T(8,128)(2,1)} custom-call(s32[1]{0:T(128)} %bitcast.position_ref, bf16[128,3072]{1,0:T(8,128)(2,1)} %bitcast.18, bf16[128,3072]{1,0:T(8,128)(2,1)} %bitcast.19, bf16[64,3072]{1,0:T(8,128)(2,1)} %bitcast.20), custom_call_target="tpu_custom_call" | custom-call | tf_op jit(solution)/shard_map/pack_kv/pallas_call | solution.py:77
  4.0 5.8 %all-to-all-start = ((bf16[8,192,384]{2,1,0:T(8,128)(2,1)}), bf16[8,192,384]{2,1,0:T(8,128)(2,1)S(1)}, u32[]{:S(2)}, u32[]{:S(2)}) async-start(bf16[8,192,384]{2,1,0:T(8,128)(2,1)} %pack_kv.1), calls=%async_computation | async-start | bytes 2359296 | tf_op jit(solution)/shard_map/all_to_all | solution.py:318
  9.9 2.2 %pack_q.1.rest_ref = bf16[8,128,384]{2,1,0:T(8,128)(2,1)} custom-call(bf16[128,3072]{1,0:T(8,128)(2,1)} %bitcast.17), custom_call_target="tpu_custom_call" | custom-call | tf_op jit(solution)/shard_map/pack_q/pallas_call | solution.py:108
  12.1 14.1 %all-to-all-done.own_ref = bf16[8,192,384]{2,1,0:T(8,128)(2,1)S(1)} async-done(((bf16[8,192,384]{2,1,0:T(8,128)(2,1)}), bf16[8,192,384]{2,1,0:T(8,128)(2,1)S(1)}, u32[]{:S(2)}, u32[]{:S(2)}) %all-to-all-start) | async-done | bytes 1179680 | tf_op jit(solution)/shard_map/all_to_all | solution.py:318
  26.1 0.1 cut_rows.1
  26.2 0.0 copy-start.5
  26.2 0.8 copy-done.5
  27.0 3.8 %all-to-all-start.1 = ((bf16[8,128,384]{2,1,0:T(8,128)(2,1)}), bf16[8,128,384]{2,1,0:T(8,128)(2,1)S(1)}, u32[]{:S(2)}, u32[]{:S(2)}) async-start(bf16[8,128,384]{2,1,0:T(8,128)(2,1)} %passed_after.2), calls=%async_computation.1 | async-start | bytes 1572864 | tf_op jit(solution)/shard_map/all_to_all | solution.py:331
  30.8 3.5 %collective-permute-start = (bf16[8,192,384]{2,1,0:T(8,128)(2,1)S(1)}, bf16[8,192,384]{2,1,0:T(8,128)(2,1)S(1)}, u32[]{:S(2)}, u32[]{:S(2)}) collective-permute-start(bf16[8,192,384]{2,1,0:T(8,128)(2,1)S(1)} %all-to-all-done.own_ref), channel_id=1, source_target_pairs={{0,8},{16,24},{32,40},{48,56},{64,72},{80,88},{96,104},{112,120},{... | collective-permute-start | bytes 3538952 | tf_op jit(solution)/shard_map/ppermute | solution.py:329
  34.3 4.9 %collective-permute-start.1 = (bf16[5,192,384]{2,1,0:T(8,128)(2,1)S(1)}, bf16[5,192,384]{2,1,0:T(8,128)(2,1)}, u32[]{:S(2)}, u32[]{:S(2)}) collective-permute-start(bf16[5,192,384]{2,1,0:T(8,128)(2,1)S(1)} %get-tuple-element.10.after_ref), channel_id=1, source_target_pairs={{8,16},{24,32},{40,48},{56,64},{72,80},{88,96},{104,112},{136,144}... | collective-permute-start | bytes 2211848 | tf_op jit(solution)/shard_map/ppermute | solution.py:326
  39.2 6.1 %collective-permute-start.2 = (bf16[3,192,384]{2,1,0:T(8,128)(2,1)}, bf16[3,192,384]{2,1,0:T(8,128)(2,1)S(1)}, u32[]{:S(2)}, u32[]{:S(2)}) collective-permute-start(bf16[3,192,384]{2,1,0:T(8,128)(2,1)} %copy-done.5), channel_id=1, source_target_pairs={{8,16},{24,32},{40,48},{56,64},{72,80},{88,96},{104,112},{136,144}... | collective-permute-start | bytes 1327112 | tf_op jit(solution)/shard_map/ppermute | solution.py:327
  45.4 0.0 collective-permute-done.mate_ref
  45.4 0.0 copy-start.3
  45.4 1.0 %copy-done.3 = bf16[8,192,384]{2,1,0:T(8,128)(2,1)} copy-done((bf16[8,192,384]{2,1,0:T(8,128)(2,1)}, bf16[8,192,384]{2,1,0:T(8,128)(2,1)S(1)}, u32[]{:S(2)}) %copy-start.3) | copy-done | bytes 1179672
  46.5 0.0 all-to-all-done.1.query_ref
  46.5 0.0 copy-start.4
  46.5 1.3 %copy-done.4 = bf16[8,192,384]{2,1,0:T(8,128)(2,1)S(1)} copy-done((bf16[8,192,384]{2,1,0:T(8,128)(2,1)S(1)}, bf16[8,192,384]{2,1,0:T(8,128)(2,1)}, u32[]{:S(2)}) %copy-start.4) | copy-done | bytes 1179672
  47.7 7.7 %attend_near.1 = (bf16[3,1024,256]{2,1,0:T(8,128)(2,1)S(1)}, f32[3,1024,128]{2,1,0:T(8,128)S(1)}, f32[3,1024,128]{2,1,0:T(8,128)S(1)}, f32[3,1024,128]{2,1,0:T(8,128)S(1)}) custom-call(bf16[8,128,384]{2,1,0:T(8,128)(2,1)S(1)} %all-to-all-done.1.query_ref, bf16[8,192,384]{2,1,0:T(8,128)(2,1)S(1)} %all-to-all-done.own_ref, bf16[8,192,384]{2,1,0:T(8,128)(2,1)S(1)} %copy-done.4), custom_call_target="tpu_custom_call" | custom-call | flops 6442450944 | bytes 4194304 | tf_op jit(solution)/shard_map/attend_near/pallas_call | solution.py:260
  55.5 0.0 collective-permute-done.2.rest_ref
  55.5 1.3 %collective-permute-start.3 = (bf16[3,192,384]{2,1,0:T(8,128)(2,1)S(1)}, bf16[3,192,384]{2,1,0:T(8,128)(2,1)S(1)}, u32[]{:S(2)}, u32[]{:S(2)}) collective-permute-start(bf16[3,192,384]{2,1,0:T(8,128)(2,1)S(1)} %passed_after.3.plain_ref), channel_id=1, source_target_pairs={{248,128},{376,256},{504,384},{0,120},{128,248},{256,376},{249,129... | collective-permute-start | bytes 1327112 | tf_op jit(solution)/shard_map/ppermute | solution.py:334
  56.8 0.0 collective-permute-done.1.direct_ref
  56.8 9.5 %collective-permute-done.3.carried_ref = bf16[3,192,384]{2,1,0:T(8,128)(2,1)S(1)} collective-permute-done((bf16[3,192,384]{2,1,0:T(8,128)(2,1)S(1)}, bf16[3,192,384]{2,1,0:T(8,128)(2,1)S(1)}, u32[]{:S(2)}, u32[]{:S(2)}) %collective-permute-start.3) | collective-permute-done | bytes 442400 | tf_op jit(solution)/shard_map/ppermute | solution.py:334
  66.3 0.0 copy-start
  66.3 0.0 copy-start.1
  66.3 0.0 copy-start.2
  66.3 6.3 %attend_far.1 = f32[8,64,128]{2,1,0:T(8,128)} custom-call(s32[1]{0:T(128)} %bitcast.position_ref, bf16[3,1024,256]{2,1,0:T(8,128)(2,1)S(1)} %get-tuple-element.11.after_ref.split_ref, bf16[5,192,384]{2,1,0:T(8,128)(2,1)} %collective-permute-done.1.direct_ref, bf16[3,192,384]{2,1,0:T(8,128)(2,1)S(1)} %passed_after.3.plain_ref, ...), custom_call_target="tpu_custom_call" | custom-call | flops 3221225472 | bytes 4194304 | tf_op jit(solution)/shard_map/attend_far/pallas_call | solution.py:274
  72.7 5.8 %all-to-all-start.2 = ((f32[8,64,128]{2,1,0:T(8,128)}), f32[8,64,128]{2,1,0:T(8,128)S(1)}, u32[]{:S(2)}, u32[]{:S(2)}) async-start(f32[8,64,128]{2,1,0:T(8,128)} %attend_far.1), calls=%async_computation.2 | async-start | bytes 524288 | tf_op jit(solution)/shard_map/all_to_all | solution.py:336
  79.1 5.5 %all-to-all-done.2.parts_ref = f32[8,64,128]{2,1,0:T(8,128)S(1)} async-done(((f32[8,64,128]{2,1,0:T(8,128)}), f32[8,64,128]{2,1,0:T(8,128)S(1)}, u32[]{:S(2)}, u32[]{:S(2)}) %all-to-all-start.2) | async-done | bytes 262176 | tf_op jit(solution)/shard_map/all_to_all | solution.py:336
  84.6 0.0 copy-done
  84.6 0.0 copy-done.1
  84.6 0.0 copy-done.2
  84.6 1.2 %finish.1 = (f32[64,128]{1,0:T(8,128)}, f32[64,128]{1,0:T(8,128)S(1)}) custom-call(s32[1]{0:T(128)} %bitcast.position_ref, s32[1]{0:T(128)S(6)} %copy.15.levels_ref, s32[257]{0:T(512)S(1)} %copy-done.2, f32[8,64,128]{2,1,0:T(8,128)S(1)} %all-to-all-done.2.parts_ref, f32[64,128]{1,0:T(8,128)S(1)} %bitcast.15, f32[64,128]{1,0:T(8,128)S(1)} %bitcast.16), custom_call_target="tpu_custom_call" | custom-call | tf_op jit(solution)/shard_map/finish/pallas_call | solution.py:299
  85.8 1.9 %collective-permute-start.4 = (f32[64,128]{1,0:T(8,128)S(1)}, f32[64,128]{1,0:T(8,128)S(1)}, u32[]{:S(2)}, u32[]{:S(2)}) collective-permute-start(f32[64,128]{1,0:T(8,128)S(1)} %get-tuple-element.16), channel_id=1, source_target_pairs={{0,504},{8,0},{16,8},{24,16},{32,24},{40,32},{48,40},{56,48},{64,5... | collective-permute-start | bytes 98312 | tf_op jit(solution)/shard_map/ppermute | solution.py:340
  87.7 6.4 %collective-permute-done.4 = f32[64,128]{1,0:T(8,128)S(1)} collective-permute-done((f32[64,128]{1,0:T(8,128)S(1)}, f32[64,128]{1,0:T(8,128)S(1)}, u32[]{:S(2)}, u32[]{:S(2)}) %collective-permute-start.4) | collective-permute-done | bytes 32800 | tf_op jit(solution)/shard_map/ppermute | solution.py:340
  94.1 0.6 copy.16
  (2 shorter events, 0.0 us)
Async XLA Ops:
  4.0 22.1 %all-to-all-start = ((bf16[8,192,384]{2,1,0:T(8,128)(2,1)}), bf16[8,192,384]{2,1,0:T(8,128)(2,1)S(1)}, u32[]{:S(2)}, u32[]{:S(2)}) async-start(bf16[8,192,384]{2,1,0:T(8,128)(2,1)} %pack_kv.1), calls=%async_computation | async-start | bytes 2359296 | tf_op jit(solution)/shard_map/all_to_all | solution.py:318
  26.2 0.8 copy-start.5
  27.0 19.5 %all-to-all-start.1 = ((bf16[8,128,384]{2,1,0:T(8,128)(2,1)}), bf16[8,128,384]{2,1,0:T(8,128)(2,1)S(1)}, u32[]{:S(2)}, u32[]{:S(2)}) async-start(bf16[8,128,384]{2,1,0:T(8,128)(2,1)} %passed_after.2), calls=%async_computation.1 | async-start | bytes 1572864 | tf_op jit(solution)/shard_map/all_to_all | solution.py:331
  30.8 14.6 %collective-permute-start = (bf16[8,192,384]{2,1,0:T(8,128)(2,1)S(1)}, bf16[8,192,384]{2,1,0:T(8,128)(2,1)S(1)}, u32[]{:S(2)}, u32[]{:S(2)}) collective-permute-start(bf16[8,192,384]{2,1,0:T(8,128)(2,1)S(1)} %all-to-all-done.own_ref), channel_id=1, source_target_pairs={{0,8},{16,24},{32,40},{48,56},{64,72},{80,88},{96,104},{112,120},{... | collective-permute-start | bytes 3538952 | tf_op jit(solution)/shard_map/ppermute | solution.py:329
  34.3 22.5 %collective-permute-start.1 = (bf16[5,192,384]{2,1,0:T(8,128)(2,1)S(1)}, bf16[5,192,384]{2,1,0:T(8,128)(2,1)}, u32[]{:S(2)}, u32[]{:S(2)}) collective-permute-start(bf16[5,192,384]{2,1,0:T(8,128)(2,1)S(1)} %get-tuple-element.10.after_ref), channel_id=1, source_target_pairs={{8,16},{24,32},{40,48},{56,64},{72,80},{88,96},{104,112},{136,144}... | collective-permute-start | bytes 2211848 | tf_op jit(solution)/shard_map/ppermute | solution.py:326
  39.2 16.2 %collective-permute-start.2 = (bf16[3,192,384]{2,1,0:T(8,128)(2,1)}, bf16[3,192,384]{2,1,0:T(8,128)(2,1)S(1)}, u32[]{:S(2)}, u32[]{:S(2)}) collective-permute-start(bf16[3,192,384]{2,1,0:T(8,128)(2,1)} %copy-done.5), channel_id=1, source_target_pairs={{8,16},{24,32},{40,48},{56,64},{72,80},{88,96},{104,112},{136,144}... | collective-permute-start | bytes 1327112 | tf_op jit(solution)/shard_map/ppermute | solution.py:327
  45.4 1.1 %copy-start.3 = (bf16[8,192,384]{2,1,0:T(8,128)(2,1)}, bf16[8,192,384]{2,1,0:T(8,128)(2,1)S(1)}, u32[]{:S(2)}) copy-start(bf16[8,192,384]{2,1,0:T(8,128)(2,1)S(1)} %collective-permute-done.mate_ref) | copy-start | bytes 3538948
  46.5 1.3 %copy-start.4 = (bf16[8,192,384]{2,1,0:T(8,128)(2,1)S(1)}, bf16[8,192,384]{2,1,0:T(8,128)(2,1)}, u32[]{:S(2)}) copy-start(bf16[8,192,384]{2,1,0:T(8,128)(2,1)} %copy-done.3) | copy-start | bytes 3538948
  55.5 10.8 %collective-permute-start.3 = (bf16[3,192,384]{2,1,0:T(8,128)(2,1)S(1)}, bf16[3,192,384]{2,1,0:T(8,128)(2,1)S(1)}, u32[]{:S(2)}, u32[]{:S(2)}) collective-permute-start(bf16[3,192,384]{2,1,0:T(8,128)(2,1)S(1)} %passed_after.3.plain_ref), channel_id=1, source_target_pairs={{248,128},{376,256},{504,384},{0,120},{128,248},{256,376},{249,129... | collective-permute-start | bytes 1327112 | tf_op jit(solution)/shard_map/ppermute | solution.py:334
  66.3 18.3 %copy-start = (f32[1,128,64]{1,2,0:T(8,128)S(1)}, f32[1,128,64]{1,2,0:T(8,128)}, u32[]{:S(2)}) copy-start(f32[1,128,64]{1,2,0:T(8,128)} %param.11) | copy-start | bytes 98308
  66.3 18.3 %copy-start.1 = (f32[128,64]{0,1:T(8,128)S(1)}, f32[128,64]{0,1:T(8,128)}, u32[]{:S(2)}) copy-start(f32[128,64]{0,1:T(8,128)} %param.15) | copy-start | bytes 98308
  66.3 18.3 %copy-start.2 = (s32[257]{0:T(512)S(1)}, s32[257]{0:T(512)}, u32[]{:S(2)}) copy-start(s32[257]{0:T(512)} %timesteps_ref.1) | copy-start | bytes 3088
  72.7 11.9 %all-to-all-start.2 = ((f32[8,64,128]{2,1,0:T(8,128)}), f32[8,64,128]{2,1,0:T(8,128)S(1)}, u32[]{:S(2)}, u32[]{:S(2)}) async-start(f32[8,64,128]{2,1,0:T(8,128)} %attend_far.1), calls=%async_computation.2 | async-start | bytes 524288 | tf_op jit(solution)/shard_map/all_to_all | solution.py:336
  85.8 8.3 %collective-permute-start.4 = (f32[64,128]{1,0:T(8,128)S(1)}, f32[64,128]{1,0:T(8,128)S(1)}, u32[]{:S(2)}, u32[]{:S(2)}) collective-permute-start(f32[64,128]{1,0:T(8,128)S(1)} %get-tuple-element.16), channel_id=1, source_target_pairs={{0,504},{8,0},{16,8},{24,16},{32,24},{40,32},{48,40},{56,48},{64,5... | collective-permute-start | bytes 98312 | tf_op jit(solution)/shard_map/ppermute | solution.py:340

commit v6 on v4

--- a/solution.py
+++ b/solution.py
@@ -21,21 +21,33 @@
 SMEM = pl.BlockSpec(memory_space=pltpu.SMEM)
 
 
-def pack_kernel(position_ref, query_ref, key_ref, value_ref, weight_ref, out_ref, stage, value_buf, weight_buf, query_sem, key_sem, value_sem, weight_sem, out_sem):
+def pack_kernel(position_ref, query_ref, key_ref, value_ref, weight_ref, out_ref, stage, value_buf, weight_buf, query_sem, key_sem, value_sem, weight_sem, out_sem, mixed_sem):
     groups, rows, part = stage.shape
     tokens = rows * 2 // 5
     half = tokens // 2
-    queries, keys, values, weights = [], [], [], []
+    queries, keys, values, weights, outs, mixes = [], [], [], [], [], []
     for s in range(groups):
         span = pl.ds(s * part, part)
+        moved, mixed = pl.ds(0, 2 * tokens), pl.ds(2 * tokens, half)
         values.append(pltpu.make_async_copy(value_ref.at[:, span], value_buf.at[s], value_sem.at[s]))
         weights.append(pltpu.make_async_copy(weight_ref.at[:, span], weight_buf.at[s], weight_sem.at[s]))
         keys.append(pltpu.make_async_copy(key_ref.at[:, span], stage.at[s, pl.ds(tokens, tokens)], key_sem.at[s]))
         queries.append(pltpu.make_async_copy(query_ref.at[:, span], stage.at[s, pl.ds(0, tokens)], query_sem.at[s]))
+        outs.append(pltpu.make_async_copy(stage.at[s, moved], out_ref.at[s, moved], out_sem.at[s]))
+        mixes.append(pltpu.make_async_copy(stage.at[s, mixed], out_ref.at[s, mixed], mixed_sem.at[s]))
+    for s in range(groups):
         values[s].start()
         weights[s].start()
+    for s in range(groups):
         keys[s].start()
         queries[s].start()
+    for s in range(groups):
+        values[s].wait()
+        weights[s].wait()
+    for s in range(groups):
+        keys[s].wait()
+        queries[s].wait()
+        outs[s].start()
     zero = jnp.zeros((HALF, HS), jnp.bfloat16)
 
     def diagonal(x, y):
@@ -43,10 +55,7 @@
             [jnp.concatenate([x, zero], axis=1), jnp.concatenate([zero, y], axis=1)], axis=0
         )
 
-    outs = []
-    for s in range(groups):
-        values[s].wait()
-        weights[s].wait()
+    for s in range(groups):
         weight = [weight_buf[s, :, h * HS : (h + 1) * HS] for h in range(3)]
         pair = lax.dot_general(
             value_buf[s, :, : 2 * HS],
@@ -61,12 +70,11 @@
         stage[s, 2 * tokens :, :HS] = pair[:half]
         stage[s, 2 * tokens :, HS : 2 * HS] = pair[half:]
         stage[s, 2 * tokens :, 2 * HS :] = last
-        keys[s].wait()
-        queries[s].wait()
-        outs.append(pltpu.make_async_copy(stage.at[s], out_ref.at[s], out_sem.at[s]))
-        outs[s].start()
-    for out in outs:
-        out.wait()
+    for s in range(groups):
+        mixes[s].start()
+    for s in range(groups):
+        outs[s].wait()
+        mixes[s].wait()
 
 
 def params(mib):
@@ -86,7 +94,7 @@
             pltpu.VMEM((groups, tokens, part), jnp.bfloat16),
             pltpu.VMEM((groups, HALF, part), jnp.bfloat16),
         ]
-        + [pltpu.SemaphoreType.DMA((groups,))] * 5,
+        + [pltpu.SemaphoreType.DMA((groups,))] * 6,
         compiler_params=params(PACK_MIB),
         name="pack",
     )(position, queries, keys, values, weight_t)
@@ -242,7 +250,7 @@
         out_shape=[jax.ShapeDtypeStruct((3, count, 2 * HS), jnp.bfloat16)]
         + [jax.ShapeDtypeStruct((3, count, HS), jnp.float32)] * 3,
         compiler_params=params(16),
-        cost_estimate=cost(2, count),
+        cost_estimate=cost(0, count),
         name="attend_near",
     )(own, mate)
 
@@ -261,27 +269,44 @@
     )(position, split, direct, plain, carried, *state)
 
 
-def finish_kernel(position_ref, levels_ref, timesteps_ref, parts_ref, latent_ref, fresh_ref, velocity_ref, sent_ref):
+def summed(parts_ref):
     velocity = parts_ref[0]
     for s in range(1, parts_ref.shape[0]):
         velocity = velocity + parts_ref[s]
+    return velocity
+
+
+def velocity_kernel(parts_ref, velocity_ref):
+    velocity_ref[...] = summed(parts_ref)
+
+
+def advance_kernel(position_ref, levels_ref, timesteps_ref, parts_ref, latent_ref, fresh_ref, sent_ref):
     level = levels_ref[0]
     step = timesteps_ref[jnp.maximum(level - 2, 0)] - timesteps_ref[level]
-    velocity_ref[...] = velocity
-    advanced = latent_ref[...] + (step.astype(jnp.float32) / 64.0) * velocity
+    advanced = latent_ref[...] + (step.astype(jnp.float32) / 64.0) * summed(parts_ref)
     sent_ref[...] = jnp.where(position_ref[0] == 0, fresh_ref[...], advanced)
 
 
-def finish(position, levels, timesteps, parts, latent_t, fresh_t):
-    shape = jax.ShapeDtypeStruct(latent_t.shape, jnp.float32)
-    return pl.pallas_call(
-        finish_kernel,
+def advance(position, levels, timesteps, parts, latent_t, fresh_t):
+    return pl.pallas_call(
+        advance_kernel,
         in_specs=[SMEM] * 3 + [VMEM] * 3,
-        out_specs=[VMEM] * 2,
-        out_shape=[shape, shape],
+        out_specs=VMEM,
+        out_shape=jax.ShapeDtypeStruct(latent_t.shape, jnp.float32),
         compiler_params=params(2),
-        name="finish",
+        name="advance",
     )(position, levels, timesteps, parts, latent_t, fresh_t)
+
+
+def total_velocity(parts):
+    return pl.pallas_call(
+        velocity_kernel,
+        in_specs=[VMEM],
+        out_specs=VMEM,
+        out_shape=jax.ShapeDtypeStruct(parts.shape[1:], jnp.float32),
+        compiler_params=params(2),
+        name="velocity",
+    )(parts)
 
 
 def turned(pairs):
@@ -310,11 +335,9 @@
     carried = lax.ppermute(plain, "queue", along_y)
     parts = attend_far(position, split, direct, plain, carried, state, groups, column, length)
     parts = lax.all_to_all(parts, "seq", split_axis=0, concat_axis=0, tiled=True)
-    velocity, sent = finish(
-        position, levels, timesteps, parts, latents[0].T, fresh_noise.T
-    )
+    sent = advance(position, levels, timesteps, parts, latents[0].T, fresh_noise.T)
     shifted = lax.ppermute(sent, "queue", [(i, (i - 1) % length) for i in range(length)])
-    return (shifted.T[None], velocity.T[None])
+    return (shifted.T[None], total_velocity(parts).T[None])
 
 
 def solution(mesh):

time: 99.2 us -> 92.6 us (0.933)
  waiting for transfers between devices: 28 us -> 19.8 us
  starting transfers between devices: 19.9 us -> 21.4 us
    ppermute x1, waiting for transfers between devices: 15 us -> 7.41 us  [on_device(): direct = lax.ppermute(direct, 'queue', pairs + turned(pairs))]
    ppermute x1, starting transfers between devices: 1.92 us -> 5.22 us  [on_device(): direct = lax.ppermute(direct, 'queue', pairs + turned(pairs))]
    ppermute x1, starting transfers between devices: 6.12 us -> 4.01 us  [on_device(): plain = lax.ppermute(rest, 'queue', inner + turned(inner) + along_z)]
  transfers between devices with their start and end apart: 6 -> 6, of which waited for: 3 -> 3; matrix products, arithmetic and copies ran while one was open for 0% -> 0% of each run, Pallas kernels for 8% -> 9%
where the time goes in v6:
time: 92.6 us; the launch traced here: 91.8 us
  blocking collectives  30.7 us (33%)
  starting transfers between devices  21.4 us (23%)
  waiting for transfers between devices  19.8 us (21%)
  Pallas kernels  17.8 us (19%)
  between operations  1.39 us (2%)
    all_to_all x1, blocking collectives, on_device(): own = lax.all_to_all(sent, 'seq', split_axis=0, concat_axis=0, tiled=True)  30.7 us
    pallas_call x1, Pallas kernels, attend_near(): pl.pallas_call(near_kernel, in_specs=[VMEM] * 2, out_specs=[VMEM] * 4, ou...  7.72 us
    ppermute x1, waiting for transfers between devices, on_device(): direct = lax.ppermute(direct, 'queue', pairs + turned(pairs))  7.41 us
    ppermute x1, waiting for transfers between devices, on_device(): lax.ppermute(sent, 'queue', [(i, (i - 1) % length) for i in range(length)])  6.96 us
    all_to_all x1, waiting for transfers between devices, on_device(): lax.all_to_all(parts, 'seq', split_axis=0, concat_axis=0, tiled=True)  5.42 us
    pallas_call x1, Pallas kernels, attend_far(): pl.pallas_call(functools.partial(far_kernel, column, length), in_specs=[S...  5.25 us
    ppermute x1, starting transfers between devices, on_device(): direct = lax.ppermute(direct, 'queue', pairs + turned(pairs))  5.22 us
    ppermute x1, starting transfers between devices, on_device(): plain = lax.ppermute(rest, 'queue', inner + turned(inner) + along_z)  4.01 us
  transfers between devices with their start and end apart: 6, of which 3 were waited for; matrix products, arithmetic and copies ran while one was open for 0% of the time, Pallas kernels for 9%

profile of v6, /device:TPU:185, one launch (start us, length us, event | category | flops | bytes accessed | tf_op | source)
XLA Modules:
  0.0 91.8 jit_solution(18087886215680173723)
XLA Ops:
  0.6 3.5 %pack.1 = bf16[8,320,384]{2,1,0:T(8,128)(2,1)} custom-call(s32[1]{0:T(128)} %bitcast.position_ref, bf16[128,3072]{1,0:T(8,128)(2,1)} %bitcast.17, bf16[128,3072]{1,0:T(8,128)(2,1)} %bitcast.18, bf16[128,3072]{1,0:T(8,128)(2,1)} %bitcast.19, bf16[64,3072]{1,0:T(8,128)(2,1)} %bitcast.20), custom_call_target="tpu_custom_call" | custom-call | tf_op jit(solution)/shard_map/pack/pallas_call | solution.py:87
  4.2 30.7 %all_to_all.10.own_ref = bf16[8,320,384]{2,1,0:T(8,128)(2,1)S(1)} all-to-all(bf16[8,320,384]{2,1,0:T(8,128)(2,1)} %pack.1), channel_id=1, replica_groups=mesh['queue'=64,'seq'=8] {'seq'}, dimensions={0} | all-to-all | bytes 3932160 | tf_op jit(solution)/shard_map/all_to_all | solution.py:321
  34.9 3.8 %collective-permute-start = (bf16[8,320,384]{2,1,0:T(8,128)(2,1)S(1)}, bf16[8,320,384]{2,1,0:T(8,128)(2,1)S(1)}, u32[]{:S(2)}, u32[]{:S(2)}) collective-permute-start(bf16[8,320,384]{2,1,0:T(8,128)(2,1)S(1)} %all_to_all.10.own_ref), channel_id=1, source_target_pairs={{0,8},{16,24},{32,40},{48,56},{64,72},{80,88},{96,104},{112,120},{... | collective-permute-start | bytes 5898248 | tf_op jit(solution)/shard_map/ppermute | solution.py:332
  38.6 0.1 cut_rows.1
  38.8 5.2 %collective-permute-start.1 = (bf16[6,192,384]{2,1,0:T(8,128)(2,1)S(1)}, bf16[6,192,384]{2,1,0:T(8,128)(2,1)S(1)}, u32[]{:S(2)}, u32[]{:S(2)}) collective-permute-start(bf16[6,192,384]{2,1,0:T(8,128)(2,1)S(1)} %get-tuple-element.9), channel_id=1, source_target_pairs={{8,16},{24,32},{40,48},{56,64},{72,80},{88,96},{104,112},{136,144}... | collective-permute-start | bytes 2654216 | tf_op jit(solution)/shard_map/ppermute | solution.py:329
  44.0 4.0 %collective-permute-start.2 = (bf16[2,192,384]{2,1,0:T(8,128)(2,1)S(1)}, bf16[2,192,384]{2,1,0:T(8,128)(2,1)S(1)}, u32[]{:S(2)}, u32[]{:S(2)}) collective-permute-start(bf16[2,192,384]{2,1,0:T(8,128)(2,1)S(1)} %get-tuple-element.10), channel_id=1, source_target_pairs={{8,16},{24,32},{40,48},{56,64},{72,80},{88,96},{104,112},{136,144}... | collective-permute-start | bytes 884744 | tf_op jit(solution)/shard_map/ppermute | solution.py:330
  48.0 0.0 collective-permute-done.mate_ref
  48.0 7.7 %attend_near.1 = (bf16[3,1024,256]{2,1,0:T(8,128)(2,1)S(1)}, f32[3,1024,128]{2,1,0:T(8,128)S(1)}, f32[3,1024,128]{2,1,0:T(8,128)S(1)}, f32[3,1024,128]{2,1,0:T(8,128)S(1)}) custom-call(bf16[8,320,384]{2,1,0:T(8,128)(2,1)S(1)} %all_to_all.10.own_ref, bf16[8,320,384]{2,1,0:T(8,128)(2,1)S(1)} %collective-permute-done.mate_ref), custom_call_target="tpu_custom_call" | custom-call | bytes 4194304 | tf_op jit(solution)/shard_map/attend_near/pallas_call | solution.py:246
  55.7 0.0 collective-permute-done.2.rest_ref
  55.8 3.1 %collective-permute-start.3 = (bf16[2,192,384]{2,1,0:T(8,128)(2,1)S(1)}, bf16[2,192,384]{2,1,0:T(8,128)(2,1)S(1)}, u32[]{:S(2)}, u32[]{:S(2)}) collective-permute-start(bf16[2,192,384]{2,1,0:T(8,128)(2,1)S(1)} %passed_after.1.plain_ref), channel_id=1, source_target_pairs={{248,128},{376,256},{504,384},{0,120},{128,248},{256,376},{249,129... | collective-permute-start | bytes 884744 | tf_op jit(solution)/shard_map/ppermute | solution.py:335
  58.9 7.4 %collective-permute-done.1.direct_ref = bf16[6,192,384]{2,1,0:T(8,128)(2,1)S(1)} collective-permute-done((bf16[6,192,384]{2,1,0:T(8,128)(2,1)S(1)}, bf16[6,192,384]{2,1,0:T(8,128)(2,1)S(1)}, u32[]{:S(2)}, u32[]{:S(2)}) %collective-permute-start.1) | collective-permute-done | bytes 884768 | tf_op jit(solution)/shard_map/ppermute | solution.py:329
  66.3 0.0 collective-permute-done.3.carried_ref
  66.3 0.0 copy-start
  66.3 0.0 copy-start.1
  66.3 0.0 copy-start.2
  66.3 5.2 %attend_far.1 = f32[8,64,128]{2,1,0:T(8,128)} custom-call(s32[1]{0:T(128)} %bitcast.position_ref, bf16[3,1024,256]{2,1,0:T(8,128)(2,1)S(1)} %get-tuple-element.8.after_ref.split_ref, bf16[6,192,384]{2,1,0:T(8,128)(2,1)S(1)} %collective-permute-done.1.direct_ref, bf16[2,192,384]{2,1,0:T(8,128)(2,1)S(1)} %passed_after.1.plain_ref, ...), custom_call_target="tpu_custom_call" | custom-call | flops 3221225472 | bytes 4194304 | tf_op jit(solution)/shard_map/attend_far/pallas_call | solution.py:260
  71.5 3.4 %all-to-all-start.1 = ((f32[8,64,128]{2,1,0:T(8,128)}), f32[8,64,128]{2,1,0:T(8,128)S(1)}, u32[]{:S(2)}, u32[]{:S(2)}) async-start(f32[8,64,128]{2,1,0:T(8,128)} %attend_far.1), calls=%async_computation.1 | async-start | bytes 524288 | tf_op jit(solution)/shard_map/all_to_all | solution.py:337
  75.6 5.4 %all-to-all-done.1.parts_ref = f32[8,64,128]{2,1,0:T(8,128)S(1)} async-done(((f32[8,64,128]{2,1,0:T(8,128)}), f32[8,64,128]{2,1,0:T(8,128)S(1)}, u32[]{:S(2)}, u32[]{:S(2)}) %all-to-all-start.1) | async-done | bytes 262176 | tf_op jit(solution)/shard_map/all_to_all | solution.py:337
  81.0 0.0 copy-done
  81.0 0.0 copy-done.1
  81.0 0.0 copy-done.2
  81.0 0.6 advance.1
  81.6 1.9 %collective-permute-start.4 = (f32[64,128]{1,0:T(8,128)S(1)}, f32[64,128]{1,0:T(8,128)S(1)}, u32[]{:S(2)}, u32[]{:S(2)}) collective-permute-start(f32[64,128]{1,0:T(8,128)S(1)} %advance.1), channel_id=1, source_target_pairs={{0,504},{8,0},{16,8},{24,16},{32,24},{40,32},{48,40},{56,48},{64,5... | collective-permute-start | bytes 98312 | tf_op jit(solution)/shard_map/ppermute | solution.py:339
  83.6 0.6 velocity.1
  84.2 7.0 %collective-permute-done.4 = f32[64,128]{1,0:T(8,128)S(1)} collective-permute-done((f32[64,128]{1,0:T(8,128)S(1)}, f32[64,128]{1,0:T(8,128)S(1)}, u32[]{:S(2)}, u32[]{:S(2)}) %collective-permute-start.4) | collective-permute-done | bytes 32800 | tf_op jit(solution)/shard_map/ppermute | solution.py:339
  91.1 0.6 copy.14
  (1 shorter events, 0.0 us)
Async XLA Ops:
  34.9 13.1 %collective-permute-start = (bf16[8,320,384]{2,1,0:T(8,128)(2,1)S(1)}, bf16[8,320,384]{2,1,0:T(8,128)(2,1)S(1)}, u32[]{:S(2)}, u32[]{:S(2)}) collective-permute-start(bf16[8,320,384]{2,1,0:T(8,128)(2,1)S(1)} %all_to_all.10.own_ref), channel_id=1, source_target_pairs={{0,8},{16,24},{32,40},{48,56},{64,72},{80,88},{96,104},{112,120},{... | collective-permute-start | bytes 5898248 | tf_op jit(solution)/shard_map/ppermute | solution.py:332
  38.8 27.5 %collective-permute-start.1 = (bf16[6,192,384]{2,1,0:T(8,128)(2,1)S(1)}, bf16[6,192,384]{2,1,0:T(8,128)(2,1)S(1)}, u32[]{:S(2)}, u32[]{:S(2)}) collective-permute-start(bf16[6,192,384]{2,1,0:T(8,128)(2,1)S(1)} %get-tuple-element.9), channel_id=1, source_target_pairs={{8,16},{24,32},{40,48},{56,64},{72,80},{88,96},{104,112},{136,144}... | collective-permute-start | bytes 2654216 | tf_op jit(solution)/shard_map/ppermute | solution.py:329
  44.0 11.8 %collective-permute-start.2 = (bf16[2,192,384]{2,1,0:T(8,128)(2,1)S(1)}, bf16[2,192,384]{2,1,0:T(8,128)(2,1)S(1)}, u32[]{:S(2)}, u32[]{:S(2)}) collective-permute-start(bf16[2,192,384]{2,1,0:T(8,128)(2,1)S(1)} %get-tuple-element.10), channel_id=1, source_target_pairs={{8,16},{24,32},{40,48},{56,64},{72,80},{88,96},{104,112},{136,144}... | collective-permute-start | bytes 884744 | tf_op jit(solution)/shard_map/ppermute | solution.py:330
  55.8 10.5 %collective-permute-start.3 = (bf16[2,192,384]{2,1,0:T(8,128)(2,1)S(1)}, bf16[2,192,384]{2,1,0:T(8,128)(2,1)S(1)}, u32[]{:S(2)}, u32[]{:S(2)}) collective-permute-start(bf16[2,192,384]{2,1,0:T(8,128)(2,1)S(1)} %passed_after.1.plain_ref), channel_id=1, source_target_pairs={{248,128},{376,256},{504,384},{0,120},{128,248},{256,376},{249,129... | collective-permute-start | bytes 884744 | tf_op jit(solution)/shard_map/ppermute | solution.py:335
  66.3 14.7 %copy-start = (f32[1,128,64]{1,2,0:T(8,128)S(1)}, f32[1,128,64]{1,2,0:T(8,128)}, u32[]{:S(2)}) copy-start(f32[1,128,64]{1,2,0:T(8,128)} %param.11) | copy-start | bytes 98308
  66.3 14.8 %copy-start.1 = (f32[128,64]{0,1:T(8,128)S(1)}, f32[128,64]{0,1:T(8,128)}, u32[]{:S(2)}) copy-start(f32[128,64]{0,1:T(8,128)} %param.15) | copy-start | bytes 98308
  66.3 14.8 %copy-start.2 = (s32[257]{0:T(512)S(1)}, s32[257]{0:T(512)}, u32[]{:S(2)}) copy-start(s32[257]{0:T(512)} %timesteps_ref.1) | copy-start | bytes 3088
  71.5 9.5 %all-to-all-start.1 = ((f32[8,64,128]{2,1,0:T(8,128)}), f32[8,64,128]{2,1,0:T(8,128)S(1)}, u32[]{:S(2)}, u32[]{:S(2)}) async-start(f32[8,64,128]{2,1,0:T(8,128)} %attend_far.1), calls=%async_computation.1 | async-start | bytes 524288 | tf_op jit(solution)/shard_map/all_to_all | solution.py:337
  81.6 9.5 %collective-permute-start.4 = (f32[64,128]{1,0:T(8,128)S(1)}, f32[64,128]{1,0:T(8,128)S(1)}, u32[]{:S(2)}, u32[]{:S(2)}) collective-permute-start(f32[64,128]{1,0:T(8,128)S(1)} %advance.1), channel_id=1, source_target_pairs={{0,504},{8,0},{16,8},{24,16},{32,24},{40,32},{48,40},{56,48},{64,5... | collective-permute-start | bytes 98312 | tf_op jit(solution)/shard_map/ppermute | solution.py:339

commit v7 on v6

--- a/solution.py
+++ b/solution.py
@@ -14,6 +14,7 @@
 ROWS = 256
 PACK_MIB = 56
 CUT = 6
+MATES = 2
 NT = (((1,), (1,)), ((), ()))
 VMEM = pl.BlockSpec(memory_space=pltpu.VMEM)
 ANY = pl.BlockSpec(memory_space=pl.ANY)
@@ -143,13 +144,16 @@
             emit(h, span, peak, jnp.dot(probs, mix, preferred_element_type=jnp.float32))
 
 
-def cut_kernel(own_ref, direct_ref, rest_ref):
+def cut_kernel(own_ref, direct_ref, rest_ref, *mate_refs):
     cut, rows, _ = direct_ref.shape
     direct_ref[...] = own_ref[:cut, -rows:, :]
     rest_ref[...] = own_ref[cut:, -rows:, :]
-
-
-def near_kernel(own_ref, mate_ref, split_ref, sums_ref, totals_ref, peaks_ref):
+    size = mate_refs[0].shape[0]
+    for i, ref in enumerate(mate_refs):
+        ref[...] = own_ref[i * size : (i + 1) * size, -rows:, :]
+
+
+def own_kernel(own_ref, split_ref, sums_ref, totals_ref, peaks_ref):
     scaled_queries(own_ref, split_ref)
     tokens = own_ref.shape[1] * 2 // 5
 
@@ -158,7 +162,22 @@
         totals_ref[h, span, :] = mixed[:, HS:]
         peaks_ref[h, span, :] = jnp.broadcast_to(peak, (ROWS, HS))
 
-    attend(split_ref, [(own_ref, tokens, tokens), (mate_ref, tokens, tokens)], emit)
+    attend(split_ref, [(own_ref, tokens, tokens)], emit)
+
+
+def mate_kernel(split_ref, *refs):
+    *mate_refs, old_sums_ref, old_totals_ref, old_peaks_ref, sums_ref, totals_ref, peaks_ref = refs
+    tokens = mate_refs[0].shape[1] * 2 // 3
+
+    def emit(h, span, peak, mixed):
+        old_peak = old_peaks_ref[h, span, :]
+        new_peak = jnp.maximum(old_peak, peak)
+        kept, added = jnp.exp2(old_peak - new_peak), jnp.exp2(peak - new_peak)
+        sums_ref[h, span, :] = old_sums_ref[h, span, :] * kept + mixed[:, :HS] * added
+        totals_ref[h, span, :] = old_totals_ref[h, span, :] * kept + mixed[:, HS:] * added
+        peaks_ref[h, span, :] = new_peak
+
+    attend(split_ref, [(ref, tokens, 0) for ref in mate_refs], emit)
 
 
 def pass_kernel(rest_ref, after_ref, out_ref):
@@ -222,8 +241,11 @@
     return pl.pallas_call(
         cut_kernel,
         in_specs=[VMEM],
-        out_specs=[VMEM] * 2,
-        out_shape=[jax.ShapeDtypeStruct((count, rows, part), own.dtype) for count in (cut, groups - cut)],
+        out_specs=[VMEM] * (2 + MATES),
+        out_shape=[
+            jax.ShapeDtypeStruct((count, rows, part), own.dtype)
+            for count in [cut, groups - cut] + [groups // MATES] * MATES
+        ],
         compiler_params=params(2),
         name="cut_rows",
     )(own)
@@ -241,18 +263,33 @@
     )(rest, after)
 
 
-def attend_near(own, mate):
+def attend_own(own):
     count = own.shape[0] * own.shape[1] * 2 // 5
     return pl.pallas_call(
-        near_kernel,
-        in_specs=[VMEM] * 2,
+        own_kernel,
+        in_specs=[VMEM],
         out_specs=[VMEM] * 4,
         out_shape=[jax.ShapeDtypeStruct((3, count, 2 * HS), jnp.bfloat16)]
         + [jax.ShapeDtypeStruct((3, count, HS), jnp.float32)] * 3,
         compiler_params=params(16),
         cost_estimate=cost(0, count),
-        name="attend_near",
-    )(own, mate)
+        name="attend_own",
+    )(own)
+
+
+def attend_mate(split, mate, state):
+    count = split.shape[1]
+    first = 1 + len(mate)
+    return pl.pallas_call(
+        mate_kernel,
+        in_specs=[VMEM] * (first + 3),
+        out_specs=[VMEM] * 3,
+        out_shape=[jax.ShapeDtypeStruct(x.shape, x.dtype) for x in state],
+        input_output_aliases={first: 0, first + 1: 1, first + 2: 2},
+        compiler_params=params(16),
+        cost_estimate=cost(0, count),
+        name="attend_mate",
+    )(split, *mate, *state)
 
 
 def attend_far(position, split, direct, plain, carried, state, groups, column, length):
@@ -319,7 +356,7 @@
     groups = lax.axis_size("seq")
     sent = pack(position, queries[0], key_proj[0], values[0], head_weight.T, groups)
     own = lax.all_to_all(sent, "seq", split_axis=0, concat_axis=0, tiled=True)
-    direct, rest = cut_rows(own, groups * CUT // 8)
+    direct, rest, *mate = cut_rows(own, groups * CUT // 8)
     column = length // 4
     inner = [(i, i + 1) for i in range(1, length - 1, 2) if (i + 1) % column]
     cross = [(i, i + 1) for i in range(column - 1, length - 1, column)]
@@ -329,8 +366,9 @@
     direct = lax.ppermute(direct, "queue", pairs + turned(pairs))
     plain = lax.ppermute(rest, "queue", inner + turned(inner) + along_z)
     mates = [(i, i + 1) for i in range(0, length, 2)]
-    mate = lax.ppermute(own, "queue", mates + turned(mates))
-    split, *state = attend_near(own, mate)
+    mate = [lax.ppermute(x, "queue", mates + turned(mates)) for x in mate]
+    split, *state = attend_own(own)
+    state = attend_mate(split, mate, state)
     plain = passed_after(plain, split)
     carried = lax.ppermute(plain, "queue", along_y)
     parts = attend_far(position, split, direct, plain, carried, state, groups, column, length)

time: 92.6 us -> 92.3 us (level)
  waiting for transfers between devices: 19.8 us -> 12.8 us
  starting transfers between devices: 21.4 us -> 27.3 us
  Pallas kernels: 17.8 us -> 18.9 us
    ppermute x1, waiting for transfers between devices: 7.41 us -> 0.01 us  [on_device(): direct = lax.ppermute(direct, 'queue', pairs + turned(pairs))]
    ppermute x1, starting transfers between devices: 3.1 us -> 4.95 us  [on_device(): carried = lax.ppermute(plain, 'queue', along_y)]
    ppermute x1, starting transfers between devices: 5.22 us -> 7.07 us  [on_device(): direct = lax.ppermute(direct, 'queue', pairs + turned(pairs))]
    all_to_all x1, starting transfers between devices: 3.41 us -> 5 us  [on_device(): lax.all_to_all(parts, 'seq', split_axis=0, concat_axis=0, tiled=True)]
    pallas_call x2 -> x3, Pallas kernels: 7.83 us -> 8.89 us  [the longest x1 4.64 us: attend_mate(): pl.pallas_call(mate_kernel, in_specs=[VMEM] * (first + 3), out_specs=[VME...]
    ppermute x1 -> x2, starting transfers between devices: 3.76 us -> 4.33 us  [on_device(): mate = [lax.ppermute(x, 'queue', mates + turned(mates)) for x in mate]]
  transfers between devices with their start and end apart: 6 -> 7, of which waited for: 3 -> 3; matrix products, arithmetic and copies ran while one was open for 0% -> 0% of each run, Pallas kernels for 9% -> 10%
where the time goes in v7:
time: 92.3 us; the launch traced here: 91.8 us
  blocking collectives  30.7 us (33%)
  starting transfers between devices  27.3 us (30%)
  Pallas kernels  18.9 us (20%)
  waiting for transfers between devices  12.8 us (14%)
  between operations  1.43 us (2%)
    all_to_all x1, blocking collectives, on_device(): own = lax.all_to_all(sent, 'seq', split_axis=0, concat_axis=0, tiled=True)  30.7 us
    ppermute x1, starting transfers between devices, on_device(): direct = lax.ppermute(direct, 'queue', pairs + turned(pairs))  7.07 us
    ppermute x1, waiting for transfers between devices, on_device(): lax.ppermute(sent, 'queue', [(i, (i - 1) % length) for i in range(length)])  6.95 us
    all_to_all x1, waiting for transfers between devices, on_device(): lax.all_to_all(parts, 'seq', split_axis=0, concat_axis=0, tiled=True)  5.48 us
    pallas_call x1, Pallas kernels, attend_far(): pl.pallas_call(functools.partial(far_kernel, column, length), in_specs=[S...  5.24 us
    all_to_all x1, starting transfers between devices, on_device(): lax.all_to_all(parts, 'seq', split_axis=0, concat_axis=0, tiled=True)  5 us
    ppermute x1, starting transfers between devices, on_device(): carried = lax.ppermute(plain, 'queue', along_y)  4.95 us
    pallas_call x1, Pallas kernels, attend_mate(): pl.pallas_call(mate_kernel, in_specs=[VMEM] * (first + 3), out_specs=[VME...  4.64 us
  transfers between devices with their start and end apart: 7, of which 3 were waited for; matrix products, arithmetic and copies ran while one was open for 0% of the time, Pallas kernels for 10%

profile of v7, /device:TPU:185, one launch (start us, length us, event | category | flops | bytes accessed | tf_op | source)
XLA Modules:
  0.0 91.8 jit_solution(15817569768532459179)
XLA Ops:
  0.6 3.5 %pack.1 = bf16[8,320,384]{2,1,0:T(8,128)(2,1)} custom-call(s32[1]{0:T(128)} %bitcast.position_ref, bf16[128,3072]{1,0:T(8,128)(2,1)} %bitcast.17, bf16[128,3072]{1,0:T(8,128)(2,1)} %bitcast.18, bf16[128,3072]{1,0:T(8,128)(2,1)} %bitcast.19, bf16[64,3072]{1,0:T(8,128)(2,1)} %bitcast.20), custom_call_target="tpu_custom_call" | custom-call | tf_op jit(solution)/shard_map/pack/pallas_call | solution.py:88
  4.2 30.7 %all_to_all.10.own_ref = bf16[8,320,384]{2,1,0:T(8,128)(2,1)S(1)} all-to-all(bf16[8,320,384]{2,1,0:T(8,128)(2,1)} %pack.1), channel_id=1, replica_groups=mesh['queue'=64,'seq'=8] {'seq'}, dimensions={0} | all-to-all | bytes 3932160 | tf_op jit(solution)/shard_map/all_to_all | solution.py:358
  34.9 0.2 cut_rows.1
  35.1 7.1 %collective-permute-start = (bf16[6,192,384]{2,1,0:T(8,128)(2,1)S(1)}, bf16[6,192,384]{2,1,0:T(8,128)(2,1)S(1)}, u32[]{:S(2)}, u32[]{:S(2)}) collective-permute-start(bf16[6,192,384]{2,1,0:T(8,128)(2,1)S(1)} %get-tuple-element.14), channel_id=1, source_target_pairs={{8,16},{24,32},{40,48},{56,64},{72,80},{88,96},{104,112},{136,144}... | collective-permute-start | bytes 2654216 | tf_op jit(solution)/shard_map/ppermute | solution.py:366
  42.2 1.9 %collective-permute-start.3 = (bf16[4,192,384]{2,1,0:T(8,128)(2,1)S(1)}, bf16[4,192,384]{2,1,0:T(8,128)(2,1)S(1)}, u32[]{:S(2)}, u32[]{:S(2)}) collective-permute-start(bf16[4,192,384]{2,1,0:T(8,128)(2,1)S(1)} %get-tuple-element.16), channel_id=1, source_target_pairs={{0,8},{16,24},{32,40},{48,56},{64,72},{80,88},{96,104},{112,120},{... | collective-permute-start | bytes 1769480 | tf_op jit(solution)/shard_map/ppermute | solution.py:369
  44.1 2.4 %collective-permute-start.4 = (bf16[4,192,384]{2,1,0:T(8,128)(2,1)S(1)}, bf16[4,192,384]{2,1,0:T(8,128)(2,1)S(1)}, u32[]{:S(2)}, u32[]{:S(2)}) collective-permute-start(bf16[4,192,384]{2,1,0:T(8,128)(2,1)S(1)} %get-tuple-element.17), channel_id=1, source_target_pairs={{0,8},{16,24},{32,40},{48,56},{64,72},{80,88},{96,104},{112,120},{... | collective-permute-start | bytes 1769480 | tf_op jit(solution)/shard_map/ppermute | solution.py:369
  46.5 4.0 %collective-permute-start.1 = (bf16[2,192,384]{2,1,0:T(8,128)(2,1)S(1)}, bf16[2,192,384]{2,1,0:T(8,128)(2,1)S(1)}, u32[]{:S(2)}, u32[]{:S(2)}) collective-permute-start(bf16[2,192,384]{2,1,0:T(8,128)(2,1)S(1)} %get-tuple-element.15), channel_id=1, source_target_pairs={{8,16},{24,32},{40,48},{56,64},{72,80},{88,96},{104,112},{136,144}... | collective-permute-start | bytes 884744 | tf_op jit(solution)/shard_map/ppermute | solution.py:367
  50.6 4.0 %attend_own.1 = (bf16[3,1024,256]{2,1,0:T(8,128)(2,1)S(1)}, f32[3,1024,128]{2,1,0:T(8,128)S(1)}, f32[3,1024,128]{2,1,0:T(8,128)S(1)}, f32[3,1024,128]{2,1,0:T(8,128)S(1)}) custom-call(bf16[8,320,384]{2,1,0:T(8,128)(2,1)S(1)} %all_to_all.10.own_ref), custom_call_target="tpu_custom_call" | custom-call | bytes 4194304 | tf_op jit(solution)/shard_map/attend_own/pallas_call | solution.py:268
  54.6 0.4 collective-permute-done.1.rest_ref
  55.0 5.0 %collective-permute-start.2 = (bf16[2,192,384]{2,1,0:T(8,128)(2,1)S(1)}, bf16[2,192,384]{2,1,0:T(8,128)(2,1)S(1)}, u32[]{:S(2)}, u32[]{:S(2)}) collective-permute-start(bf16[2,192,384]{2,1,0:T(8,128)(2,1)S(1)} %passed_after.1.plain_ref), channel_id=1, source_target_pairs={{248,128},{376,256},{504,384},{0,120},{128,248},{256,376},{249,129... | collective-permute-start | bytes 884744 | tf_op jit(solution)/shard_map/ppermute | solution.py:373
  60.0 0.0 collective-permute-done.3.refs_0_
  60.0 0.0 collective-permute-done.4.refs_1_
  60.0 4.6 %attend_mate.1 = (f32[3,1024,128]{2,1,0:T(8,128)S(1)}, f32[3,1024,128]{2,1,0:T(8,128)S(1)}, f32[3,1024,128]{2,1,0:T(8,128)S(1)}) custom-call(bf16[3,1024,256]{2,1,0:T(8,128)(2,1)S(1)} %get-tuple-element.13.after_ref.split_ref, bf16[4,192,384]{2,1,0:T(8,128)(2,1)S(1)} %collective-permute-done.3.refs_0_, ...), custom_call_target="tpu_custom_call", output_to_operand_aliasing={{0}: (3, {}), {1}: (4, {}), {2}: (5, {})} | custom-call | bytes 4194304 | tf_op jit(solution)/shard_map/attend_mate/pallas_call | solution.py:283
  64.6 0.0 collective-permute-done.2.carried_ref
  64.6 0.0 collective-permute-done.direct_ref
  64.7 0.0 copy-start
  64.7 0.0 copy-start.1
  64.7 0.0 copy-start.2
  64.7 5.2 %attend_far.1 = f32[8,64,128]{2,1,0:T(8,128)} custom-call(s32[1]{0:T(128)} %bitcast.position_ref, bf16[3,1024,256]{2,1,0:T(8,128)(2,1)S(1)} %get-tuple-element.13.after_ref.split_ref, bf16[6,192,384]{2,1,0:T(8,128)(2,1)S(1)} %collective-permute-done.direct_ref, bf16[2,192,384]{2,1,0:T(8,128)(2,1)S(1)} %passed_after.1.plain_ref, ...), custom_call_target="tpu_custom_call" | custom-call | flops 3221225472 | bytes 4194304 | tf_op jit(solution)/shard_map/attend_far/pallas_call | solution.py:297
  69.9 5.0 %all-to-all-start.1 = ((f32[8,64,128]{2,1,0:T(8,128)}), f32[8,64,128]{2,1,0:T(8,128)S(1)}, u32[]{:S(2)}, u32[]{:S(2)}) async-start(f32[8,64,128]{2,1,0:T(8,128)} %attend_far.1), calls=%async_computation.1 | async-start | bytes 524288 | tf_op jit(solution)/shard_map/all_to_all | solution.py:375
  75.6 5.5 %all-to-all-done.1.parts_ref = f32[8,64,128]{2,1,0:T(8,128)S(1)} async-done(((f32[8,64,128]{2,1,0:T(8,128)}), f32[8,64,128]{2,1,0:T(8,128)S(1)}, u32[]{:S(2)}, u32[]{:S(2)}) %all-to-all-start.1) | async-done | bytes 262176 | tf_op jit(solution)/shard_map/all_to_all | solution.py:375
  81.1 0.0 copy-done
  81.1 0.0 copy-done.1
  81.1 0.0 copy-done.2
  81.1 0.6 advance.1
  81.7 1.9 %collective-permute-start.5 = (f32[64,128]{1,0:T(8,128)S(1)}, f32[64,128]{1,0:T(8,128)S(1)}, u32[]{:S(2)}, u32[]{:S(2)}) collective-permute-start(f32[64,128]{1,0:T(8,128)S(1)} %advance.1), channel_id=1, source_target_pairs={{0,504},{8,0},{16,8},{24,16},{32,24},{40,32},{48,40},{56,48},{64,5... | collective-permute-start | bytes 98312 | tf_op jit(solution)/shard_map/ppermute | solution.py:377
  83.6 0.6 velocity.1
  84.2 6.9 %collective-permute-done.5 = f32[64,128]{1,0:T(8,128)S(1)} collective-permute-done((f32[64,128]{1,0:T(8,128)S(1)}, f32[64,128]{1,0:T(8,128)S(1)}, u32[]{:S(2)}, u32[]{:S(2)}) %collective-permute-start.5) | collective-permute-done | bytes 32800 | tf_op jit(solution)/shard_map/ppermute | solution.py:377
  91.2 0.6 copy.20
  (1 shorter events, 0.0 us)
Async XLA Ops:
  35.1 29.5 %collective-permute-start = (bf16[6,192,384]{2,1,0:T(8,128)(2,1)S(1)}, bf16[6,192,384]{2,1,0:T(8,128)(2,1)S(1)}, u32[]{:S(2)}, u32[]{:S(2)}) collective-permute-start(bf16[6,192,384]{2,1,0:T(8,128)(2,1)S(1)} %get-tuple-element.14), channel_id=1, source_target_pairs={{8,16},{24,32},{40,48},{56,64},{72,80},{88,96},{104,112},{136,144}... | collective-permute-start | bytes 2654216 | tf_op jit(solution)/shard_map/ppermute | solution.py:366
  42.2 17.8 %collective-permute-start.3 = (bf16[4,192,384]{2,1,0:T(8,128)(2,1)S(1)}, bf16[4,192,384]{2,1,0:T(8,128)(2,1)S(1)}, u32[]{:S(2)}, u32[]{:S(2)}) collective-permute-start(bf16[4,192,384]{2,1,0:T(8,128)(2,1)S(1)} %get-tuple-element.16), channel_id=1, source_target_pairs={{0,8},{16,24},{32,40},{48,56},{64,72},{80,88},{96,104},{112,120},{... | collective-permute-start | bytes 1769480 | tf_op jit(solution)/shard_map/ppermute | solution.py:369
  44.1 15.9 %collective-permute-start.4 = (bf16[4,192,384]{2,1,0:T(8,128)(2,1)S(1)}, bf16[4,192,384]{2,1,0:T(8,128)(2,1)S(1)}, u32[]{:S(2)}, u32[]{:S(2)}) collective-permute-start(bf16[4,192,384]{2,1,0:T(8,128)(2,1)S(1)} %get-tuple-element.17), channel_id=1, source_target_pairs={{0,8},{16,24},{32,40},{48,56},{64,72},{80,88},{96,104},{112,120},{... | collective-permute-start | bytes 1769480 | tf_op jit(solution)/shard_map/ppermute | solution.py:369
  46.5 8.5 %collective-permute-start.1 = (bf16[2,192,384]{2,1,0:T(8,128)(2,1)S(1)}, bf16[2,192,384]{2,1,0:T(8,128)(2,1)S(1)}, u32[]{:S(2)}, u32[]{:S(2)}) collective-permute-start(bf16[2,192,384]{2,1,0:T(8,128)(2,1)S(1)} %get-tuple-element.15), channel_id=1, source_target_pairs={{8,16},{24,32},{40,48},{56,64},{72,80},{88,96},{104,112},{136,144}... | collective-permute-start | bytes 884744 | tf_op jit(solution)/shard_map/ppermute | solution.py:367
  55.0 9.6 %collective-permute-start.2 = (bf16[2,192,384]{2,1,0:T(8,128)(2,1)S(1)}, bf16[2,192,384]{2,1,0:T(8,128)(2,1)S(1)}, u32[]{:S(2)}, u32[]{:S(2)}) collective-permute-start(bf16[2,192,384]{2,1,0:T(8,128)(2,1)S(1)} %passed_after.1.plain_ref), channel_id=1, source_target_pairs={{248,128},{376,256},{504,384},{0,120},{128,248},{256,376},{249,129... | collective-permute-start | bytes 884744 | tf_op jit(solution)/shard_map/ppermute | solution.py:373
  64.7 16.4 %copy-start = (f32[1,128,64]{1,2,0:T(8,128)S(1)}, f32[1,128,64]{1,2,0:T(8,128)}, u32[]{:S(2)}) copy-start(f32[1,128,64]{1,2,0:T(8,128)} %param.11) | copy-start | bytes 98308
  64.7 16.4 %copy-start.1 = (f32[128,64]{0,1:T(8,128)S(1)}, f32[128,64]{0,1:T(8,128)}, u32[]{:S(2)}) copy-start(f32[128,64]{0,1:T(8,128)} %param.15) | copy-start | bytes 98308
  64.7 16.4 %copy-start.2 = (s32[257]{0:T(512)S(1)}, s32[257]{0:T(512)}, u32[]{:S(2)}) copy-start(s32[257]{0:T(512)} %timesteps_ref.1) | copy-start | bytes 3088
  69.9 11.1 %all-to-all-start.1 = ((f32[8,64,128]{2,1,0:T(8,128)}), f32[8,64,128]{2,1,0:T(8,128)S(1)}, u32[]{:S(2)}, u32[]{:S(2)}) async-start(f32[8,64,128]{2,1,0:T(8,128)} %attend_far.1), calls=%async_computation.1 | async-start | bytes 524288 | tf_op jit(solution)/shard_map/all_to_all | solution.py:375
  81.7 9.5 %collective-permute-start.5 = (f32[64,128]{1,0:T(8,128)S(1)}, f32[64,128]{1,0:T(8,128)S(1)}, u32[]{:S(2)}, u32[]{:S(2)}) collective-permute-start(f32[64,128]{1,0:T(8,128)S(1)} %advance.1), channel_id=1, source_target_pairs={{0,504},{8,0},{16,8},{24,16},{32,24},{40,32},{48,40},{56,48},{64,5... | collective-permute-start | bytes 98312 | tf_op jit(solution)/shard_map/ppermute | solution.py:377
